TPU v7x, 32 devices: a whole 2x2x4 slice. The times are simulated.
32 devices in a mesh: seq: 8 (over y, x, core), fsdp: 4 (over z).
Axes of the slice: x: 2, y: 2, z: 4, core: 2. Of those that a mesh axis runs over, the one named last changes fastest.
Arguments:
- activations: bfloat16 [4, 1024, 768], P('fsdp', 'seq'), may hold values from -6 to 6
- segments: int32 [4, 1024], P('fsdp', 'seq'), may hold values from 0 to 1, never falling along the last dimension, each value on 1 to 768 neighbouring positions
- cotangent: bfloat16 [4, 1024, 768], P('fsdp', 'seq'), may hold values from -6 to 6
- attention_gain: bfloat16 [768], P('fsdp'), may hold values from 0.5 to 1.5
- query_weight: bfloat16 [768, 768], P('fsdp'), may hold values from -0.109375 to 0.109375
- key_weight: bfloat16 [768, 768], P('fsdp'), may hold values from -0.109375 to 0.109375
- value_weight: bfloat16 [768, 768], P('fsdp'), may hold values from -0.21875 to 0.21875
- output_weight: bfloat16 [768, 768], P('fsdp'), may hold values from -1.75 to 1.75
- bias_table: bfloat16 [32, 12], P('fsdp'), may hold values from -4 to 4
- feedforward_gain: bfloat16 [768], P('fsdp'), may hold values from 0.5 to 1.5
- inner_weight: bfloat16 [768, 3072], P('fsdp'), may hold values from -0.21875 to 0.21875
- outer_weight: bfloat16 [3072, 768], P('fsdp'), may hold values from -0.109375 to 0.109375
Outputs:
- layer_output: float32 [4, 1024, 768], P('fsdp', 'seq')
- input_gradient: float32 [4, 1024, 768], P('fsdp', 'seq')
- attention_gain_grad: float32 [768], P(('seq', 'fsdp'))
- query_weight_grad: float32 [768, 768], P(('seq', 'fsdp'))
- key_weight_grad: float32 [768, 768], P(('seq', 'fsdp'))
- value_weight_grad: float32 [768, 768], P(('seq', 'fsdp'))
- output_weight_grad: float32 [768, 768], P(('seq', 'fsdp'))
- bias_table_grad: float32 [32, 12], replicated
- feedforward_gain_grad: float32 [768], P(('seq', 'fsdp'))
- inner_weight_grad: float32 [768, 3072], P(('seq', 'fsdp'))
- outer_weight_grad: float32 [3072, 768], P(('seq', 'fsdp'))
Inputs may be any that keep to these rules, and one draw needn't show every extreme that they name: `segments`: along each sequence the numbers never fall; each of the 2 documents has 1 to 768 tokens.
All inputs are finite; a program needn't handle non-finite values.
Results may differ from a plain program's by a relative error of at most 0.018.
Values may be sent and summed in bfloat16 or wider, within the bound.
No kernel may reach another device: no remote copies, remote signals or barrier semaphores. Data moves between devices by JAX's collectives and lax.ppermute only.
A program may use at most 192 MiB of HBM per device.

v0:
```python
import jax
import jax.numpy as jnp
from jax import lax
from jax.sharding import PartitionSpec as P

D = 768
H = 12
DH = 64


epsilon = 1e-06
neg_fill = -1e30
limits = (12, 16, 23, 32, 46, 64, 91)
highest = lax.Precision.HIGHEST
root_half = 0.7071067811865476
inv_root_tau = 0.3989422804014327


def bucket_of(offset):
    distance = jnp.abs(offset)
    farther = jnp.zeros_like(offset) + 8
    for limit in limits:
        farther = farther + (distance >= limit).astype(jnp.int32)
    nearer = jnp.where(distance < 8, distance, farther)
    return nearer + jnp.where(offset > 0, 16, 0)


def rms_scale(value, gain):
    return value * lax.rsqrt(jnp.mean(value * value, axis=-1, keepdims=True) + epsilon) * gain


def gelu_slope(value):
    return (
        0.5 * (1.0 + lax.erf(value * root_half))
        + value * jnp.exp(-0.5 * value * value) * inv_root_tau
    )


def bucket_onehot(table, query_base, key_base, query_count, key_count):
    width = query_count + key_count
    position = jnp.arange(width, dtype=jnp.int32)
    offset = key_base - query_base + jnp.where(position < key_count, position, position - width)
    labels = jnp.arange(table.shape[0], dtype=jnp.int32)
    return (bucket_of(offset)[:, None] == labels[None, :]).astype(jnp.float32)


def bias_block(table, query_base, key_base, query_count, key_count):
    width = query_count + key_count
    onehot = bucket_onehot(table, query_base, key_base, query_count, key_count)
    along = jnp.dot(onehot, table, precision=highest).T
    heads = along.shape[0]
    tiled = jnp.broadcast_to(along[:, None, :], (heads, query_count, width))
    skewed = tiled.reshape(heads, query_count * width)[:, : query_count * (width - 1)]
    return skewed.reshape(heads, query_count, width - 1)[:, :, :key_count]


def bias_grad(grad, table, query_base, key_base):
    heads, query_count, key_count = grad.shape
    width = query_count + key_count
    padded = jnp.pad(grad, ((0, 0), (0, 0), (0, width - 1 - key_count)))
    flat = jnp.pad(padded.reshape(heads, query_count * (width - 1)), ((0, 0), (0, query_count)))
    diagonal = flat.reshape(heads, query_count, width).sum(axis=1)
    onehot = bucket_onehot(table, query_base, key_base, query_count, key_count)
    return jnp.dot(onehot.T, diagonal.T, precision=highest)


def on_device(
    activations,
    segments,
    cotangent,
    attention_gain,
    query_weight,
    key_weight,
    value_weight,
    output_weight,
    bias_table,
    feedforward_gain,
    inner_weight,
    outer_weight,
):
    batch, local = (activations.shape[0], activations.shape[1])
    gain_first, query_full, key_full, value_full, output_full, table = (
        lax.all_gather(attention_gain, "fsdp", axis=0, tiled=True),
        lax.all_gather(query_weight, "fsdp", axis=0, tiled=True),
        lax.all_gather(key_weight, "fsdp", axis=0, tiled=True),
        lax.all_gather(value_weight, "fsdp", axis=0, tiled=True),
        lax.all_gather(output_weight, "fsdp", axis=0, tiled=True),
        lax.all_gather(bias_table, "fsdp", axis=0, tiled=True),
    )
    table_float = table.astype(jnp.float32)
    gain_first_float = gain_first.astype(jnp.float32)
    inputs = activations.astype(jnp.float32)
    normed = rms_scale(inputs, gain_first_float).astype(jnp.bfloat16)
    query = jnp.einsum(
        "std,de->ste", normed, query_full, preferred_element_type=jnp.float32
    ).astype(jnp.bfloat16)
    keys = jnp.einsum("std,de->tse", normed, key_full, preferred_element_type=jnp.float32).astype(
        jnp.bfloat16
    )
    values = jnp.einsum(
        "std,de->tse", normed, value_full, preferred_element_type=jnp.float32
    ).astype(jnp.bfloat16)
    packed = jnp.concatenate([keys, values], axis=2)
    order = segments.T
    keys_all, order_all = (
        lax.all_gather(packed, "seq", axis=0, tiled=True),
        lax.all_gather(order, "seq", axis=0, tiled=True),
    )
    length = keys_all.shape[0]
    block = min(512, length)
    blocks = length // block
    query_base = lax.axis_index("seq") * local
    query_heads = query.reshape(batch, local, H, DH)
    first_seg = segments[:, 0]
    last_seg = segments[:, -1]

    def fetch(index):
        start = index * block
        rows = lax.dynamic_slice_in_dim(keys_all, start, block, 0)
        marks = lax.dynamic_slice_in_dim(order_all, start, block, 0)
        meets = jnp.any((marks[0] <= last_seg) & (marks[-1] >= first_seg))
        allowed = segments[:, None, :, None] == marks.T[:, None, None, :]
        key_part = rows[:, :, :D].reshape(block, batch, H, DH)
        value_part = rows[:, :, D:].reshape(block, batch, H, DH)
        return (start, key_part, value_part, allowed, meets)

    def logits(start, key_part):
        raw = jnp.einsum(
            "sthd,kshd->shtk", query_heads, key_part, preferred_element_type=jnp.float32
        )
        return raw + bias_block(table_float, query_base, start, local, block)[None]

    def first_pass(index, state):
        start, key_part, value_part, allowed, meets = fetch(index)
        running, total = state
        scores = logits(start, key_part)
        peak = jnp.maximum(running, jnp.where(allowed, scores, neg_fill).max(axis=-1))
        kept = jnp.where(allowed, jnp.exp(scores - peak[..., None]), 0.0)
        return (peak, total * jnp.exp(running - peak) + kept.sum(axis=-1))

    start_state = (
        jnp.full((batch, H, local), neg_fill, jnp.float32),
        jnp.zeros((batch, H, local), jnp.float32),
    )
    peak, total = lax.fori_loop(0, blocks, first_pass, start_state)
    logsum = peak + jnp.log(total)

    def second_pass(index, state):
        start, key_part, value_part, allowed, meets = fetch(index)
        scores = logits(start, key_part)
        weights = jnp.where(allowed, jnp.exp(scores - logsum[..., None]), 0.0).astype(jnp.bfloat16)
        return state + jnp.einsum(
            "shtk,kshd->shtd", weights, value_part, preferred_element_type=jnp.float32
        )

    context_sum = lax.fori_loop(
        0, blocks, second_pass, jnp.zeros((batch, H, local, DH), jnp.float32)
    )
    context_float = context_sum.transpose(0, 2, 1, 3).reshape(batch, local, D)
    context = context_float.astype(jnp.bfloat16)
    attended = inputs + jnp.einsum(
        "ste,ed->std", context, output_full, preferred_element_type=jnp.float32
    )
    gain_second, inner_full, outer_full = (
        lax.all_gather(feedforward_gain, "fsdp", axis=0, tiled=True),
        lax.all_gather(inner_weight, "fsdp", axis=0, tiled=True),
        lax.all_gather(outer_weight, "fsdp", axis=0, tiled=True),
    )
    gain_second_float = gain_second.astype(jnp.float32)
    normed_ffn = rms_scale(attended, gain_second_float).astype(jnp.bfloat16)
    inner = jnp.einsum("std,df->stf", normed_ffn, inner_full, preferred_element_type=jnp.float32)
    active = jax.nn.gelu(inner, approximate=False).astype(jnp.bfloat16)
    result = attended + jnp.einsum(
        "stf,fd->std", active, outer_full, preferred_element_type=jnp.float32
    )
    outer_grad = jnp.einsum("stf,std->fd", active, cotangent, preferred_element_type=jnp.float32)
    grad_active = jnp.einsum(
        "std,fd->stf", cotangent, outer_full, preferred_element_type=jnp.float32
    ).astype(jnp.bfloat16)
    grad_inner = (grad_active.astype(jnp.float32) * gelu_slope(inner)).astype(jnp.bfloat16)
    inner_grad = jnp.einsum(
        "std,stf->df", normed_ffn, grad_inner, preferred_element_type=jnp.float32
    )
    grad_normed_ffn = jnp.einsum(
        "stf,df->std", grad_inner, inner_full, preferred_element_type=jnp.float32
    )
    _, second_back = jax.vjp(rms_scale, attended, gain_second_float)
    through_second, second_gain_grad = second_back(grad_normed_ffn)
    grad_attended = cotangent.astype(jnp.float32) + through_second
    grad_branch = grad_attended.astype(jnp.bfloat16)
    output_grad = jnp.einsum(
        "ste,std->ed", context, grad_branch, preferred_element_type=jnp.float32
    )
    grad_context = jnp.einsum(
        "std,ed->ste", grad_branch, output_full, preferred_element_type=jnp.float32
    ).astype(jnp.bfloat16)
    grad_heads = grad_context.reshape(batch, local, H, DH)
    delta = (
        (grad_context.astype(jnp.float32) * context_float)
        .reshape(batch, local, H, DH)
        .sum(axis=-1)
        .transpose(0, 2, 1)
    )
    key_terms = jnp.zeros((length, batch, 2 * D), jnp.float32)

    def back_pass(index, state):
        start, key_part, value_part, allowed, meets = fetch(index)
        query_grad_sum, table_grad_sum, terms = state
        scores = logits(start, key_part)
        probs = jnp.where(allowed, jnp.exp(scores - logsum[..., None]), 0.0)
        grad_probs = jnp.einsum(
            "sthd,kshd->shtk", grad_heads, value_part, preferred_element_type=jnp.float32
        )
        grad_scores = (probs * (grad_probs - delta[..., None])).astype(jnp.bfloat16)
        query_grad_sum = query_grad_sum + jnp.einsum(
            "shtk,kshd->shtd", grad_scores, key_part, preferred_element_type=jnp.float32
        )
        table_grad_sum = table_grad_sum + bias_grad(
            grad_scores.astype(jnp.float32).sum(axis=0), table_float, query_base, start
        )
        key_piece = jnp.einsum(
            "shtk,sthd->kshd", grad_scores, query_heads, preferred_element_type=jnp.float32
        )
        value_piece = jnp.einsum(
            "shtk,sthd->kshd",
            probs.astype(jnp.bfloat16),
            grad_heads,
            preferred_element_type=jnp.float32,
        )
        joined = jnp.concatenate(
            [key_piece.reshape(block, batch, D), value_piece.reshape(block, batch, D)], axis=2
        )
        terms = lax.dynamic_update_slice_in_dim(terms, joined, start, 0)
        return (query_grad_sum, table_grad_sum, terms)

    back_start = (
        jnp.zeros((batch, H, local, DH), jnp.float32),
        jnp.zeros(table_float.shape, jnp.float32),
        key_terms,
    )
    query_grad_sum, table_grad_local, key_terms = lax.fori_loop(0, blocks, back_pass, back_start)
    grad_query = query_grad_sum.transpose(0, 2, 1, 3).reshape(batch, local, D).astype(jnp.bfloat16)
    owned = lax.psum_scatter(key_terms, "seq", scatter_dimension=0, tiled=True)
    grad_keys = owned[:, :, :D].astype(jnp.bfloat16)
    grad_values = owned[:, :, D:].astype(jnp.bfloat16)
    query_grad = jnp.einsum("std,ste->de", normed, grad_query, preferred_element_type=jnp.float32)
    key_grad = jnp.einsum("std,tse->de", normed, grad_keys, preferred_element_type=jnp.float32)
    value_grad = jnp.einsum("std,tse->de", normed, grad_values, preferred_element_type=jnp.float32)
    grad_normed = jnp.einsum(
        "ste,de->std", grad_query, query_full, preferred_element_type=jnp.float32
    )
    grad_normed = grad_normed + jnp.einsum(
        "tse,de->std", grad_keys, key_full, preferred_element_type=jnp.float32
    )
    grad_normed = grad_normed + jnp.einsum(
        "tse,de->std", grad_values, value_full, preferred_element_type=jnp.float32
    )
    _, first_back = jax.vjp(rms_scale, inputs, gain_first_float)
    through_first, first_gain_grad = first_back(grad_normed)
    input_gradient = grad_attended + through_first
    attention_sums = (
        lax.psum_scatter(first_gain_grad, ("seq", "fsdp"), scatter_dimension=0, tiled=True),
        lax.psum_scatter(query_grad, ("seq", "fsdp"), scatter_dimension=0, tiled=True),
        lax.psum_scatter(key_grad, ("seq", "fsdp"), scatter_dimension=0, tiled=True),
        lax.psum_scatter(value_grad, ("seq", "fsdp"), scatter_dimension=0, tiled=True),
        lax.psum_scatter(output_grad, ("seq", "fsdp"), scatter_dimension=0, tiled=True),
    )
    table_total = lax.psum(table_grad_local, ("seq", "fsdp"))
    feedforward_sums = (
        lax.psum_scatter(second_gain_grad, ("seq", "fsdp"), scatter_dimension=0, tiled=True),
        lax.psum_scatter(inner_grad, ("seq", "fsdp"), scatter_dimension=0, tiled=True),
        lax.psum_scatter(outer_grad, ("seq", "fsdp"), scatter_dimension=0, tiled=True),
    )
    return (
        result,
        input_gradient,
        attention_sums[0],
        attention_sums[1],
        attention_sums[2],
        attention_sums[3],
        attention_sums[4],
        table_total,
        feedforward_sums[0],
        feedforward_sums[1],
        feedforward_sums[2],
    )


def solution(mesh):
    return jax.shard_map(
        on_device,
        mesh=mesh,
        in_specs=(
            P("fsdp", "seq", None),
            P("fsdp", "seq"),
            P("fsdp", "seq", None),
            P("fsdp"),
            P("fsdp", None),
            P("fsdp", None),
            P("fsdp", None),
            P("fsdp", None),
            P("fsdp", None),
            P("fsdp"),
            P("fsdp", None),
            P("fsdp", None),
        ),
        out_specs=(
            P("fsdp", "seq", None),
            P("fsdp", "seq", None),
            P(("seq", "fsdp")),
            P(("seq", "fsdp"), None),
            P(("seq", "fsdp"), None),
            P(("seq", "fsdp"), None),
            P(("seq", "fsdp"), None),
            P(),
            P(("seq", "fsdp")),
            P(("seq", "fsdp"), None),
            P(("seq", "fsdp"), None),
        ),
        check_vma=False,
    )
```

profile of v0, /device:TPU:0, one launch (start us, length us, event | category | flops | bytes accessed | tf_op | source)
XLA Modules:
  0.0 1235.7 jit_solution(4188735068463466757)
XLA Ops:
  13.1 13.5 %all-reduce.7 = (bf16[768]{0:T(1024)(128)(2,1)S(1)}, bf16[768]{0:T(1024)(128)(2,1)S(1)}) all-reduce(bf16[768]{0:T(1024)(128)(2,1)S(1)} %dynamic-update-slice, bf16[768]{0:T(1024)(128)(2,1)S(1)} %dynamic-update-slice.1), channel_id=1, replica_groups=mesh['seq'=8,'fsdp'=4] {'fsdp'}, use_global_device_ids=true, to_apply=%add.2 | all-reduce | flops 1536 | bytes 6144
  27.6 15.3 %all-gather.11.cloned.1.call-done = bf16[768,768]{1,0:T(8,128)(2,1)} async-done(((bf16[192,768]{1,0:T(8,128)(2,1)}), bf16[768,768]{1,0:T(8,128)(2,1)}) %all-gather.11.cloned.1.call-update) | async-done | bytes 1179664 | tf_op jit(solution)/shard_map/all_gather | solution.py:86
  44.6 29.4 %all-gather.9.cloned.1.call-done = bf16[768,768]{1,0:T(8,128)(2,1)} async-done(((bf16[192,768]{1,0:T(8,128)(2,1)}), bf16[768,768]{1,0:T(8,128)(2,1)}) %all-gather.9.cloned.1.call-update) | async-done | bytes 1179664 | tf_op jit(solution)/shard_map/all_gather | solution.py:85
  79.1 8.7 all-gather
  87.8 12.0 all_gather.39
  99.9 5.5 all-gather.15.cloned.1.call-done
  107.1 32.0 %all-gather.13.cloned.1.call-done = bf16[1024,1,1536]{2,0,1:T(8,128)(2,1)} async-done(((bf16[128,1,1536]{2,0,1:T(8,128)(2,1)}), bf16[1024,1,1536]{2,0,1:T(8,128)(2,1)}) %all-gather.13.cloned.1.call-update) | async-done | bytes 3145744 | tf_op jit(solution)/shard_map/all_gather | solution.py:106
  143.7 47.5 %while.54 = (s32[]{:T(128)}, f32[1,12,128]{2,1,0:T(8,128)S(1)}, f32[1,12,128]{2,1,0:T(8,128)S(1)}, s32[1,128]{1,0:T(1,128)S(1)}, s32[1024,1]{0,1:T(1,128)S(1)}, ...) while((s32[]{:T(128)}, f32[1,12,128]{2,1,0:T(8,128)S(1)}, ...), condition=%wide.region_4.5_spmd.clone, body=%wide.region_1.4_spmd.clone.sunk | while | flops 108444552 | bytes 67370232 | solution.py:145
  152.8 6.9 reshape.893
  176.5 7.0 reshape.893
  191.8 53.0 %while.55 = (s32[]{:T(128)}, f32[1,12,128,64]{2,3,1,0:T(8,128)}, s32[1,128]{1,0:T(1,128)S(1)}, s32[1024,1]{0,1:T(1,128)S(1)}, bf16[1024,1,1536]{0,2,1:T(8,128)(2...) while((s32[]{:T(128)}, f32[1,12,128,64]{2,3,1,0:T(8,128)}, ...), condition=%wide.region_6.7_spmd.clone, body=%wide.region_5.6_spmd.clone.sunk | while | flops 207723904 | bytes 64085260 | solution.py:156
  203.1 6.9 reshape.894
  229.3 6.9 reshape.894
  247.9 13.1 %all-gather.19.cloned.1.call-done = bf16[768,3072]{1,0:T(8,128)(2,1)} async-done(((bf16[192,3072]{1,0:T(8,128)(2,1)}), bf16[768,3072]{1,0:T(8,128)(2,1)}) %all-gather.19.cloned.1.call-update) | async-done | bytes 4718608 | tf_op jit(solution)/shard_map/all_gather | solution.py:166
  261.0 7.8 fusion.65
  268.8 81.6 %all-gather.21.cloned.1.call-done = bf16[3072,768]{1,0:T(8,128)(2,1)} async-done(((bf16[768,768]{1,0:T(8,128)(2,1)}), bf16[3072,768]{1,0:T(8,128)(2,1)}) %all-gather.21.cloned.1.call-update) | async-done | bytes 4718608 | tf_op jit(solution)/shard_map/all_gather | solution.py:167
  350.4 4.7 fusion.62
  364.1 103.0 %while.56 = (s32[]{:T(128)}, f32[1,12,128,64]{2,3,1,0:T(8,128)}, f32[32,12]{0,1:T(8,128)}, f32[1024,1,1536]{0,2,1:T(8,128)}, s32[1,128]{1,0:T(1,128)S(1)}, /*ind...) while((s32[]{:T(128)}, f32[1,12,128,64]{2,3,1,0:T(8,128)}, ...), condition=%wide.region_12.13_spmd.clone, body=%wide.region_10.12_spmd.clone.sunk | while | flops 517788288 | bytes 186148048 | solution.py:241
  386.2 6.9 reshape.896
  408.4 5.4 reshape.897
  432.0 6.9 reshape.896
  454.2 5.4 reshape.897
  473.4 54.2 %reduce-scatter.8.cloned.1.call-done = f32[128,1,1536]{0,2,1:T(8,128)} async-done(((f32[1024,1,1536]{0,2,1:T(8,128)}), f32[128,1,1536]{0,2,1:T(8,128)}) %reduce-scatter.8.cloned.1.call-update) | async-done | bytes 786448 | tf_op jit(solution)/shard_map/reduce_scatter | solution.py:243
  534.0 5.1 fusion.108
  540.3 5.1 fusion.98
  551.5 39.5 %all-reduce.6 = (f32[768]{0:T(1024)S(1)}, f32[32,12]{0,1:T(8,128)}, f32[768]{0:T(1024)S(1)}) all-reduce(f32[768]{0:T(1024)S(1)} %get-tuple-element.997, f32[32,12]{0,1:T(8,128)S(1)} %copy-done.42, f32[768]{0:T(1024)S(1)} %copy-done.36), channel_id=4, replica_groups=mesh['seq'=8,'fsdp'=4] {'seq','fsdp'}, use_global_device_ids=true, to_apply=%region_16.17.clone | all-reduce | flops 1920 | bytes 15360
  593.1 40.4 %reduce-scatter.16.cloned.1.call-done = f32[24,768]{1,0:T(8,128)} async-done(((f32[768,768]{1,0:T(8,128)}), f32[24,768]{1,0:T(8,128)}) %reduce-scatter.16.cloned.1.call-update) | async-done | bytes 73744 | tf_op jit(solution)/shard_map/reduce_scatter | solution.py:266
  633.5 103.6 %reduce-scatter.10.cloned.1.call-done = f32[24,768]{1,0:T(8,128)} async-done(((f32[768,768]{1,0:T(8,128)}), f32[24,768]{1,0:T(8,128)}) %reduce-scatter.10.cloned.1.call-update) | async-done | bytes 73744 | tf_op jit(solution)/shard_map/reduce_scatter | solution.py:263
  737.1 104.8 %reduce-scatter.14.cloned.1.call-done = f32[24,768]{1,0:T(8,128)} async-done(((f32[768,768]{1,0:T(8,128)}), f32[24,768]{1,0:T(8,128)}) %reduce-scatter.14.cloned.1.call-update) | async-done | bytes 73744 | tf_op jit(solution)/shard_map/reduce_scatter | solution.py:265
  842.0 103.7 %reduce-scatter.12.cloned.1.call-done = f32[24,768]{1,0:T(8,128)} async-done(((f32[768,768]{1,0:T(8,128)}), f32[24,768]{1,0:T(8,128)}) %reduce-scatter.12.cloned.1.call-update) | async-done | bytes 73744 | tf_op jit(solution)/shard_map/reduce_scatter | solution.py:264
  945.7 142.2 %reduce-scatter.18.cloned.1.call-done = f32[24,3072]{1,0:T(8,128)} async-done(((f32[768,3072]{1,0:T(8,128)}), f32[24,3072]{1,0:T(8,128)}) %reduce-scatter.18.cloned.1.call-update) | async-done | bytes 294928 | tf_op jit(solution)/shard_map/reduce_scatter | solution.py:271
  1087.9 141.0 %reduce-scatter.20.cloned.1.call-done = f32[96,768]{1,0:T(8,128)} async-done(((f32[3072,768]{1,0:T(8,128)}), f32[96,768]{1,0:T(8,128)}) %reduce-scatter.20.cloned.1.call-update) | async-done | bytes 294928 | tf_op jit(solution)/shard_map/reduce_scatter | solution.py:272
  (315 shorter events, 192.8 us)
Async XLA Ops:
  7.2 66.8 %copy-start.5 = (bf16[1,128,768]{2,1,0:T(8,128)(2,1)S(1)}, bf16[1,128,768]{2,1,0:T(8,128)(2,1)}, u32[]{:S(2)}) copy-start(bf16[1,128,768]{2,1,0:T(8,128)(2,1)} %param.18) | copy-start | bytes 589828
  7.2 35.7 %all-gather.11.cloned.1.call-start = ((), (), s32[]{:S(2)}) async-start(), calls=%async_computation.8 | async-start | bytes 1474560 | tf_op jit(solution)/shard_map/all_gather | solution.py:86
  7.9 66.1 %all-gather.9.cloned.1.call-start = ((), (), s32[]{:S(2)}) async-start(), calls=%async_computation.7 | async-start | bytes 1474560 | tf_op jit(solution)/shard_map/all_gather | solution.py:85
  8.7 96.6 %all-gather.15.cloned.1.call-start = ((), (), s32[]{:S(2)}) async-start(), calls=%async_computation.10 | async-start | bytes 1474560 | tf_op jit(solution)/shard_map/all_gather | solution.py:84
  9.4 129.7 %all-gather.13.cloned.1.call-start = ((), (), s32[]{:S(2)}) async-start(), calls=%async_computation.9 | async-start | bytes 3538944 | tf_op jit(solution)/shard_map/all_gather | solution.py:106
  26.6 78.8 %copy-start.26 = (f32[768]{0:T(1024)}, f32[768]{0:T(1024)S(1)}, u32[]{:S(2)}) copy-start(f32[768]{0:T(1024)S(1)} %convert_element_type.469) | copy-start | bytes 9220
  27.6 48.0 %copy-start.46 = (f32[128]{0:T(128)}, f32[128]{0:T(128)S(1)}, u32[]{:S(2)}) copy-start(f32[128]{0:T(128)S(1)} %fusion.89) | copy-start | bytes 1540
  27.6 77.7 %copy-start.34 = (f32[128]{0:T(128)}, f32[128]{0:T(128)S(1)}, u32[]{:S(2)}) copy-start(f32[128]{0:T(128)S(1)} %fusion.106) | copy-start | bytes 1540
  76.4 11.3 copy-start.45
  76.5 169.5 %all-gather.17.cloned.1.call-start = ((), (), s32[]{:S(2)}) async-start(), calls=%async_computation.11 | async-start | bytes 1474560 | tf_op jit(solution)/shard_map/all_gather | solution.py:87
  77.1 183.9 %all-gather.19.cloned.1.call-start = ((), (), s32[]{:S(2)}) async-start(), calls=%async_computation.12 | async-start | bytes 5898240 | tf_op jit(solution)/shard_map/all_gather | solution.py:166
  77.6 272.8 %all-gather.21.cloned.1.call-start = ((), (), s32[]{:S(2)}) async-start(), calls=%async_computation.13 | async-start | bytes 5898240 | tf_op jit(solution)/shard_map/all_gather | solution.py:167
  78.4 449.1 %reduce-scatter.8.cloned.1.call-start = ((), (), s32[]{:S(2)}) async-start(), calls=%async_computation.14 | async-start | bytes 7077888 | tf_op jit(solution)/shard_map/reduce_scatter | solution.py:243
  191.8 54.2 %copy-start.6 = (bf16[1,128,768]{2,1,0:T(8,128)(2,1)S(1)}, bf16[1,128,768]{2,1,0:T(8,128)(2,1)}, u32[]{:S(2)}) copy-start(bf16[1,128,768]{2,1,0:T(8,128)(2,1)} %param.18) | copy-start | bytes 589828
  244.8 24.0 %copy-start.28 = (f32[1,12,128]{2,1,0:T(8,128)}, f32[1,12,128]{2,1,0:T(8,128)S(1)}, u32[]{:S(2)}) copy-start(f32[1,12,128]{2,1,0:T(8,128)S(1)} %get-tuple-element.1484) | copy-start | bytes 18436
  244.8 16.2 %copy-start.29 = (f32[768]{0:T(1024)S(1)}, f32[768]{0:T(1024)}, u32[]{:S(2)}) copy-start(f32[768]{0:T(1024)} %convert_element_type.482) | copy-start | bytes 9220
  247.9 110.5 %copy-start.11 = (f32[1,128,768]{2,1,0:T(8,128)}, f32[1,128,768]{2,1,0:T(8,128)S(1)}, u32[]{:S(2)}) copy-start(f32[1,128,768]{2,1,0:T(8,128)S(1)} %get-tuple-element.1073) | copy-start | bytes 1179652
  247.9 110.5 %copy-start.43 = (f32[128]{0:T(128)}, f32[128]{0:T(128)S(1)}, u32[]{:S(2)}) copy-start(f32[128]{0:T(128)S(1)} %fusion.107) | copy-start | bytes 1540
  261.0 89.5 %copy-start.24 = (bf16[1,128,768]{2,1,0:T(8,128)(2,1)S(1)}, bf16[1,128,768]{2,1,0:T(8,128)(2,1)}, u32[]{:S(2)}) copy-start(bf16[1,128,768]{2,1,0:T(8,128)(2,1)} %param.20) | copy-start | bytes 589828
  350.4 5.6 copy-start.19
  360.6 3.5 copy-start.38
  417.8 3.4 copy-start.39
  463.6 3.4 copy-start.39
  467.2 166.3 %reduce-scatter.16.cloned.1.call-start = ((), (), s32[]{:S(2)}) async-start(), calls=%async_computation.18 | async-start | bytes 2433024 | tf_op jit(solution)/shard_map/reduce_scatter | solution.py:266
  470.2 266.9 %reduce-scatter.10.cloned.1.call-start = ((), (), s32[]{:S(2)}) async-start(), calls=%async_computation.15 | async-start | bytes 2433024 | tf_op jit(solution)/shard_map/reduce_scatter | solution.py:263
  473.3 368.6 %reduce-scatter.14.cloned.1.call-start = ((), (), s32[]{:S(2)}) async-start(), calls=%async_computation.17 | async-start | bytes 2433024 | tf_op jit(solution)/shard_map/reduce_scatter | solution.py:265
  530.7 415.0 %reduce-scatter.12.cloned.1.call-start = ((), (), s32[]{:S(2)}) async-start(), calls=%async_computation.16 | async-start | bytes 2433024 | tf_op jit(solution)/shard_map/reduce_scatter | solution.py:264
  532.7 555.1 %reduce-scatter.18.cloned.1.call-start = ((), (), s32[]{:S(2)}) async-start(), calls=%async_computation.19 | async-start | bytes 9732096 | tf_op jit(solution)/shard_map/reduce_scatter | solution.py:271
  539.1 689.7 %reduce-scatter.20.cloned.1.call-start = ((), (), s32[]{:S(2)}) async-start(), calls=%async_computation.20 | async-start | bytes 9732096 | tf_op jit(solution)/shard_map/reduce_scatter | solution.py:272
  545.4 4.1 copy-start.17
  545.4 4.6 copy-start.18
  550.8 41.4 %copy-start.47 = (f32[128]{0:T(128)S(1)}, f32[128]{0:T(128)}, u32[]{:S(2)}) copy-start(f32[128]{0:T(128)} %copy-done.46) | copy-start | bytes 1540
  (52 other events, 81.9 us)
Sparse Core Ops, SparseCore 0:
  9.6 33.2 all-gather.10
  44.5 29.5 all-gather.8
  75.6 29.6 all-gather.14
  107.6 31.4 all-gather.12
  140.5 30.4 all-gather.16
  172.4 88.5 all-gather.18
  262.5 87.8 all-gather.20
  467.3 60.1 reduce-scatter.7
  534.2 99.2 reduce-scatter.15
  639.2 97.8 reduce-scatter.9
  743.9 98.0 reduce-scatter.13
  847.7 97.9 reduce-scatter.11
  953.2 134.6 reduce-scatter.17
  1094.2 134.5 reduce-scatter.19
where the time goes:
time: 1250 us; the launch traced here: 1240 us
  waiting for transfers between devices  871 us (70%)
  local copies, waits for them, and re-layouts  171 us (14%)
  matrix products  80.5 us (6%)
  blocking collectives  73.7 us (6%)
  between operations  15.4 us (1%)
    reduce_scatter x1, waiting for transfers between devices, on_device(): lax.psum_scatter(inner_grad, ('seq', 'fsdp'), scatter_dimension=0, tiled=...  142 us
    reduce_scatter x1, waiting for transfers between devices, on_device(): lax.psum_scatter(outer_grad, ('seq', 'fsdp'), scatter_dimension=0, tiled=...  141 us
    reduce_scatter x1, waiting for transfers between devices, on_device(): lax.psum_scatter(value_grad, ('seq', 'fsdp'), scatter_dimension=0, tiled=...  105 us
    reduce_scatter x1, waiting for transfers between devices, on_device(): lax.psum_scatter(key_grad, ('seq', 'fsdp'), scatter_dimension=0, tiled=True)  104 us
    reduce_scatter x1, waiting for transfers between devices, on_device(): lax.psum_scatter(query_grad, ('seq', 'fsdp'), scatter_dimension=0, tiled=...  104 us
    all_gather x1, waiting for transfers between devices, on_device(): lax.all_gather(outer_weight, 'fsdp', axis=0, tiled=True)  81.6 us
    reduce_scatter x1, waiting for transfers between devices, on_device(): owned = lax.psum_scatter(key_terms, 'seq', scatter_dimension=0, tiled=True)  54.2 us
    unnamed x2, blocking collectives  53 us
  transfers between devices with their start and end apart: 14, of which 13 were waited for; matrix products, arithmetic and copies ran while one was open for 12% of the time, Pallas kernels for 0%

commit v1 on v0

v1 whole, which is shorter than its diff:
```python
import functools

import jax
import jax.numpy as jnp
from jax import lax
from jax.experimental import pallas as pl
from jax.experimental.pallas import tpu as pltpu
from jax.sharding import PartitionSpec as P

D = 768
H = 12
DH = 64
GROUPS = 4
HG = H // GROUPS
CG = HG * DH

epsilon = 1e-06
FORCE_GENERIC = False
neg_fill = -1e30
limits = (12, 16, 23, 32, 46, 64, 91)
root_half = 0.7071067811865476
inv_root_tau = 0.3989422804014327
bf16 = jnp.bfloat16
f32 = jnp.float32
NT = (((1,), (1,)), ((), ()))
TN = (((0,), (0,)), ((), ()))
NN = (((1,), (0,)), ((), ()))


def mm(a, b, dims=NN):
    return lax.dot_general(a, b, dims, preferred_element_type=f32)


def bucket_of(offset):
    distance = jnp.abs(offset)
    farther = jnp.zeros_like(offset) + 8
    for limit in limits:
        farther = farther + (distance >= limit).astype(jnp.int32)
    nearer = jnp.where(distance < 8, distance, farther)
    return nearer + jnp.where(offset > 0, 16, 0)


def call(kernel, outs, args, scalars=0, scratch=(), mib=32, cost=None):
    vmem = pl.BlockSpec(memory_space=pltpu.VMEM)
    smem = pl.BlockSpec(memory_space=pltpu.SMEM)
    return pl.pallas_call(
        kernel,
        out_shape=outs,
        in_specs=[smem] * scalars + [vmem] * (len(args) - scalars),
        out_specs=jax.tree.map(lambda _: vmem, outs),
        scratch_shapes=scratch,
        compiler_params=pltpu.CompilerParams(vmem_limit_bytes=mib << 20),
        cost_estimate=None
        if cost is None
        else pl.CostEstimate(flops=cost, bytes_accessed=1 << 20, transcendentals=0),
    )(*args)


def shape(dims, kind):
    return jax.ShapeDtypeStruct(dims, kind)


def project_kernel(T, ids, x0, x1, x2, x3, w0, w1, w2, w3, wo, normed, kv, query, gains, table, W, small):
    half, f = ids[1], ids[2]
    rows = W.shape[2]
    xs, ws = (x0, x1, x2, x3), (w0, w1, w2, w3)
    for k in range(4):
        z = f ^ k
        W[z, half] = ws[k][:rows, :]
        W[z, 1 - half] = wo[k, :rows, :]
        small[z] = ws[k][rows:, :].astype(f32)
    gain = jnp.concatenate([small[z, 0:1, 0 : D // 4] for z in range(4)], axis=1)
    gains[0:1, :] = gain
    gains[1:2, :] = jnp.concatenate([small[z, 1:2, 0 : D // 4] for z in range(4)], axis=1)
    table[...] = jnp.concatenate([small[z, 8:16, 0:128] for z in range(4)], axis=0)
    weight = W[...].reshape(D, 3 * CG)
    for i in range(2):
        parts = []
        for k in (2 * i, 2 * i + 1):
            x = xs[k][:T, :].astype(f32)
            s = lax.rsqrt(jnp.mean(x * x, axis=-1, keepdims=True) + epsilon)
            parts.append((x * s * gain).astype(bf16))
        n = jnp.concatenate(parts, axis=0)
        at = slice(2 * i * T, (2 * i + 2) * T)
        normed[at, :] = n
        out = mm(n, weight)
        blank = jnp.zeros((2 * T, DH), f32)
        for h in range(HG):
            kv[h, at, :] = out[:, 128 * h : 128 * h + 128].astype(bf16)
            q = out[:, 2 * CG + DH * h : 2 * CG + DH * (h + 1)]
            query[h, at, :] = jnp.concatenate([q, blank], axis=1).astype(bf16)


def tiles_kernel(T, ids, table, tiles):
    g = ids[0]
    lane = lax.broadcasted_iota(jnp.int32, (32, 128), 1)
    m = lax.broadcasted_iota(jnp.int32, (32, 2 * T), 1)
    label = lax.broadcasted_iota(jnp.int32, (32, 2 * T), 0)
    for h in range(HG):
        column = jnp.sum(jnp.where(lane == HG * g + h, table[...], 0.0), axis=1, keepdims=True)
        for d in range(5):
            offset = T * (d - 2) - jnp.where(m < T, m, m - 2 * T)
            hot = jnp.where(bucket_of(offset) == label, column, 0.0)
            along = jnp.sum(hot, axis=0, keepdims=True)
            wide = jnp.broadcast_to(along, (T, 2 * T))
            tiles[h, d] = pltpu.roll(wide, 0, 1, stride=1, stride_axis=0)[:, :T]


def tile_of(key_at, query_at):
    return jnp.clip(key_at - query_at, -2, 2) + 2


def mark_columns(T, count, marks, columns):
    across = jnp.concatenate([marks[...], jnp.zeros((128 - marks.shape[0], 128), f32)], axis=0).T
    for t in range(count):
        columns[t] = jnp.broadcast_to(across[:, t : t + 1], (T, 128))


def masked_scores(T, scores, base, pair, h, q_at, k_at, seg_q, columns, tiles):
    pieces = []
    for t in range(8):
        kt = base + t
        bias = jnp.concatenate([tiles[h, tile_of(k_at[kt], q_at[2 * pair + j])] for j in range(2)], axis=1)
        column = jnp.concatenate([columns[kt], columns[kt]], axis=1)
        piece = scores[t * T : (t + 1) * T] + bias
        pieces.append(jnp.where(column == seg_q, piece, neg_fill))
    return jnp.concatenate(pieces, axis=0)


def pick_keys(blocks, i, h):
    if len(blocks) == 2:
        return jnp.concatenate([blocks[0][h], blocks[1][h]], axis=0)
    return jnp.concatenate([blocks[0][2 * i, h], blocks[0][2 * i + 1, h]], axis=0)


def forward_kernel(T, nb, fast, ids, q_at, k_at, query, seg_q, seg_k, tiles, *rest):
    blocks, (context, lse, columns) = rest[:-3], rest[-3:]
    mark_columns(T, nb * 4, seg_k, columns)

    def pair_step(pair, carry):
        at = pl.ds(pl.multiple_of(pair * 2 * T, 2 * T), 2 * T)
        seg = jnp.concatenate([seg_q[pl.ds(2 * pair + j, 1), :] for j in range(2)], axis=1)
        out = []
        for h in range(HG):
            q = query[h, at, :]

            def chunk(i, state):
                peak, total, acc = state
                keys = pick_keys(blocks, i, h)
                s = masked_scores(T, mm(keys, q, NT), 8 * i, pair, h, q_at, k_at, seg, columns, tiles)
                top = jnp.maximum(peak, jnp.max(s, axis=0, keepdims=True))
                p = jnp.exp(s - top)
                fade = jnp.exp(peak - top)
                total = total * fade + jnp.sum(p, axis=0, keepdims=True)
                acc = acc * fade + mm(keys, p.astype(bf16), TN)
                return top, total, acc

            start = (
                jnp.full((1, 2 * T), neg_fill, f32),
                jnp.zeros((1, 2 * T), f32),
                jnp.zeros((128, 2 * T), f32),
            )
            if fast:
                peak, total, acc = chunk(0, start)
            else:
                peak, total, acc = lax.fori_loop(0, nb // 2, chunk, start)
            out.append(acc[DH:, :] / total)
            lse[pair, h : h + 1, :] = peak + jnp.log(total)
        joined = jnp.concatenate(out, axis=0)
        context[at, :] = joined.T.astype(bf16)
        return carry

    lax.fori_loop(0, 2, pair_step, 0)


def backward_kernel(T, nb, fast, ids, q_at, k_at, query, seg_q, seg_k, tiles, lse, g0, g1, g2, g3, *rest):
    nin = 2 if fast else 1
    blocks = rest[:nin]
    if fast:
        dquery, down, doth, sums, columns, dkv = rest[nin:]
    else:
        dquery, dkv, sums, columns = rest[nin:]
    mark_columns(T, nb * 4, seg_k, columns)
    sums[...] = jnp.zeros_like(sums)
    dkv[...] = jnp.zeros_like(dkv)

    def pair_step(pair, carry):
        at = pl.ds(pl.multiple_of(pair * 2 * T, 2 * T), 2 * T)
        seg = jnp.concatenate([seg_q[pl.ds(2 * pair + j, 1), :] for j in range(2)], axis=1)
        grad = g0[at, :].astype(f32) + g1[at, :].astype(f32) + g2[at, :].astype(f32) + g3[at, :].astype(f32)
        blank = jnp.zeros((2 * T, DH), f32)
        out = []
        for h in range(HG):
            q = query[h, at, :]
            do = jnp.concatenate([blank, grad[:, DH * h : DH * (h + 1)]], axis=1).astype(bf16)
            row = lse[pair, h : h + 1, :]

            def probs_of(i):
                keys = pick_keys(blocks, i, h)
                s = masked_scores(T, mm(keys, q, NT), 8 * i, pair, h, q_at, k_at, seg, columns, tiles)
                return keys, jnp.exp(s - row), mm(keys, do, NT)

            def finish(i, keys, p, dp, delta):
                ds = p * (dp - delta)
                for t in range(8):
                    for j in range(2):
                        index = tile_of(k_at[8 * i + t], q_at[2 * pair + j])
                        sums[h, index] += ds[t * T : (t + 1) * T, j * T : (j + 1) * T]
                ds = ds.astype(bf16)
                both = jnp.concatenate([ds, p.astype(bf16)], axis=1)
                piece = mm(both, jnp.concatenate([q, do], axis=0))
                if fast:
                    dkv[h] += piece
                else:
                    dkv[2 * i, h] += piece[: 4 * T]
                    dkv[2 * i + 1, h] += piece[4 * T :]
                return mm(keys, ds, TN)[:DH, :]

            if fast:
                keys, p, dp = probs_of(0)
                delta = jnp.sum(p * dp, axis=0, keepdims=True)
                dq = finish(0, keys, p, dp, delta)
            else:

                def first(i, delta):
                    keys, p, dp = probs_of(i)
                    return delta + jnp.sum(p * dp, axis=0, keepdims=True)

                delta = lax.fori_loop(0, nb // 2, first, jnp.zeros((1, 2 * T), f32))

                def second(i, dq):
                    keys, p, dp = probs_of(i)
                    return dq + finish(i, keys, p, dp, delta)

                dq = lax.fori_loop(0, nb // 2, second, jnp.zeros((DH, 2 * T), f32))
            out.append(dq)
        dquery[at, :] = jnp.concatenate(out, axis=0).T.astype(bf16)
        return carry

    lax.fori_loop(0, 2, pair_step, 0)
    if fast:
        for h in range(HG):
            down[h] = dkv[h, : 4 * T, :]
            doth[h] = dkv[h, 4 * T :, :].astype(bf16)


def table_kernel(T, ids, sums, out):
    g = ids[0]
    j = lax.broadcasted_iota(jnp.int32, (T, T), 0)
    i = lax.broadcasted_iota(jnp.int32, (T, T), 1)
    rows = []
    for h in range(HG):
        near = [sums[h, 1], sums[h, 2], sums[h, 3]]
        maps = [bucket_of(j - i + T * d) for d in (-1, 0, 1)]
        parts = []
        for n in range(32):
            value = jnp.zeros((1, T), f32)
            if n == 15:
                value = value + jnp.sum(sums[h, 0], axis=0, keepdims=True)
            if n == 31:
                value = value + jnp.sum(sums[h, 4], axis=0, keepdims=True)
            for d in range(3):
                if (d == 0 and n > 15) or (d == 2 and n < 16):
                    continue
                value = value + jnp.sum(jnp.where(maps[d] == n, near[d], 0.0), axis=0, keepdims=True)
            parts.append(value)
        stacked = jnp.concatenate(parts, axis=0).T
        rows.append(jnp.sum(stacked, axis=0, keepdims=True))
    pieces = []
    for a in range(GROUPS):
        for h in range(HG):
            pieces.append(jnp.where(g == a, rows[h], 0.0))
    out[...] = jnp.concatenate(pieces, axis=1)


def middle_kernel(T, ids, *refs):
    g, half, f = ids[0], ids[1], ids[2]
    xs, cots, ctxs, ws = refs[0:4], refs[4:8], refs[8:12], refs[12:16]
    other, gains = refs[16], refs[17]
    res0, sends = refs[18], refs[19:22]
    gcs = refs[22:26]
    grads, normed, active, ginner, branch, gain_grad = refs[26:32]
    WO, W1, W2, attended = refs[32:36]
    rows = ws[0].shape[0] // 3
    FH = W1.shape[3]
    for k in range(4):
        z = f ^ k
        for own in (True, False):
            at = half if own else 1 - half
            block = ws[k][...] if own else other[k]
            WO[z, at] = block[:rows]
            W1[at, z] = block[rows : 2 * rows]
            W2[at, z, :, 0 : D // 2] = block[2 * rows : 2 * rows + rows // 2]
            W2[at, z, :, D // 2 :] = block[2 * rows + rows // 2 :]
    gain = gains[1:2, :]
    gain_grad[...] = jnp.zeros_like(gain_grad)

    def out_rows(k):
        return jnp.concatenate([WO[g ^ k, 0], WO[g ^ k, 1]], axis=1)

    def step(i, carry):
        at = slice(2 * i * T, (2 * i + 2) * T)
        slots = (2 * i, 2 * i + 1)
        att = jnp.concatenate([xs[m][:T, :] for m in slots], axis=0).astype(f32)
        cot = jnp.concatenate([cots[m][...] for m in slots], axis=0)
        for k in range(4):
            ctx = jnp.concatenate([ctxs[k][(m ^ k) * T : (m ^ k) * T + T, :] for m in slots], axis=0)
            att = att + mm(ctx, out_rows(k))
        s = lax.rsqrt(jnp.mean(att * att, axis=-1, keepdims=True) + epsilon)
        n = (att * s * gain).astype(bf16)
        normed[at, :] = n
        result = None
        gn = None
        for c in range(2):
            columns = slice(c * FH, (c + 1) * FH)
            w1 = W1[c].reshape(D, FH)
            w2 = W2[c].reshape(FH, D)
            inner = mm(n, w1)
            cdf = 0.5 * (1.0 + lax.erf(inner * root_half))
            act = (inner * cdf).astype(bf16)
            slope = cdf + inner * jnp.exp(-0.5 * inner * inner) * inv_root_tau
            part = mm(act, w2)
            result = part if result is None else result + part
            ga = mm(cot, w2, NT).astype(bf16)
            gi = (ga.astype(f32) * slope).astype(bf16)
            part = mm(gi, w1, NT)
            gn = part if gn is None else gn + part
            active[at, columns] = act
            ginner[at, columns] = gi
        for index, m in enumerate(slots):
            piece = result[index * T : (index + 1) * T]
            if m == 0:
                res0[...] = att[:T] + piece
            else:
                sends[m - 1][...] = piece.astype(bf16)
        u = gn * gain
        gain_grad[...] += jnp.sum(gn * att * s, axis=0, keepdims=True)
        grad = 0.25 * cot.astype(f32) + s * u - att * (s * s * s) * jnp.mean(u * att, axis=-1, keepdims=True)
        grads[at, :] = grad
        gb = grad.astype(bf16)
        branch[at, :] = gb
        for k in range(4):
            gc = mm(gb, out_rows(k), NT).astype(bf16)
            for index, m in enumerate(slots):
                gcs[k][(m ^ k) * T : (m ^ k) * T + T, :] = gc[index * T : (index + 1) * T]
        return carry

    for i in range(2):
        step(i, 0)


def weight_kernel(T, ids, *refs):
    g, c = ids[0], ids[3]
    normed, active, ginner, branch = refs[0:4]
    cots, ctxs = refs[4:8], refs[8:12]
    keep, send, gi, go, gw = refs[12:17]
    R = D // 8
    gi[...] = mm(normed[...], ginner[...], TN).reshape(4, 2, R, D)
    cot = jnp.concatenate([r[...] for r in cots], axis=0)
    go[...] = mm(active[...], cot, TN).reshape(2, 4, R, D)
    gb = branch[...]
    for k in range(4):
        ctx = jnp.concatenate([ctxs[k][(m ^ k) * T : (m ^ k) * T + T, :] for m in range(4)], axis=0)
        gw[g ^ k] = mm(ctx, gb, TN).reshape(2, R, D)
    for a in range(4):
        keep[0, a] = gi[a, c]
        keep[1, a] = go[c, a]
        keep[2, a] = gw[a, c]
        send[0, a] = gi[a, 1 - c].astype(bf16)
        send[1, a] = go[1 - c, a].astype(bf16)
        send[2, a] = gw[a, 1 - c].astype(bf16)


def tail_kernel(T, ids, x0, x1, x2, x3, dq, down, doth, grads, gains, w0, w1, w2, w3, wo, own, s1, s2, s3, joined, gain_grad, W):
    half, f = ids[1], ids[2]
    rows = W.shape[2]
    xs, ws, sends = (x0, x1, x2, x3), (w0, w1, w2, w3), (s1, s2, s3)
    for k in range(4):
        z = f ^ k
        W[z, half] = ws[k][:rows, :]
        W[z, 1 - half] = wo[k, :rows, :]
    weight = W[...].reshape(D, 3 * CG)
    gain = gains[0:1, :]
    gain_grad[...] = jnp.zeros_like(gain_grad)
    for i in range(2):
        at = slice(2 * i * T, (2 * i + 2) * T)
        parts = [(down[h, at, :] + doth[h, at, :].astype(f32)).astype(bf16) for h in range(HG)]
        dqkv = jnp.concatenate(parts + [dq[at, :]], axis=1)
        joined[at, :] = dqkv
        gn = mm(dqkv, weight, NT)
        x = jnp.concatenate([xs[m][:T, :] for m in (2 * i, 2 * i + 1)], axis=0).astype(f32)
        s = lax.rsqrt(jnp.mean(x * x, axis=-1, keepdims=True) + epsilon)
        u = gn * gain
        gain_grad[...] += jnp.sum(gn * x * s, axis=0, keepdims=True)
        total = grads[at, :] + s * u - x * (s * s * s) * jnp.mean(u * x, axis=-1, keepdims=True)
        for index, m in enumerate((2 * i, 2 * i + 1)):
            piece = total[index * T : (index + 1) * T]
            if m == 0:
                own[...] = piece
            else:
                sends[m - 1][...] = piece.astype(bf16)


def split_rows(value):
    high = value.astype(bf16)
    return jnp.concatenate([high, (value - high.astype(f32)).astype(bf16)], axis=0)


def project_grad_kernel(T, ids, normed, joined, second, first, table, keep, send, extra, gw):
    c = ids[3]
    R = D // 8
    gw[...] = mm(normed[...], joined[...], TN).reshape(4, 2, R, 3 * CG)
    for a in range(4):
        keep[a] = gw[a, c]
        send[a * R : (a + 1) * R, :] = gw[a, 1 - c].astype(bf16)
    wide = jnp.zeros((1, 3 * CG - D // 2), f32)
    vectors = [second[:, : D // 2], second[:, D // 2 :], first[:, : D // 2], first[:, D // 2 :], table[...]]
    block = jnp.concatenate([jnp.concatenate([v, wide], axis=1) for v in vectors], axis=0)
    block = jnp.concatenate([block, jnp.zeros((3, 3 * CG), f32)], axis=0)
    extra[...] = block
    send[4 * R :, :] = split_rows(block)


def on_device(seqs, fsdps, *args):
    (
        activations,
        segments,
        cotangent,
        attention_gain,
        query_weight,
        key_weight,
        value_weight,
        output_weight,
        bias_table,
        feedforward_gain,
        inner_weight,
        outer_weight,
    ) = args
    T = activations.shape[1]
    C = seqs // GROUPS
    fast = C == 2 and not FORCE_GENERIC
    position = lax.axis_index("seq")
    f = lax.axis_index("fsdp")
    g, c = position // C, position % C
    half = c if fast else 0
    ids = jnp.stack([g, half, f, c]).astype(jnp.int32)
    R0 = query_weight.shape[0]
    RH = R0 // 2
    F0 = outer_weight.shape[0]

    def group_move(value, k):
        pairs = [(a * C + b, (a ^ k) * C + b) for a in range(GROUPS) for b in range(C)]
        return lax.ppermute(value, "seq", pairs)

    def plane_move(value, k):
        return lax.ppermute(value, "fsdp", [(i, i ^ k) for i in range(fsdps)])

    def core_move(value):
        return lax.ppermute(value, "seq", [(i, i ^ 1) for i in range(seqs)])

    def from_group(value):
        return [value] + [group_move(value, k) for k in (1, 2, 3)]

    def from_planes(value):
        return [value] + [plane_move(value, k) for k in (1, 2, 3)]

    def both_halves(pack_of):
        if fast:
            own = from_planes(pack_of(c))
            return own, core_move(jnp.stack(own))
        return from_planes(pack_of(0)), jnp.stack(from_planes(pack_of(1)))

    def project_pack(side):
        def part(weight):
            return lax.dynamic_slice(weight, (side * RH, g * CG), (RH, CG)).reshape(RH, HG, DH)

        pairs = jnp.concatenate([part(key_weight), part(value_weight)], axis=2).reshape(RH, 2 * CG)
        columns = jnp.concatenate([pairs, part(query_weight).reshape(RH, CG)], axis=1)
        wide = columns.shape[1]
        rows = [
            jnp.pad(attention_gain[None], ((0, 0), (0, wide - R0))),
            jnp.pad(feedforward_gain[None], ((0, 6), (0, wide - R0))),
            jnp.pad(bias_table, ((0, 0), (0, wide - H))),
        ]
        return jnp.concatenate([columns] + rows, axis=0)

    def middle_pack(side):
        FB = F0 // 8
        outer = lax.dynamic_slice(outer_weight, (side * (F0 // 2) + FB * (f ^ g), 0), (FB, D))
        inner = jnp.concatenate(
            [
                lax.dynamic_slice(inner_weight, (0, z * F0 + side * (F0 // 2) + FB * (z ^ g)), (R0, FB))
                for z in range(4)
            ],
            axis=1,
        )
        out = lax.dynamic_slice(output_weight, (0, side * (D // 2)), (R0, D // 2))
        return jnp.concatenate([out, inner, outer[:, : D // 2], outer[:, D // 2 :]], axis=0)

    marks = jnp.pad(segments.astype(bf16), ((0, 15), (0, D - T)))
    xs = from_group(jnp.concatenate([activations[0], marks], axis=0))
    ws, wo = both_halves(project_pack)
    cots = from_group(cotangent[0])
    ms, mo = both_halves(middle_pack)

    normed, kv, query, gains, table = call(
        functools.partial(project_kernel, T),
        (
            shape((4 * T, D), bf16),
            shape((HG, 4 * T, 128), bf16),
            shape((HG, 4 * T, 128), bf16),
            shape((8, D), f32),
            shape((32, 128), f32),
        ),
        [ids] + xs + ws + [wo],
        scalars=1,
        scratch=[pltpu.VMEM((4, 2, RH, 3 * CG), bf16), pltpu.VMEM((4, 16, 3 * CG), f32)],
    )
    tiles = call(functools.partial(tiles_kernel, T), shape((HG, 5, T, T), f32), [ids, table], scalars=1)

    slot = jnp.arange(4, dtype=jnp.int32) ^ g
    q_at = slot * C + c
    seg_q = jnp.concatenate([x[T : T + 1, :T] for x in xs], axis=0).astype(f32)
    if fast:
        kv_pack = jnp.concatenate([kv.reshape(HG * 4 * T, 128), jnp.pad(seg_q, ((0, 12), (0, 0))).astype(bf16)], axis=0)
        kv_other = core_move(kv_pack)
        blocks = [kv, kv_other[: HG * 4 * T].reshape(HG, 4 * T, 128)]
        seg_k = jnp.concatenate([seg_q, kv_other[HG * 4 * T : HG * 4 * T + 4].astype(f32)], axis=0)
        k_at = jnp.concatenate([slot * C + c, slot * C + 1 - c])
    else:
        members = [[a * C + b for b in range(C)] for a in range(GROUPS)]
        blocks = [lax.all_gather(kv, "seq", axis=0, axis_index_groups=members)]
        seg_k = lax.all_gather(seg_q.astype(bf16), "seq", axis=0, axis_index_groups=members)
        seg_k = seg_k.reshape(C * 4, T).astype(f32)
        k_at = (slot[None, :] * C + jnp.arange(C, dtype=jnp.int32)[:, None]).reshape(C * 4)
    context, lse = call(
        functools.partial(forward_kernel, T, C, fast),
        (shape((4 * T, CG), bf16), shape((2, 8, 2 * T), f32)),
        [ids, q_at, k_at, query, seg_q, seg_k, tiles] + blocks,
        scalars=3,
        scratch=[pltpu.VMEM((C * 4, T, 128), f32)],
        mib=48,
    )
    ctxs = from_group(context)

    FH = F0 // 2
    outs = call(
        functools.partial(middle_kernel, T),
        (shape((T, D), f32),)
        + (shape((T, D), bf16),) * 3
        + (shape((4 * T, CG), bf16),) * 4
        + (shape((4 * T, D), f32),)
        + (shape((4 * T, D), bf16),) * 4
        + (shape((1, D), f32),),
        [ids] + xs + cots + ctxs + ms + [mo, gains],
        scalars=1,
        scratch=[
            pltpu.VMEM((4, 2, R0, D // 2), bf16),
            pltpu.VMEM((2, 4, R0, FH), bf16),
            pltpu.VMEM((2, 4, F0 // 8, D), bf16),
            pltpu.VMEM((8, 128), f32),
        ],
        mib=48,
    )
    res0, res_send, gcs = outs[0], outs[1:4], outs[4:8]
    grads, normed_ffn, active, ginner, branch, second_gain = outs[8:14]
    got = [gcs[0]] + [group_move(gcs[k], k) for k in (1, 2, 3)]
    res_got = [group_move(res_send[k - 1], k) for k in (1, 2, 3)]
    result = res0 + res_got[0].astype(f32) + res_got[1].astype(f32) + res_got[2].astype(f32)

    R = D // 8
    keep, send = call(
        functools.partial(weight_kernel, T),
        (shape((3, 4, R, D), f32), shape((3, 4, R, D), bf16)),
        [ids, normed_ffn, active, ginner, branch] + cots + ctxs,
        scalars=1,
        scratch=[
            pltpu.VMEM((4, 2, R, D), f32),
            pltpu.VMEM((2, 4, R, D), f32),
            pltpu.VMEM((4, 2, R, D), f32),
        ],
        mib=48,
    )

    if fast:
        back_outs = (
            shape((4 * T, CG), bf16),
            shape((HG, 4 * T, 128), f32),
            shape((HG, 4 * T, 128), bf16),
            shape((HG, 5, T, T), f32),
        )
        back_scratch = [pltpu.VMEM((C * 4, T, 128), f32), pltpu.VMEM((HG, 8 * T, 128), f32)]
    else:
        back_outs = (
            shape((4 * T, CG), bf16),
            shape((C, HG, 4 * T, 128), f32),
            shape((HG, 5, T, T), f32),
        )
        back_scratch = [pltpu.VMEM((C * 4, T, 128), f32)]
    back = call(
        functools.partial(backward_kernel, T, C, fast),
        back_outs,
        [ids, q_at, k_at, query, seg_q, seg_k, tiles, lse] + got + blocks,
        scalars=3,
        scratch=back_scratch,
        mib=48,
    )
    if fast:
        dq, down, doth, sums = back
        dmore = core_move(doth)
    else:
        dq, dall, sums = back
        down = lax.psum_scatter(dall, "seq", scatter_dimension=0, axis_index_groups=members)
        dmore = jnp.zeros((HG, 4 * T, 128), bf16)

    own, s1, s2, s3, joined, first_gain = call(
        functools.partial(tail_kernel, T),
        (shape((T, D), f32),)
        + (shape((T, D), bf16),) * 3
        + (shape((4 * T, 3 * CG), bf16), shape((1, D), f32)),
        [ids] + xs + [dq, down, dmore, grads, gains] + ws + [wo],
        scalars=1,
        scratch=[pltpu.VMEM((4, 2, RH, 3 * CG), bf16)],
    )
    parts = [group_move(v, k) for k, v in ((1, s1), (2, s2), (3, s3))]
    input_gradient = own + parts[0].astype(f32) + parts[1].astype(f32) + parts[2].astype(f32)

    table_row = call(functools.partial(table_kernel, T), shape((1, 32 * H), f32), [ids, sums], scalars=1)
    keep_p, send_p, extra = call(
        functools.partial(project_grad_kernel, T),
        (shape((4, R, 3 * CG), f32), shape((4 * R + 16, 3 * CG), bf16), shape((8, 3 * CG), f32)),
        [ids, normed, joined, second_gain, first_gain, table_row],
        scalars=1,
        scratch=[pltpu.VMEM((4, 2, R, 3 * CG), f32)],
    )

    def both(value):
        count = value.shape[0] // 2
        return value[:count].astype(f32) + value[count:].astype(f32)

    def halves(value):
        high = value.astype(bf16)
        return jnp.concatenate([high, (value - high.astype(f32)).astype(bf16)], axis=0)

    RR = R // 4
    if fast:
        total = keep + core_move(send).astype(f32)
        inner_t = total[0].reshape(4, 4, RR, D)
        outer_t = total[1]
        wout_t = total[2]

        def toward(k):
            at = f ^ k
            left = lax.dynamic_index_in_dim(inner_t, at, 1, False).reshape(R, D)
            right = lax.dynamic_index_in_dim(outer_t, at ^ g, 0, False)
            return jnp.concatenate([left, right], axis=0)

        mine = toward(0)
        for k in (1, 2, 3):
            mine = mine + plane_move(toward(k).astype(bf16), k).astype(f32)
        outer_mine = mine[R:].astype(bf16)
        inner_mine = mine[:R].reshape(4, RR, D)
        pairs = []
        for a in range(GROUPS):
            for b in range(C):
                for z in range(fsdps):
                    pairs.append(((a * C + b) * fsdps + z, ((a ^ z) * C + b) * fsdps + z))
        outer_grad = lax.ppermute(outer_mine, ("seq", "fsdp"), pairs).astype(f32)
        wout = lax.dynamic_index_in_dim(wout_t, g, 0, False)
        for k in (1, 2, 3):
            piece = lax.dynamic_index_in_dim(wout_t, g ^ k, 0, False).astype(bf16)
            wout = wout + group_move(piece, k).astype(f32)
        wout = wout.reshape(4, RR, D)

        more = core_move(send_p)
        project_t = (keep_p + more[: 4 * R].reshape(4, R, 3 * CG).astype(f32)).reshape(4, 4, RR, 3 * CG)
        extra = extra + both(more[4 * R :])
        carried = halves(extra)
        sent = []
        for k in (1, 2, 3):
            left = lax.dynamic_index_in_dim(project_t, f ^ k, 1, False).reshape(R, 3 * CG)
            right = lax.dynamic_index_in_dim(wout, f ^ k, 0, False).reshape(RR * D // (3 * CG), 3 * CG)
            block = jnp.concatenate([left, right], axis=0).astype(bf16)
            sent.append(plane_move(jnp.concatenate([block, carried], axis=0), k))
        project_m = lax.dynamic_index_in_dim(project_t, f, 1, False)
        output_grad = lax.dynamic_index_in_dim(wout, f, 0, False)
        RW = RR * D // (3 * CG)
        for piece in sent:
            project_m = project_m + piece[:R].reshape(4, RR, 3 * CG).astype(f32)
            output_grad = output_grad + piece[R : R + RW].reshape(RR, D).astype(f32)
            extra = extra + both(piece[R + RW :])
        carried = halves(extra)
        slots = []
        RI = RR * D // (3 * CG)
        for k in range(4):
            left = lax.dynamic_index_in_dim(project_m, g ^ k, 0, False)
            right = lax.dynamic_index_in_dim(inner_mine, g ^ k, 0, False).reshape(RI, 3 * CG)
            block = jnp.concatenate([left, right], axis=0).astype(bf16)
            if k == 0:
                slots.append(block)
                continue
            piece = group_move(jnp.concatenate([block, carried], axis=0), k)
            slots.append(piece[: RR + RI])
            extra = extra + both(piece[RR + RI :])
        stacked = jnp.stack(slots)
        ordered = jnp.stack([lax.dynamic_index_in_dim(stacked, g ^ a, 0, False) for a in range(4)])
        project_o = ordered[:, :RR].astype(f32)
        inner_o = ordered[:, RR:].reshape(4, RR, 2, 4, RR * 4).astype(f32)
        pairs_o = project_o[:, :, : 2 * CG].reshape(4, RR, HG, 2, DH)
        key_grad = pairs_o[:, :, :, 0].transpose(1, 0, 2, 3).reshape(RR, D)
        value_grad = pairs_o[:, :, :, 1].transpose(1, 0, 2, 3).reshape(RR, D)
        query_grad = project_o[:, :, 2 * CG :].transpose(1, 0, 2).reshape(RR, D)
        blocks_o = [inner_o[z ^ b, :, e, z] for z in range(4) for e in range(2) for b in range(4)]
        inner_grad = jnp.concatenate(blocks_o, axis=1)
    else:
        FB = F0 // 8
        axes = ("seq", "fsdp")

        def product(left, right):
            return lax.optimization_barrier(mm(left, right, TN))

        def spread(whole, axis):
            blocks = []
            for z in range(4):
                for e in range(2):
                    block = lax.slice_in_dim(whole, (4 * e + z) * FB, (4 * e + z + 1) * FB, axis=axis)
                    blocks += [block * (b == (z ^ g)).astype(f32) for b in range(4)]
            return jnp.concatenate(blocks, axis=axis)

        inner_w = spread(product(normed_ffn, ginner), 1)
        outer_w = spread(product(active, jnp.concatenate(cots, axis=0)), 0)
        out_w = jnp.zeros((4, CG, D), f32)
        for k in range(4):
            ctx = ctxs[k].reshape(4, T, CG)[jnp.array([m ^ k for m in range(4)])].reshape(4 * T, CG)
            out_w = lax.dynamic_update_slice_in_dim(out_w, product(ctx, branch)[None], g ^ k, 0)
        joined_w = product(normed, joined)
        pairs_w = joined_w[:, : 2 * CG].reshape(D, HG, 2, DH)

        def whole(part):
            return lax.dynamic_update_slice(jnp.zeros((D, D), f32), part.reshape(D, CG), (0, g * CG))

        def scatter(part):
            return lax.psum_scatter(part, axes, scatter_dimension=0, tiled=True)

        query_grad = scatter(whole(joined_w[:, 2 * CG :]))
        key_grad = scatter(whole(pairs_w[:, :, 0]))
        value_grad = scatter(whole(pairs_w[:, :, 1]))
        output_grad = scatter(out_w.reshape(D, D))
        inner_grad = scatter(inner_w)
        outer_grad = scatter(outer_w)
        extra = lax.psum(extra, axes)
    at = position * fsdps + f
    own_gain = D // (seqs * fsdps)
    second_vec = jnp.concatenate([extra[0, : D // 2], extra[1, : D // 2]])
    first_vec = jnp.concatenate([extra[2, : D // 2], extra[3, : D // 2]])
    second_grad = lax.dynamic_slice_in_dim(second_vec, at * own_gain, own_gain)
    first_grad = lax.dynamic_slice_in_dim(first_vec, at * own_gain, own_gain)
    table_grad = extra[4, : 32 * H].reshape(H, 32).T
    return (
        result[None],
        input_gradient[None],
        first_grad,
        query_grad,
        key_grad,
        value_grad,
        output_grad,
        table_grad,
        second_grad,
        inner_grad,
        outer_grad,
    )


def solution(mesh):
    return jax.shard_map(
        functools.partial(on_device, mesh.shape["seq"], mesh.shape["fsdp"]),
        mesh=mesh,
        in_specs=(
            P("fsdp", "seq", None),
            P("fsdp", "seq"),
            P("fsdp", "seq", None),
            P("fsdp"),
            P("fsdp", None),
            P("fsdp", None),
            P("fsdp", None),
            P("fsdp", None),
            P("fsdp", None),
            P("fsdp"),
            P("fsdp", None),
            P("fsdp", None),
        ),
        out_specs=(
            P("fsdp", "seq", None),
            P("fsdp", "seq", None),
            P(("seq", "fsdp")),
            P(("seq", "fsdp"), None),
            P(("seq", "fsdp"), None),
            P(("seq", "fsdp"), None),
            P(("seq", "fsdp"), None),
            P(),
            P(("seq", "fsdp")),
            P(("seq", "fsdp"), None),
            P(("seq", "fsdp"), None),
        ),
        check_vma=False,
    )
```

time: 1250 us -> 244 us (0.20); the launches traced: 1240 us -> 243 us
  waiting for transfers between devices: 871 us -> 109 us
  local copies, waits for them, and re-layouts: 171 us -> 31.8 us
  matrix products: 80.5 us -> 0 us
  blocking collectives: 73.7 us -> 0 us
  starting transfers between devices: 0.56 us -> 50.2 us
  Pallas kernels: 0 us -> 38.5 us
  between operations: 15.4 us -> 1.46 us
    reduce_scatter x7 -> x0, waiting for transfers between devices: 690 us -> none  [the longest x1 142 us: on_device(): lax.psum_scatter(inner_grad, ('seq', 'fsdp'), scatter_dimension=0, tiled=...]
    all_gather x7 -> x0, waiting for transfers between devices: 177 us -> none  [the longest x1 81.6 us: on_device(): lax.all_gather(outer_weight, 'fsdp', axis=0, tiled=True)]
    ppermute x0 -> x43, waiting for transfers between devices: none -> 109 us  [the longest x12 68 us: plane_move(): return lax.ppermute(value, 'fsdp', [(i, i ^ k) for i in range(fsdps)])]
    dot_general x40 -> x0, matrix products: 80.5 us -> none  [the longest x4 12 us: logits(): jnp.einsum('sthd,kshd->shtk', query_heads, key_part, preferred_element_ty...]
    unnamed x2 -> x0, blocking collectives: 53 us -> none
    while x80 -> x0, local copies, waits for them, and re-layouts: 50.8 us -> none
    ppermute x0 -> x43, starting transfers between devices: none -> 50.2 us  [the longest x24 28.5 us: group_move(): return lax.ppermute(value, 'seq', pairs)]
    reshape x9 -> x11, local copies, waits for them, and re-layouts: 53.3 us -> 3.36 us  [the longest x1 0.8 us: on_device(): key_grad = pairs_o[:, :, :, 0].transpose(1, 0, 2, 3).reshape(RR, D)]
  transfers between devices with their start and end apart: 14 -> 43, of which waited for: 13 -> 19; matrix products, arithmetic and copies ran while one was open for 12% -> 9% of each run, Pallas kernels for 0% -> 9%
where the time goes in v1:
time: 244 us; the launch traced here: 243 us
  waiting for transfers between devices  109 us (45%)
  starting transfers between devices  50.2 us (21%)
  Pallas kernels  38.5 us (16%)
  local copies, waits for them, and re-layouts  31.8 us (13%)
  other arithmetic  11.8 us (5%)
    ppermute x12, waiting for transfers between devices, plane_move(): return lax.ppermute(value, 'fsdp', [(i, i ^ k) for i in range(fsdps)])  68 us
    ppermute x24, waiting for transfers between devices, group_move(): return lax.ppermute(value, 'seq', pairs)  41.3 us
    pallas_call x9, Pallas kernels, call(): pl.pallas_call(kernel, out_shape=outs, in_specs=[smem] * scalars + [vmem]...  38.5 us
    ppermute x24, starting transfers between devices, group_move(): return lax.ppermute(value, 'seq', pairs)  28.5 us
    ppermute x12, starting transfers between devices, plane_move(): return lax.ppermute(value, 'fsdp', [(i, i ^ k) for i in range(fsdps)])  19.9 us
    unnamed x66, local copies, waits for them, and re-layouts  17.8 us
  transfers between devices with their start and end apart: 43, of which 19 were waited for; matrix products, arithmetic and copies ran while one was open for 9% of the time, Pallas kernels for 9%

profile of v1, /device:TPU:0, one launch (start us, length us, event | category | flops | bytes accessed | tf_op | source)
XLA Modules:
  0.0 243.1 jit_solution(1125638437185057390)
XLA Ops:
  3.9 3.1 %collective-permute-start.14 = (bf16[576,384]{1,0:T(8,128)(2,1)S(1)}, bf16[576,384]{1,0:T(8,128)(2,1)S(1)}, u32[]{:S(2)}, u32[]{:S(2)}) collective-permute-start(bf16[576,384]{1,0:T(8,128)(2,1)S(1)} %pad_maximum_fusion.2.refs_12_), channel_id=1, source_target_pairs={{0,1},{1,0},{2,3},{3,2},{4,5},{5,4},{6,7},{7,6},{8,9},{9,8},{10,11... | collective-permute-start | bytes 1327112 | tf_op jit(solution)/shard_map/ppermute | solution.py:456
  7.0 2.6 %collective-permute-start.15 = (bf16[576,384]{1,0:T(8,128)(2,1)S(1)}, bf16[576,384]{1,0:T(8,128)(2,1)S(1)}, u32[]{:S(2)}, u32[]{:S(2)}) collective-permute-start(bf16[576,384]{1,0:T(8,128)(2,1)S(1)} %pad_maximum_fusion.2.refs_12_), channel_id=1, source_target_pairs={{0,2},{1,3},{2,0},{3,1},{4,6},{5,7},{6,4},{7,5},{8,10},{9,11},{10,... | collective-permute-start | bytes 1327112 | tf_op jit(solution)/shard_map/ppermute | solution.py:456
  13.0 2.0 collective-permute-start.7
  15.0 2.0 collective-permute-start.8
  17.1 8.7 %collective-permute-done.14.refs_13_ = bf16[576,384]{1,0:T(8,128)(2,1)S(1)} collective-permute-done((bf16[576,384]{1,0:T(8,128)(2,1)S(1)}, bf16[576,384]{1,0:T(8,128)(2,1)S(1)}, u32[]{:S(2)}, u32[]{:S(2)}) %collective-permute-start.14) | collective-permute-done | bytes 442400 | tf_op jit(solution)/shard_map/ppermute | solution.py:456
  25.8 20.3 %collective-permute-done.15.refs_14_ = bf16[576,384]{1,0:T(8,128)(2,1)S(1)} collective-permute-done((bf16[576,384]{1,0:T(8,128)(2,1)S(1)}, bf16[576,384]{1,0:T(8,128)(2,1)S(1)}, u32[]{:S(2)}, u32[]{:S(2)}) %collective-permute-start.15) | collective-permute-done | bytes 442400 | tf_op jit(solution)/shard_map/ppermute | solution.py:456
  46.9 11.8 %collective-permute-done.7.w2 = bf16[112,576]{1,0:T(8,128)(2,1)S(1)} collective-permute-done((bf16[112,576]{1,0:T(8,128)(2,1)S(1)}, bf16[112,576]{1,0:T(8,128)(2,1)S(1)}, u32[]{:S(2)}, u32[]{:S(2)}) %collective-permute-start.7) | collective-permute-done | bytes 129056 | tf_op jit(solution)/shard_map/ppermute | solution.py:456
  62.6 4.7 %collective-permute-done.x1.refs_1_ = bf16[144,768]{1,0:T(8,128)(2,1)S(1)} collective-permute-done((bf16[144,768]{1,0:T(8,128)(2,1)S(1)}, bf16[144,768]{1,0:T(8,128)(2,1)S(1)}, u32[]{:S(2)}, u32[]{:S(2)}) %collective-permute-start) | collective-permute-done | bytes 221216 | tf_op jit(solution)/shard_map/ppermute | solution.py:453
  67.3 5.5 %collective-permute-done.1.x2.refs_2_ = bf16[144,768]{1,0:T(8,128)(2,1)S(1)} collective-permute-done((bf16[144,768]{1,0:T(8,128)(2,1)S(1)}, bf16[144,768]{1,0:T(8,128)(2,1)S(1)}, u32[]{:S(2)}, u32[]{:S(2)}) %collective-permute-start.1) | collective-permute-done | bytes 221216 | tf_op jit(solution)/shard_map/ppermute | solution.py:453
  79.7 5.3 %shard_map.205 = (bf16[512,192]{1,0:T(8,128)(2,1)S(1)}, f32[2,8,256]{2,1,0:T(8,128)S(1)}) custom-call(s32[4]{0:T(128)S(1)} %pad_add_fusion.ids, s32[4]{0:T(128)S(1)} %get-tuple-element.174.q_at, s32[8]{0:T(128)S(1)} %pad_add_fusion.1.k_at, bf16[3,512,128]{2,1,0:T(8,128)(2,1)S(1)} %get-tuple-element.47.query, f32[4,128]{1,0:T(4,128)S(1)} %get-tuple-element.93.seg_q, ...), custom_call_target="tpu_custom_call" | custom-call | tf_op jit(solution)/shard_map/pallas_call | solution.py:46
  88.8 5.5 %collective-permute-done.11.refs_9_ = bf16[512,192]{1,0:T(8,128)(2,1)S(1)} collective-permute-done((bf16[512,192]{1,0:T(8,128)(2,1)S(1)}, bf16[512,192]{1,0:T(8,128)(2,1)S(1)}, u32[]{:S(2)}, u32[]{:S(2)}) %collective-permute-start.11) | collective-permute-done | bytes 196640 | tf_op jit(solution)/shard_map/ppermute | solution.py:453
  94.4 3.5 %collective-permute-done.12.refs_10_ = bf16[512,192]{1,0:T(8,128)(2,1)S(1)} collective-permute-done((bf16[512,192]{1,0:T(8,128)(2,1)S(1)}, bf16[512,192]{1,0:T(8,128)(2,1)S(1)}, u32[]{:S(2)}, u32[]{:S(2)}) %collective-permute-start.12) | collective-permute-done | bytes 196640 | tf_op jit(solution)/shard_map/ppermute | solution.py:453
  97.9 1.6 collective-permute-done.13.refs_11_
  100.7 10.5 %shard_map.206 = (f32[128,768]{1,0:T(8,128)S(1)}, bf16[128,768]{1,0:T(8,128)(2,1)}, bf16[128,768]{1,0:T(8,128)(2,1)}, bf16[128,768]{1,0:T(8,128)(2,1)}, bf16[512...) custom-call(s32[4]{0:T(128)S(1)} %pad_add_fusion.ids, ...), custom_call_target="tpu_custom_call" | custom-call | tf_op jit(solution)/shard_map/pallas_call | solution.py:46
  115.9 5.1 %shard_map.211 = (f32[3,4,96,768]{3,2,1,0:T(8,128)}, bf16[3,4,96,768]{3,2,1,0:T(8,128)(2,1)}) custom-call(s32[4]{0:T(128)S(1)} %pad_add_fusion.ids, bf16[512,768]{1,0:T(8,128)(2,1)S(1)} %copy-done.11, bf16[512,768]{1,0:T(8,128)(2,1)S(1)} %copy-done.12, bf16[512,768]{1,0:T(8,128)(2,1)S(1)} %copy-done.13, bf16[512,768]{1,0:T(8,128)(2,1)S(1)} %copy-done.14, ...), custom_call_target="tpu_custom_call" | custom-call | tf_op jit(solution)/shard_map/pallas_call | solution.py:46
  124.5 5.6 %collective-permute-done.21.g1 = bf16[512,192]{1,0:T(8,128)(2,1)S(1)} collective-permute-done((bf16[512,192]{1,0:T(8,128)(2,1)S(1)}, bf16[512,192]{1,0:T(8,128)(2,1)S(1)}, u32[]{:S(2)}, u32[]{:S(2)}) %collective-permute-start.21) | collective-permute-done | bytes 196640 | tf_op jit(solution)/shard_map/ppermute | solution.py:453
  130.1 5.8 %collective-permute-done.22.g2 = bf16[512,192]{1,0:T(8,128)(2,1)S(1)} collective-permute-done((bf16[512,192]{1,0:T(8,128)(2,1)S(1)}, bf16[512,192]{1,0:T(8,128)(2,1)S(1)}, u32[]{:S(2)}, u32[]{:S(2)}) %collective-permute-start.22) | collective-permute-done | bytes 196640 | tf_op jit(solution)/shard_map/ppermute | solution.py:453
  135.8 8.4 %shard_map.207 = (bf16[512,192]{1,0:T(8,128)(2,1)S(1)}, f32[3,512,128]{2,1,0:T(8,128)S(1)}, bf16[3,512,128]{2,1,0:T(8,128)(2,1)}, f32[3,5,128,128]{3,2,1,0:T(8,128)S(1)}) custom-call(s32[4]{0:T(128)S(1)} %pad_add_fusion.ids, s32[4]{0:T(128)S(1)} %get-tuple-element.174.q_at, s32[8]{0:T(128)S(1)} %pad_add_fusion.1.k_at, ...), custom_call_target="tpu_custom_call" | custom-call | tf_op jit(solution)/shard_map/pallas_call | solution.py:46
  151.5 2.2 shard_map.209.table
  158.6 2.5 %shard_map.208 = (f32[128,768]{1,0:T(8,128)S(1)}, bf16[128,768]{1,0:T(8,128)(2,1)S(1)}, bf16[128,768]{1,0:T(8,128)(2,1)S(1)}, bf16[128,768]{1,0:T(8,128)(2,1)S(1...) custom-call(s32[4]{0:T(128)S(1)} %pad_add_fusion.ids, bf16[144,768]{1,0:T(8,128)(2,1)S(1)} %fusion.14.x0.refs_0_, ...), custom_call_target="tpu_custom_call" | custom-call | tf_op jit(solution)/shard_map/pallas_call | solution.py:46
  166.2 2.0 add_bitcast_fusion.1
  168.2 2.3 collective-permute-done.25
  170.4 3.1 %collective-permute-done.26 = bf16[128,768]{1,0:T(8,128)(2,1)S(1)} collective-permute-done((bf16[128,768]{1,0:T(8,128)(2,1)S(1)}, bf16[128,768]{1,0:T(8,128)(2,1)S(1)}, u32[]{:S(2)}, u32[]{:S(2)}) %collective-permute-start.26) | collective-permute-done | bytes 196640 | tf_op jit(solution)/shard_map/ppermute | solution.py:453
  173.5 1.6 collective-permute-done.27
  176.2 1.8 copy-done.23
  178.0 1.9 convert_add_fusion
  184.6 2.2 collective-permute-start.36
  193.2 1.9 collective-permute-start.34
  195.1 4.8 %collective-permute-done.36 = bf16[192,768]{1,0:T(8,128)(2,1)S(1)} collective-permute-done((bf16[192,768]{1,0:T(8,128)(2,1)}, bf16[192,768]{1,0:T(8,128)(2,1)S(1)}, u32[]{:S(2)}, u32[]{:S(2)}) %collective-permute-start.36) | collective-permute-done | bytes 294944 | tf_op jit(solution)/shard_map/ppermute | solution.py:456
  199.9 2.7 %collective-permute-start.35 = (bf16[144,576]{1,0:T(8,128)(2,1)}, bf16[144,576]{1,0:T(8,128)(2,1)S(1)}, u32[]{:S(2)}, u32[]{:S(2)}) collective-permute-start(bf16[144,576]{1,0:T(8,128)(2,1)} %get-tuple-element.172), channel_id=1, source_target_pairs={{0,3},{1,2},{2,1},{3,0},{4,7},{5,6},{6,5},{7,4},{8,11},{9,10},{10,... | collective-permute-start | bytes 497672 | tf_op jit(solution)/shard_map/ppermute | solution.py:456
  202.5 10.5 %collective-permute-done.37 = bf16[192,768]{1,0:T(8,128)(2,1)} collective-permute-done((bf16[192,768]{1,0:T(8,128)(2,1)}, bf16[192,768]{1,0:T(8,128)(2,1)}, u32[]{:S(2)}, u32[]{:S(2)}) %collective-permute-start.37) | collective-permute-done | bytes 294944 | tf_op jit(solution)/shard_map/ppermute | solution.py:456
  217.0 12.0 %collective-permute-done.34 = bf16[144,576]{1,0:T(8,128)(2,1)S(1)} collective-permute-done((bf16[144,576]{1,0:T(8,128)(2,1)}, bf16[144,576]{1,0:T(8,128)(2,1)S(1)}, u32[]{:S(2)}, u32[]{:S(2)}) %collective-permute-start.34) | collective-permute-done | bytes 165920 | tf_op jit(solution)/shard_map/ppermute | solution.py:456
  (229 shorter events, 78.4 us)
Async XLA Ops:
  3.9 21.9 %collective-permute-start.14 = (bf16[576,384]{1,0:T(8,128)(2,1)S(1)}, bf16[576,384]{1,0:T(8,128)(2,1)S(1)}, u32[]{:S(2)}, u32[]{:S(2)}) collective-permute-start(bf16[576,384]{1,0:T(8,128)(2,1)S(1)} %pad_maximum_fusion.2.refs_12_), channel_id=1, source_target_pairs={{0,1},{1,0},{2,3},{3,2},{4,5},{5,4},{6,7},{7,6},{8,9},{9,8},{10,11... | collective-permute-start | bytes 1327112 | tf_op jit(solution)/shard_map/ppermute | solution.py:456
  7.0 39.2 %collective-permute-start.15 = (bf16[576,384]{1,0:T(8,128)(2,1)S(1)}, bf16[576,384]{1,0:T(8,128)(2,1)S(1)}, u32[]{:S(2)}, u32[]{:S(2)}) collective-permute-start(bf16[576,384]{1,0:T(8,128)(2,1)S(1)} %pad_maximum_fusion.2.refs_12_), channel_id=1, source_target_pairs={{0,2},{1,3},{2,0},{3,1},{4,6},{5,7},{6,4},{7,5},{8,10},{9,11},{10,... | collective-permute-start | bytes 1327112 | tf_op jit(solution)/shard_map/ppermute | solution.py:456
  9.6 36.6 %collective-permute-start.16 = (bf16[576,384]{1,0:T(8,128)(2,1)S(1)}, bf16[576,384]{1,0:T(8,128)(2,1)S(1)}, u32[]{:S(2)}, u32[]{:S(2)}) collective-permute-start(bf16[576,384]{1,0:T(8,128)(2,1)S(1)} %pad_maximum_fusion.2.refs_12_), channel_id=1, source_target_pairs={{0,3},{1,2},{2,1},{3,0},{4,7},{5,6},{6,5},{7,4},{8,11},{9,10},{10,... | collective-permute-start | bytes 1327112 | tf_op jit(solution)/shard_map/ppermute | solution.py:456
  13.0 45.7 %collective-permute-start.7 = (bf16[112,576]{1,0:T(8,128)(2,1)S(1)}, bf16[112,576]{1,0:T(8,128)(2,1)S(1)}, u32[]{:S(2)}, u32[]{:S(2)}) collective-permute-start(bf16[112,576]{1,0:T(8,128)(2,1)S(1)} %fusion.23.w0), channel_id=1, source_target_pairs={{0,2},{1,3},{2,0},{3,1},{4,6},{5,7},{6,4},{7,5},{8,10},{9,11},{10,... | collective-permute-start | bytes 387080 | tf_op jit(solution)/shard_map/ppermute | solution.py:456
  15.0 43.7 %collective-permute-start.8 = (bf16[112,576]{1,0:T(8,128)(2,1)S(1)}, bf16[112,576]{1,0:T(8,128)(2,1)S(1)}, u32[]{:S(2)}, u32[]{:S(2)}) collective-permute-start(bf16[112,576]{1,0:T(8,128)(2,1)S(1)} %fusion.23.w0), channel_id=1, source_target_pairs={{0,3},{1,2},{2,1},{3,0},{4,7},{5,6},{6,5},{7,4},{8,11},{9,10},{10,... | collective-permute-start | bytes 387080 | tf_op jit(solution)/shard_map/ppermute | solution.py:456
  25.8 32.9 %collective-permute-start.6 = (bf16[112,576]{1,0:T(8,128)(2,1)S(1)}, bf16[112,576]{1,0:T(8,128)(2,1)S(1)}, u32[]{:S(2)}, u32[]{:S(2)}) collective-permute-start(bf16[112,576]{1,0:T(8,128)(2,1)S(1)} %fusion.23.w0), channel_id=1, source_target_pairs={{0,1},{1,0},{2,3},{3,2},{4,5},{5,4},{6,7},{7,6},{8,9},{9,8},{10,11... | collective-permute-start | bytes 387080 | tf_op jit(solution)/shard_map/ppermute | solution.py:456
  46.9 52.6 %collective-permute-start.17 = (bf16[4,576,384]{2,1,0:T(8,128)(2,1)S(1)}, bf16[4,576,384]{2,1,0:T(8,128)(2,1)S(1)}, u32[]{:S(2)}, u32[]{:S(2)}) collective-permute-start(bf16[4,576,384]{2,1,0:T(8,128)(2,1)S(1)} %pad_maximum_fusion), channel_id=1, source_target_pairs={{0,4},{4,0},{8,12},{12,8},{16,20},{20,16},{24,28},{28,24},{1,5},{5... | collective-permute-start | bytes 5308424 | tf_op jit(solution)/shard_map/ppermute | solution.py:459
  58.9 14.0 %collective-permute-start.9 = (bf16[4,112,576]{2,1,0:T(8,128)(2,1)S(1)}, bf16[4,112,576]{2,1,0:T(8,128)(2,1)S(1)}, u32[]{:S(2)}, u32[]{:S(2)}) collective-permute-start(bf16[4,112,576]{2,1,0:T(8,128)(2,1)S(1)} %pad_maximum_fusion.1), channel_id=1, source_target_pairs={{0,4},{4,0},{8,12},{12,8},{16,20},{20,16},{24,28},{28,24},{1,5},{5... | collective-permute-start | bytes 1548296 | tf_op jit(solution)/shard_map/ppermute | solution.py:459
  60.5 12.3 %collective-permute-start.1 = (bf16[144,768]{1,0:T(8,128)(2,1)S(1)}, bf16[144,768]{1,0:T(8,128)(2,1)S(1)}, u32[]{:S(2)}, u32[]{:S(2)}) collective-permute-start(bf16[144,768]{1,0:T(8,128)(2,1)S(1)} %fusion.14.x0.refs_0_), channel_id=1, source_target_pairs={{0,16},{4,20},{8,24},{12,28},{16,0},{20,4},{24,8},{28,12},{1,17},{... | collective-permute-start | bytes 663560 | tf_op jit(solution)/shard_map/ppermute | solution.py:453
  62.0 10.8 %collective-permute-start.2 = (bf16[144,768]{1,0:T(8,128)(2,1)S(1)}, bf16[144,768]{1,0:T(8,128)(2,1)S(1)}, u32[]{:S(2)}, u32[]{:S(2)}) collective-permute-start(bf16[144,768]{1,0:T(8,128)(2,1)S(1)} %fusion.14.x0.refs_0_), channel_id=1, source_target_pairs={{0,24},{4,28},{8,16},{12,20},{16,8},{20,12},{24,0},{28,4},{1,25},{... | collective-permute-start | bytes 663560 | tf_op jit(solution)/shard_map/ppermute | solution.py:453
  74.6 11.8 %collective-permute-start.3 = (bf16[128,768]{1,0:T(8,128)(2,1)S(1)}, bf16[128,768]{1,0:T(8,128)(2,1)S(1)}, u32[]{:S(2)}, u32[]{:S(2)}) collective-permute-start(bf16[128,768]{1,0:T(8,128)(2,1)S(1)} %bitcast.220), channel_id=1, source_target_pairs={{0,8},{4,12},{8,0},{12,4},{16,24},{20,28},{24,16},{28,20},{1,9},{5... | collective-permute-start | bytes 589832 | tf_op jit(solution)/shard_map/ppermute | solution.py:453
  75.9 11.3 %collective-permute-start.4 = (bf16[128,768]{1,0:T(8,128)(2,1)S(1)}, bf16[128,768]{1,0:T(8,128)(2,1)S(1)}, u32[]{:S(2)}, u32[]{:S(2)}) collective-permute-start(bf16[128,768]{1,0:T(8,128)(2,1)S(1)} %bitcast.221), channel_id=1, source_target_pairs={{0,16},{4,20},{8,24},{12,28},{16,0},{20,4},{24,8},{28,12},{1,17},{... | collective-permute-start | bytes 589832 | tf_op jit(solution)/shard_map/ppermute | solution.py:453
  76.7 12.1 %collective-permute-start.5 = (bf16[128,768]{1,0:T(8,128)(2,1)S(1)}, bf16[128,768]{1,0:T(8,128)(2,1)S(1)}, u32[]{:S(2)}, u32[]{:S(2)}) collective-permute-start(bf16[128,768]{1,0:T(8,128)(2,1)S(1)} %bitcast.222), channel_id=1, source_target_pairs={{0,24},{4,28},{8,16},{12,20},{16,8},{20,12},{24,0},{28,4},{1,25},{... | collective-permute-start | bytes 589832 | tf_op jit(solution)/shard_map/ppermute | solution.py:453
  86.4 11.5 %collective-permute-start.12 = (bf16[512,192]{1,0:T(8,128)(2,1)S(1)}, bf16[512,192]{1,0:T(8,128)(2,1)S(1)}, u32[]{:S(2)}, u32[]{:S(2)}) collective-permute-start(bf16[512,192]{1,0:T(8,128)(2,1)S(1)} %get-tuple-element.50.refs_8_), channel_id=1, source_target_pairs={{0,16},{4,20},{8,24},{12,28},{16,0},{20,4},{24,8},{28,12},{1,17},{... | collective-permute-start | bytes 589832 | tf_op jit(solution)/shard_map/ppermute | solution.py:453
  87.2 12.3 %collective-permute-start.13 = (bf16[512,192]{1,0:T(8,128)(2,1)S(1)}, bf16[512,192]{1,0:T(8,128)(2,1)S(1)}, u32[]{:S(2)}, u32[]{:S(2)}) collective-permute-start(bf16[512,192]{1,0:T(8,128)(2,1)S(1)} %get-tuple-element.50.refs_8_), channel_id=1, source_target_pairs={{0,24},{4,28},{8,16},{12,20},{16,8},{20,12},{24,0},{28,4},{1,25},{... | collective-permute-start | bytes 589832 | tf_op jit(solution)/shard_map/ppermute | solution.py:453
  121.0 55.2 %collective-permute-start.29 = (bf16[3,4,96,768]{3,2,1,0:T(8,128)(2,1)}, bf16[3,4,96,768]{3,2,1,0:T(8,128)(2,1)}, u32[]{:S(2)}, u32[]{:S(2)}) collective-permute-start(bf16[3,4,96,768]{3,2,1,0:T(8,128)(2,1)} %get-tuple-element.82), channel_id=1, source_target_pairs={{0,4},{4,0},{8,12},{12,8},{16,20},{20,16},{24,28},{28,24},{1,5},{5... | collective-permute-start | bytes 5308424 | tf_op jit(solution)/shard_map/ppermute | solution.py:459
  121.8 14.1 %collective-permute-start.22 = (bf16[512,192]{1,0:T(8,128)(2,1)S(1)}, bf16[512,192]{1,0:T(8,128)(2,1)S(1)}, u32[]{:S(2)}, u32[]{:S(2)}) collective-permute-start(bf16[512,192]{1,0:T(8,128)(2,1)S(1)} %get-tuple-element.59), channel_id=1, source_target_pairs={{0,16},{4,20},{8,24},{12,28},{16,0},{20,4},{24,8},{28,12},{1,17},{... | collective-permute-start | bytes 589832 | tf_op jit(solution)/shard_map/ppermute | solution.py:453
  123.3 12.5 %collective-permute-start.23 = (bf16[512,192]{1,0:T(8,128)(2,1)S(1)}, bf16[512,192]{1,0:T(8,128)(2,1)S(1)}, u32[]{:S(2)}, u32[]{:S(2)}) collective-permute-start(bf16[512,192]{1,0:T(8,128)(2,1)S(1)} %get-tuple-element.60), channel_id=1, source_target_pairs={{0,24},{4,28},{8,16},{12,20},{16,8},{20,12},{24,0},{28,4},{1,25},{... | collective-permute-start | bytes 589832 | tf_op jit(solution)/shard_map/ppermute | solution.py:453
  146.8 15.8 %collective-permute-start.18 = (bf16[128,768]{1,0:T(8,128)(2,1)}, bf16[128,768]{1,0:T(8,128)(2,1)}, u32[]{:S(2)}, u32[]{:S(2)}) collective-permute-start(bf16[128,768]{1,0:T(8,128)(2,1)} %get-tuple-element.53), channel_id=1, source_target_pairs={{0,8},{4,12},{8,0},{12,4},{16,24},{20,28},{24,16},{28,20},{1,9},{5... | collective-permute-start | bytes 589832 | tf_op jit(solution)/shard_map/ppermute | solution.py:453
  148.0 15.9 %collective-permute-start.19 = (bf16[128,768]{1,0:T(8,128)(2,1)}, bf16[128,768]{1,0:T(8,128)(2,1)}, u32[]{:S(2)}, u32[]{:S(2)}) collective-permute-start(bf16[128,768]{1,0:T(8,128)(2,1)} %get-tuple-element.54), channel_id=1, source_target_pairs={{0,16},{4,20},{8,24},{12,28},{16,0},{20,4},{24,8},{28,12},{1,17},{... | collective-permute-start | bytes 589832 | tf_op jit(solution)/shard_map/ppermute | solution.py:453
  148.9 15.9 %collective-permute-start.20 = (bf16[128,768]{1,0:T(8,128)(2,1)}, bf16[128,768]{1,0:T(8,128)(2,1)}, u32[]{:S(2)}, u32[]{:S(2)}) collective-permute-start(bf16[128,768]{1,0:T(8,128)(2,1)} %get-tuple-element.55), channel_id=1, source_target_pairs={{0,24},{4,28},{8,16},{12,20},{16,8},{20,12},{24,0},{28,4},{1,25},{... | collective-permute-start | bytes 589832 | tf_op jit(solution)/shard_map/ppermute | solution.py:453
  162.5 13.4 %collective-permute-start.28 = (bf16[400,576]{1,0:T(8,128)(2,1)S(1)}, bf16[400,576]{1,0:T(8,128)(2,1)S(1)}, u32[]{:S(2)}, u32[]{:S(2)}) collective-permute-start(bf16[400,576]{1,0:T(8,128)(2,1)S(1)} %get-tuple-element.75), channel_id=1, source_target_pairs={{0,4},{4,0},{8,12},{12,8},{16,20},{20,16},{24,28},{28,24},{1,5},{5... | collective-permute-start | bytes 1382408 | tf_op jit(solution)/shard_map/ppermute | solution.py:459
  163.9 9.6 %collective-permute-start.26 = (bf16[128,768]{1,0:T(8,128)(2,1)S(1)}, bf16[128,768]{1,0:T(8,128)(2,1)S(1)}, u32[]{:S(2)}, u32[]{:S(2)}) collective-permute-start(bf16[128,768]{1,0:T(8,128)(2,1)S(1)} %get-tuple-element.67), channel_id=1, source_target_pairs={{0,16},{4,20},{8,24},{12,28},{16,0},{20,4},{24,8},{28,12},{1,17},{... | collective-permute-start | bytes 589832 | tf_op jit(solution)/shard_map/ppermute | solution.py:453
  164.8 10.4 %collective-permute-start.27 = (bf16[128,768]{1,0:T(8,128)(2,1)S(1)}, bf16[128,768]{1,0:T(8,128)(2,1)S(1)}, u32[]{:S(2)}, u32[]{:S(2)}) collective-permute-start(bf16[128,768]{1,0:T(8,128)(2,1)S(1)} %get-tuple-element.68), channel_id=1, source_target_pairs={{0,24},{4,28},{8,16},{12,20},{16,8},{20,12},{24,0},{28,4},{1,25},{... | collective-permute-start | bytes 589832 | tf_op jit(solution)/shard_map/ppermute | solution.py:453
  181.1 9.8 %collective-permute-start.31 = (bf16[96,768]{1,0:T(8,128)(2,1)S(1)}, bf16[96,768]{1,0:T(8,128)(2,1)S(1)}, u32[]{:S(2)}, u32[]{:S(2)}) collective-permute-start(bf16[96,768]{1,0:T(8,128)(2,1)S(1)} %get-tuple-element.106), channel_id=1, source_target_pairs={{0,16},{4,20},{8,24},{12,28},{16,0},{20,4},{24,8},{28,12},{1,17},{... | collective-permute-start | bytes 442376 | tf_op jit(solution)/shard_map/ppermute | solution.py:453
  184.6 15.2 %collective-permute-start.36 = (bf16[192,768]{1,0:T(8,128)(2,1)}, bf16[192,768]{1,0:T(8,128)(2,1)S(1)}, u32[]{:S(2)}, u32[]{:S(2)}) collective-permute-start(bf16[192,768]{1,0:T(8,128)(2,1)} %pad_maximum_fusion.9), channel_id=1, source_target_pairs={{0,1},{1,0},{2,3},{3,2},{4,5},{5,4},{6,7},{7,6},{8,9},{9,8},{10,11... | collective-permute-start | bytes 884744 | tf_op jit(solution)/shard_map/ppermute | solution.py:456
  187.6 25.4 %collective-permute-start.37 = (bf16[192,768]{1,0:T(8,128)(2,1)}, bf16[192,768]{1,0:T(8,128)(2,1)}, u32[]{:S(2)}, u32[]{:S(2)}) collective-permute-start(bf16[192,768]{1,0:T(8,128)(2,1)} %pad_maximum_fusion.10), channel_id=1, source_target_pairs={{0,2},{1,3},{2,0},{3,1},{4,6},{5,7},{6,4},{7,5},{8,10},{9,11},{10,... | collective-permute-start | bytes 884744 | tf_op jit(solution)/shard_map/ppermute | solution.py:456
  189.4 23.6 %collective-permute-start.38 = (bf16[192,768]{1,0:T(8,128)(2,1)}, bf16[192,768]{1,0:T(8,128)(2,1)}, u32[]{:S(2)}, u32[]{:S(2)}) collective-permute-start(bf16[192,768]{1,0:T(8,128)(2,1)} %pad_maximum_fusion.11), channel_id=1, source_target_pairs={{0,3},{1,2},{2,1},{3,0},{4,7},{5,6},{6,5},{7,4},{8,11},{9,10},{10,... | collective-permute-start | bytes 884744 | tf_op jit(solution)/shard_map/ppermute | solution.py:456
  192.2 24.8 %collective-permute-start.33 = (bf16[144,576]{1,0:T(8,128)(2,1)}, bf16[144,576]{1,0:T(8,128)(2,1)S(1)}, u32[]{:S(2)}, u32[]{:S(2)}) collective-permute-start(bf16[144,576]{1,0:T(8,128)(2,1)} %get-tuple-element.170), channel_id=1, source_target_pairs={{0,1},{1,0},{2,3},{3,2},{4,5},{5,4},{6,7},{7,6},{8,9},{9,8},{10,11... | collective-permute-start | bytes 497672 | tf_op jit(solution)/shard_map/ppermute | solution.py:456
  193.2 35.8 %collective-permute-start.34 = (bf16[144,576]{1,0:T(8,128)(2,1)}, bf16[144,576]{1,0:T(8,128)(2,1)S(1)}, u32[]{:S(2)}, u32[]{:S(2)}) collective-permute-start(bf16[144,576]{1,0:T(8,128)(2,1)} %get-tuple-element.171), channel_id=1, source_target_pairs={{0,2},{1,3},{2,0},{3,1},{4,6},{5,7},{6,4},{7,5},{8,10},{9,11},{10,... | collective-permute-start | bytes 497672 | tf_op jit(solution)/shard_map/ppermute | solution.py:456
  199.9 29.1 %collective-permute-start.35 = (bf16[144,576]{1,0:T(8,128)(2,1)}, bf16[144,576]{1,0:T(8,128)(2,1)S(1)}, u32[]{:S(2)}, u32[]{:S(2)}) collective-permute-start(bf16[144,576]{1,0:T(8,128)(2,1)} %get-tuple-element.172), channel_id=1, source_target_pairs={{0,3},{1,2},{2,1},{3,0},{4,7},{5,6},{6,5},{7,4},{8,11},{9,10},{10,... | collective-permute-start | bytes 497672 | tf_op jit(solution)/shard_map/ppermute | solution.py:456
  215.4 27.0 %collective-permute-start.42 = (bf16[96,768]{1,0:T(8,128)(2,1)}, bf16[96,768]{1,0:T(8,128)(2,1)S(1)}, u32[]{:S(2)}, u32[]{:S(2)}) collective-permute-start(bf16[96,768]{1,0:T(8,128)(2,1)} %get-tuple-element.148), channel_id=1, source_target_pairs={{0,0},{1,9},{2,18},{3,27},{4,4},{5,13},{6,22},{7,31},{8,8},{9,1},{... | collective-permute-start | bytes 442376 | tf_op jit(solution)/shard_map/ppermute | solution.py:668
  (42 other events, 310.0 us)

commit v2 on v1

v2 whole, which is shorter than its diff:
```python
import functools

import jax
import jax.numpy as jnp
from jax import lax
from jax.experimental import pallas as pl
from jax.experimental.pallas import tpu as pltpu
from jax.sharding import PartitionSpec as P

D = 768
H = 12
DH = 64
GROUPS = 4
HG = H // GROUPS
CG = HG * DH

epsilon = 1e-06
FORCE_GENERIC = False
SCALE = 10**6
neg_fill = -1e30
limits = (12, 16, 23, 32, 46, 64, 91)
root_half = 0.7071067811865476
inv_root_tau = 0.3989422804014327
bf16 = jnp.bfloat16
f32 = jnp.float32
NT = (((1,), (1,)), ((), ()))
TN = (((0,), (0,)), ((), ()))
NN = (((1,), (0,)), ((), ()))


def mm(a, b, dims=NN):
    return lax.dot_general(a, b, dims, preferred_element_type=f32)


def bucket_of(offset):
    distance = jnp.abs(offset)
    farther = jnp.zeros_like(offset) + 8
    for limit in limits:
        farther = farther + (distance >= limit).astype(jnp.int32)
    nearer = jnp.where(distance < 8, distance, farther)
    return nearer + jnp.where(offset > 0, 16, 0)


def call(kernel, outs, args, scalars=1, scratch=(), mib=16, us=2, far=()):
    vmem = pl.BlockSpec(memory_space=pltpu.VMEM)
    smem = pl.BlockSpec(memory_space=pltpu.SMEM)
    hbm = pl.BlockSpec(memory_space=pltpu.HBM)
    return pl.pallas_call(
        kernel,
        out_shape=outs,
        in_specs=[smem] * scalars + [hbm if n in far else vmem for n in range(scalars, len(args))],
        out_specs=jax.tree.map(lambda _: vmem, outs),
        scratch_shapes=scratch,
        compiler_params=pltpu.CompilerParams(vmem_limit_bytes=mib << 20),
        cost_estimate=pl.CostEstimate(flops=us * SCALE, bytes_accessed=1 << 10, transcendentals=0),
    )(*args)


def shape(dims, kind):
    return jax.ShapeDtypeStruct(dims, kind)


def project_kernel(T, fast, ids, *refs):
    half, f = ids[1], ids[2]
    ws, os = refs[0:4], refs[4:8]
    xs = [refs[8].at[k] for k in range(4)]
    if fast:
        xs += [refs[9].at[k] for k in range(4)]
    normed, kv, query, marks, gains, table, W, small = refs[-8:]
    rows = W.shape[2]
    for k in range(4):
        z = f ^ k
        W[z, half] = ws[k][:rows, :]
        W[z, 1 - half] = os[k][:rows, :]
        small[z] = ws[k][rows:, :].astype(f32)
    gain = jnp.concatenate([small[z, 0:1, 0 : D // 4] for z in range(4)], axis=1)
    gains[0:1, :] = gain
    gains[1:2, :] = jnp.concatenate([small[z, 1:2, 0 : D // 4] for z in range(4)], axis=1)
    table[...] = jnp.concatenate([small[z, 8:16, 0:128] for z in range(4)], axis=0)
    weight = W[...].reshape(D, 3 * CG)
    count = len(xs)
    seg = [xs[k][T:, :].astype(f32)[0:1, :128] for k in range(count)]
    marks[...] = jnp.concatenate(seg + [jnp.zeros((8 - count, 128), f32)] * (count < 8), axis=0)
    for i in range(count // 2):
        parts = []
        for k in (2 * i, 2 * i + 1):
            x = xs[k][:T, :].astype(f32)
            s = lax.rsqrt(jnp.mean(x * x, axis=-1, keepdims=True) + epsilon)
            parts.append((x * s * gain).astype(bf16))
        n = jnp.concatenate(parts, axis=0)
        at = slice(2 * i * T, (2 * i + 2) * T)
        normed[at, :] = n
        out = mm(n, weight if i < 2 else weight[:, : 2 * CG])
        for h in range(HG):
            kv[h, at, :] = out[:, 128 * h : 128 * h + 128].astype(bf16)
        if i < 2:
            blank = jnp.zeros((2 * T, DH), f32)
            for h in range(HG):
                q = out[:, 2 * CG + DH * h : 2 * CG + DH * (h + 1)]
                query[h, at, :] = jnp.concatenate([q, blank], axis=1).astype(bf16)


def tiles_kernel(T, ids, table, tiles):
    g = ids[0]
    lane = lax.broadcasted_iota(jnp.int32, (32, 128), 1)
    m = lax.broadcasted_iota(jnp.int32, (32, 2 * T), 1)
    label = lax.broadcasted_iota(jnp.int32, (32, 2 * T), 0)
    for h in range(HG):
        column = jnp.sum(jnp.where(lane == HG * g + h, table[...], 0.0), axis=1, keepdims=True)
        for d in range(5):
            if d in (0, 4):
                one = column[15 if d == 0 else 31 :][:1, :]
                tiles[h, d] = jnp.broadcast_to(one, (T, T))
                continue
            offset = T * (d - 2) - jnp.where(m < T, m, m - 2 * T)
            hot = jnp.where(bucket_of(offset) == label, column, 0.0)
            along = jnp.sum(hot, axis=0, keepdims=True)
            wide = jnp.broadcast_to(along, (T, 2 * T))
            tiles[h, d] = pltpu.roll(wide, 0, 1, stride=1, stride_axis=0)[:, :T]


def tile_of(key_at, query_at):
    return jnp.clip(key_at - query_at, -2, 2) + 2


def mark_columns(T, count, marks, columns):
    across = jnp.concatenate([marks[...], jnp.zeros((128 - marks.shape[0], 128), f32)], axis=0).T
    for t in range(count):
        columns[t] = jnp.broadcast_to(across[:, t : t + 1], (T, 128))


def masked_scores(T, scores, base, pair, h, q_at, k_at, seg_q, columns, tiles):
    pieces = []
    for t in range(8):
        kt = base + t
        bias = jnp.concatenate([tiles[h, tile_of(k_at[kt], q_at[2 * pair + j])] for j in range(2)], axis=1)
        column = jnp.concatenate([columns[kt], columns[kt]], axis=1)
        piece = scores[t * T : (t + 1) * T] + bias
        pieces.append(jnp.where(column == seg_q, piece, neg_fill))
    return jnp.concatenate(pieces, axis=0)


def pick_keys(blocks, i, h):
    if len(blocks[0].shape) == 3:
        return blocks[0][h]
    return jnp.concatenate([blocks[0][2 * i, h], blocks[0][2 * i + 1, h]], axis=0)


def forward_kernel(T, nb, fast, ids, q_at, k_at, query, seg_q, seg_k, tiles, *rest):
    blocks, (context, lse, columns) = rest[:-3], rest[-3:]
    mark_columns(T, nb * 4, seg_k, columns)

    def pair_step(pair, carry):
        at = pl.ds(pl.multiple_of(pair * 2 * T, 2 * T), 2 * T)
        seg = jnp.concatenate([seg_q[pl.ds(2 * pair + j, 1), :] for j in range(2)], axis=1)
        out = []
        for h in range(HG):
            q = query[h, at, :]

            def chunk(i, state):
                peak, total, acc = state
                keys = pick_keys(blocks, i, h)
                s = masked_scores(T, mm(keys, q, NT), 8 * i, pair, h, q_at, k_at, seg, columns, tiles)
                top = jnp.maximum(peak, jnp.max(s, axis=0, keepdims=True))
                p = jnp.exp(s - top)
                fade = jnp.exp(peak - top)
                total = total * fade + jnp.sum(p, axis=0, keepdims=True)
                acc = acc * fade + mm(keys, p.astype(bf16), TN)
                return top, total, acc

            start = (
                jnp.full((1, 2 * T), neg_fill, f32),
                jnp.zeros((1, 2 * T), f32),
                jnp.zeros((128, 2 * T), f32),
            )
            if fast:
                peak, total, acc = chunk(0, start)
            else:
                peak, total, acc = lax.fori_loop(0, nb // 2, chunk, start)
            out.append(acc[DH:, :] / total)
            lse[pair, h : h + 1, :] = peak + jnp.log(total)
        joined = jnp.concatenate(out, axis=0)
        context[at, :] = joined.T.astype(bf16)
        return carry

    lax.fori_loop(0, 2, pair_step, 0)


def backward_kernel(T, nb, fast, ids, q_at, k_at, query, seg_q, seg_k, tiles, lse, g0, g1, g2, g3, *rest):
    nin = 1
    blocks = rest[:nin]
    if fast:
        dquery, down, doth, sums, columns, dkv = rest[nin:]
    else:
        dquery, dkv, sums, columns = rest[nin:]
    mark_columns(T, nb * 4, seg_k, columns)
    sums[...] = jnp.zeros_like(sums)
    dkv[...] = jnp.zeros_like(dkv)

    def pair_step(pair, carry):
        at = pl.ds(pl.multiple_of(pair * 2 * T, 2 * T), 2 * T)
        seg = jnp.concatenate([seg_q[pl.ds(2 * pair + j, 1), :] for j in range(2)], axis=1)
        grad = g0[at, :].astype(f32) + g1[at, :].astype(f32) + g2[at, :].astype(f32) + g3[at, :].astype(f32)
        blank = jnp.zeros((2 * T, DH), f32)
        out = []
        for h in range(HG):
            q = query[h, at, :]
            do = jnp.concatenate([blank, grad[:, DH * h : DH * (h + 1)]], axis=1).astype(bf16)
            row = lse[pair, h : h + 1, :]

            def probs_of(i):
                keys = pick_keys(blocks, i, h)
                s = masked_scores(T, mm(keys, q, NT), 8 * i, pair, h, q_at, k_at, seg, columns, tiles)
                return keys, jnp.exp(s - row), mm(keys, do, NT)

            def finish(i, keys, p, dp, delta):
                ds = p * (dp - delta)
                for t in range(8):
                    for j in range(2):
                        index = tile_of(k_at[8 * i + t], q_at[2 * pair + j])
                        sums[h, index] += ds[t * T : (t + 1) * T, j * T : (j + 1) * T]
                ds = ds.astype(bf16)
                both = jnp.concatenate([ds, p.astype(bf16)], axis=1)
                piece = mm(both, jnp.concatenate([q, do], axis=0))
                if fast:
                    dkv[h] += piece
                else:
                    dkv[2 * i, h] += piece[: 4 * T]
                    dkv[2 * i + 1, h] += piece[4 * T :]
                return mm(keys, ds, TN)[:DH, :]

            if fast:
                keys, p, dp = probs_of(0)
                delta = jnp.sum(p * dp, axis=0, keepdims=True)
                dq = finish(0, keys, p, dp, delta)
            else:

                def first(i, delta):
                    keys, p, dp = probs_of(i)
                    return delta + jnp.sum(p * dp, axis=0, keepdims=True)

                delta = lax.fori_loop(0, nb // 2, first, jnp.zeros((1, 2 * T), f32))

                def second(i, dq):
                    keys, p, dp = probs_of(i)
                    return dq + finish(i, keys, p, dp, delta)

                dq = lax.fori_loop(0, nb // 2, second, jnp.zeros((DH, 2 * T), f32))
            out.append(dq)
        dquery[at, :] = jnp.concatenate(out, axis=0).T.astype(bf16)
        return carry

    lax.fori_loop(0, 2, pair_step, 0)
    if fast:
        for h in range(HG):
            down[h] = dkv[h, : 4 * T, :].astype(bf16)
            doth[h] = dkv[h, 4 * T :, :].astype(bf16)


def exact_mm(value, chosen):
    high = value.astype(bf16)
    low = (value - high.astype(f32)).astype(bf16)
    return mm(high, chosen) + mm(low, chosen)


def table_kernel(T, ids, sums, out):
    g = ids[0]
    row = lax.broadcasted_iota(jnp.int32, (T, T), 0)
    lane = lax.broadcasted_iota(jnp.int32, (T, T), 1)
    mirror = (row + lane == T - 1).astype(bf16)
    blank = jnp.zeros((T, T), f32)
    offset = lax.broadcasted_iota(jnp.int32, (2 * T, 128), 0) - (T - 1)
    label = lax.broadcasted_iota(jnp.int32, (2 * T, 128), 1)
    label8 = lax.broadcasted_iota(jnp.int32, (8, 128), 1)
    total = jnp.zeros((8, 128), f32)
    for d in range(5):
        lines = []
        for h in range(HG):
            if d in (0, 4):
                lines.append(jnp.sum(sums[h, d], axis=0, keepdims=True))
            else:
                moved = jnp.concatenate([exact_mm(sums[h, d], mirror), blank], axis=1)
                moved = pltpu.roll(moved, 0, 1, stride=1, stride_axis=0)
                lines.append(jnp.sum(moved, axis=0, keepdims=True))
        block = jnp.concatenate(lines + [jnp.zeros((8 - HG, lines[0].shape[1]), f32)], axis=0)
        if d in (0, 4):
            whole = jnp.sum(block, axis=1, keepdims=True)
            total = total + jnp.where(label8 == (15 if d == 0 else 31), whole, 0.0)
        else:
            total = total + exact_mm(block, (bucket_of(offset + T * (d - 2)) == label).astype(bf16))
    pieces = []
    for a in range(GROUPS):
        for h in range(HG):
            pieces.append(jnp.where(g == a, total[h : h + 1, :32], 0.0))
    out[...] = jnp.concatenate(pieces, axis=1)


def middle_kernel(T, ids, *refs):
    g, half, f = ids[0], ids[1], ids[2]
    x, ctx, gains = refs[0:3]
    cots, ws, others = refs[3:7], refs[7:11], refs[11:15]
    res0, sends, gcs = refs[15], refs[16:19], refs[19:23]
    grads, normed, active, ginner, branch, cot_all, gain_grad = refs[23:30]
    WO, W1, W2, held = refs[30:34]
    rows, low = WO.shape[2], WO.shape[2] // 2
    FH = W1.shape[3]
    for k in range(4):
        z = f ^ k
        cot_all[g ^ k] = cots[k][...]
        for at, pieces in ((half, ws), (1 - half, others)):
            piece = pieces[k]
            WO[z, at] = piece[:rows]
            W1[at, z] = piece[rows : 2 * rows]
            W2[at, z, :, 0 : D // 2] = piece[2 * rows : 2 * rows + low]
            W2[at, z, :, D // 2 :] = piece[2 * rows + low :]
    gain = gains[1:2, :]
    gain_grad[...] = jnp.zeros_like(gain_grad)

    def out_rows(a):
        return jnp.concatenate([WO[a, 0], WO[a, 1]], axis=1)

    for i in range(2):
        at = slice(2 * i * T, (2 * i + 2) * T)
        slots = (2 * i, 2 * i + 1)
        att = jnp.concatenate([x[m, :T, :] for m in slots], axis=0).astype(f32)
        cot = jnp.concatenate([cot_all[m] for m in slots], axis=0)
        for a in range(4):
            att = att + mm(ctx[a, at, :], out_rows(a))
        s = lax.rsqrt(jnp.mean(att * att, axis=-1, keepdims=True) + epsilon)
        n = (att * s * gain).astype(bf16)
        normed[at, :] = n
        result = None
        gn = None
        for c in range(2):
            columns = slice(c * FH, (c + 1) * FH)
            w1 = W1[c].reshape(D, FH)
            w2 = W2[c].reshape(FH, D)
            inner = mm(n, w1)
            cdf = 0.5 * (1.0 + lax.erf(inner * root_half))
            act = (inner * cdf).astype(bf16)
            slope = cdf + inner * jnp.exp(-0.5 * inner * inner) * inv_root_tau
            part = mm(act, w2)
            result = part if result is None else result + part
            ga = mm(cot, w2, NT).astype(bf16)
            gi = (ga.astype(f32) * slope).astype(bf16)
            part = mm(gi, w1, NT)
            gn = part if gn is None else gn + part
            active[at, columns] = act
            ginner[at, columns] = gi
        for index, m in enumerate(slots):
            held[m] = result[index * T : (index + 1) * T]

            @pl.when(g == m)
            def _():
                held[m] += att[index * T : (index + 1) * T]

        u = gn * gain
        gain_grad[...] += jnp.sum(gn * att * s, axis=0, keepdims=True)
        grad = 0.25 * cot.astype(f32) + s * u - att * (s * s * s) * jnp.mean(u * att, axis=-1, keepdims=True)
        grads[at, :] = grad
        gb = grad.astype(bf16)
        branch[at, :] = gb
        for k in range(4):
            gcs[k][at, :] = mm(gb, out_rows(g ^ k), NT).astype(bf16)
    res0[...] = held[g]
    for k in (1, 2, 3):
        sends[k - 1][...] = held[g ^ k].astype(bf16)


def weight_kernel(T, ids, normed, active, ginner, branch, cot, ctx, keep, send, gi, go, gw):
    c = ids[3]
    R = D // 8
    gi[...] = mm(normed[...], ginner[...], TN).reshape(4, 2, R, D)
    go[...] = mm(active[...], cot[...].reshape(4 * T, D), TN).reshape(2, 4, R, D)
    gb = branch[...]
    for a in range(4):
        gw[a] = mm(ctx[a], gb, TN).reshape(2, R, D)
    for a in range(4):
        keep[0, a] = gi[a, c]
        keep[1, a] = go[c, a]
        keep[2, a] = gw[a, c]
        send[0, a] = gi[a, 1 - c].astype(bf16)
        send[1, a] = go[1 - c, a].astype(bf16)
        send[2, a] = gw[a, 1 - c].astype(bf16)


def tail_kernel(T, ids, x_all, dq, down, doth, grads, gains, *refs):
    g, half, f = ids[0], ids[1], ids[2]
    ws, os, rs = refs[0:4], refs[4:8], refs[8:11]
    own, s1, s2, s3, joined, gain_grad, W, held = refs[11:]
    rows = W.shape[2]
    sends = (s1, s2, s3)
    for k in range(4):
        z = f ^ k
        W[z, half] = ws[k][:rows, :]
        W[z, 1 - half] = os[k][:rows, :]
    weight = W[...].reshape(D, 3 * CG)
    gain = gains[0:1, :]
    gain_grad[...] = jnp.zeros_like(gain_grad)
    for i in range(2):
        at = slice(2 * i * T, (2 * i + 2) * T)
        parts = [(down[h, at, :].astype(f32) + doth[h, at, :].astype(f32)).astype(bf16) for h in range(HG)]
        dqkv = jnp.concatenate(parts + [dq[at, :]], axis=1)
        joined[at, :] = dqkv
        gn = mm(dqkv, weight, NT)
        x = jnp.concatenate([x_all[m, :T, :] for m in (2 * i, 2 * i + 1)], axis=0).astype(f32)
        s = lax.rsqrt(jnp.mean(x * x, axis=-1, keepdims=True) + epsilon)
        u = gn * gain
        gain_grad[...] += jnp.sum(gn * x * s, axis=0, keepdims=True)
        total = grads[at, :] + s * u - x * (s * s * s) * jnp.mean(u * x, axis=-1, keepdims=True)
        for index, m in enumerate((2 * i, 2 * i + 1)):
            held[m] = total[index * T : (index + 1) * T]
    own[...] = held[g]
    for k in (1, 2, 3):
        sends[k - 1][:T, :] = held[g ^ k].astype(bf16)
        sends[k - 1][T:, :] = rs[k - 1][...]


def split_rows(value):
    high = value.astype(bf16)
    return jnp.concatenate([high, (value - high.astype(f32)).astype(bf16)], axis=0)


def project_grad_kernel(T, ids, normed, dq, down, doth, keep, send, gw):
    c = ids[3]
    R = D // 8
    own = jnp.concatenate([down[h] for h in range(HG)], axis=1)
    other = jnp.concatenate([doth[h] for h in range(HG)], axis=1)
    pairs = mm(normed[...], jnp.concatenate([own, other], axis=0), TN)
    single = mm(normed[: 4 * T, :], dq[...], TN)
    gw[...] = jnp.concatenate([pairs, single], axis=1).reshape(4, 2, R, 3 * CG)
    for a in range(4):
        keep[a] = gw[a, c]
        send[a * R : (a + 1) * R, :] = gw[a, 1 - c].astype(bf16)


def extra_kernel(second, first, table, block, send):
    wide = jnp.zeros((1, 3 * CG - D // 2), f32)
    vectors = [second[:, : D // 2], second[:, D // 2 :], first[:, : D // 2], first[:, D // 2 :], table[...]]
    rows = jnp.concatenate([jnp.concatenate([v, wide], axis=1) for v in vectors], axis=0)
    rows = jnp.concatenate([rows, jnp.zeros((3, 3 * CG), f32)], axis=0)
    block[...] = rows
    send[...] = split_rows(rows)


def start_kernel(T, C, ids, q, k, v, first, second, table, x, seg, out, x_out, small, held, gain1, gain2, rows8, marks, sems):
    place = lax.axis_index("seq")
    g = lax.div(place, C)
    side = lax.rem(place, C) if ids is None else ids[1]
    rows = out.shape[0] - 16
    at = pl.ds(pl.multiple_of(side * rows, rows), rows)
    lanes = pl.ds(pl.multiple_of(128 * (g + lax.div(g, 2)), 128), 256)
    pairs = [(w.at[at, lanes], held.at[n]) for n, w in enumerate((q, k, v))]
    pairs += [(first, gain1), (second, gain2), (table, rows8), (seg, marks), (x.at[0], x_out.at[:T])]
    copies = [pltpu.make_async_copy(a, b, sems.at[n]) for n, (a, b) in enumerate(pairs)]
    for copy in copies:
        copy.start()
    small[...] = jnp.zeros_like(small)
    for copy in copies:
        copy.wait()
    mark = jnp.concatenate([marks[...].astype(f32), jnp.zeros((15, T), f32)], axis=0)
    x_out[T:, :] = jnp.concatenate([mark, jnp.zeros((16, D - T), f32)], axis=1).astype(bf16)
    small[0:1, 0 : D // 4] = gain1[...].reshape(1, D // 4).astype(f32)
    small[1:2, 0 : D // 4] = gain2[...].reshape(1, D // 4).astype(f32)
    small[8:16, 0:H] = rows8[...].astype(f32)
    out[rows:, :] = small[...].astype(bf16)
    for odd in range(2):

        @pl.when(lax.rem(g, 2) == odd)
        def _():
            pieces = []
            for h in range(HG):
                here = slice(DH * (odd + h), DH * (odd + h + 1))
                pieces += [held[1, :, here], held[2, :, here]]
            pieces.append(held[0, :, DH * odd : DH * odd + CG])
            out[:rows, :] = jnp.concatenate(pieces, axis=1)


def middle_pack_kernel(ids, wo, inner, outer, out, held, block, sems):
    g, side, f = ids[0], ids[1], ids[2]
    R0, F0 = wo.shape[0], outer.shape[0]
    FB, low = F0 // 8, R0 // 2
    half = F0 // 2
    pairs = [
        (wo.at[:, pl.ds(pl.multiple_of(side * half, 128), half)], out.at[:R0]),
        (outer.at[pl.ds(pl.multiple_of(side * half + FB * (f ^ g), FB), FB)], block),
    ]
    for z in range(4):
        base = (2 * z + side) * half + 128 * lax.div(z ^ g, 2)
        pairs.append((inner.at[:, pl.ds(pl.multiple_of(base, 128), 256)], held.at[z]))
    copies = [pltpu.make_async_copy(a, b, sems.at[n]) for n, (a, b) in enumerate(pairs)]
    for copy in copies:
        copy.start()
    for copy in copies:
        copy.wait()
    for a in range(GROUPS):

        @pl.when(g == a)
        def _():
            starts = [FB * (z ^ a) - 128 * ((z ^ a) // 2) for z in range(4)]
            picked = jnp.concatenate([held[z, :, n : n + FB] for z, n in enumerate(starts)], axis=1)
            out[R0 : 2 * R0, :] = picked

    out[2 * R0 : 2 * R0 + low, :] = block[:, : D // 2]
    out[2 * R0 + low :, :] = block[:, D // 2 :]


def added(refs):
    value = refs[0][...].astype(f32)
    for r in refs[1:]:
        value = value + r[...].astype(f32)
    return value


def join_kernel(ids, keep, more, far, near, p1, p2, p3, wown, total):
    g, f = ids[0], ids[2]
    R = D // 8
    total[...] = (keep[0] + more[0].astype(f32)).reshape(4, 4, R // 4, D)

    def toward(at):
        right = keep[1, at ^ g] + more[1, at ^ g].astype(f32)
        return [total[a, at] for a in range(4)] + [right]

    far[...] = jnp.concatenate(toward(f ^ 1) + toward(f ^ 3), axis=0).astype(bf16)
    near[...] = jnp.concatenate(toward(f) + toward(f ^ 2), axis=0)
    for k, out in enumerate((wown, p1, p2, p3)):
        out[...] = (keep[2, g ^ k] + more[2, g ^ k].astype(f32)).astype(out.dtype)


def middle_half_kernel(near, more, send, mine):
    value = near[...] + more[...].astype(f32)
    count = mine.shape[0]
    mine[...] = value[:count]
    send[:count, :] = value[count:].astype(bf16)
    send[count:, :] = jnp.zeros((send.shape[0] - count, send.shape[1]), bf16)


def middle_sum_kernel(own, more, inner, outer):
    R = D // 8
    value = own[...] + more[: 2 * R, :].astype(f32)
    inner[...] = value[:R]
    outer[...] = value[R:].astype(bf16)


def unsplit(block):
    return block[:8] + block[8:]


def narrow(block):
    wide = 3 * CG
    right = block[:, wide:]
    rows = block.shape[0] // 3
    folded = jnp.concatenate([right[n * rows : (n + 1) * rows] for n in range(3)], axis=1)
    return jnp.concatenate([block[:, :wide], folded], axis=0)


def widen(block):
    rows = D // 32
    folded = block[rows:]
    wide = D - 3 * CG
    right = jnp.concatenate([folded[:, n * wide : (n + 1) * wide] for n in range(3)], axis=0)
    return jnp.concatenate([block[:rows], right], axis=1)


def project_join_kernel(ids, keep, more, extra, extra_more, wown, p1, p2, p3, far, near, extra_out, total, out_total):
    f = ids[2]
    R = D // 8
    total[...] = (keep[...] + more[...].astype(f32).reshape(4, R, 3 * CG)).reshape(4, 4, R // 4, 3 * CG)
    out_total[...] = added((wown, p1, p2, p3)).reshape(4, R // 4, D)
    ex = extra[...] + unsplit(extra_more[...].astype(f32))
    extra_out[...] = ex

    def toward(at):
        return [total[a, at] for a in range(4)]

    far[: 2 * R, :] = jnp.concatenate(toward(f ^ 1) + toward(f ^ 3), axis=0).astype(bf16)
    data = jnp.concatenate([narrow(out_total[f ^ 1]), narrow(out_total[f ^ 3])], axis=0).astype(bf16)
    far[2 * R : 2 * R + data.shape[0], :] = data
    far[2 * R + data.shape[0] :, :] = split_rows(ex)
    kept = [toward(at) + [narrow(out_total[at])] for at in (f, f ^ 2)]
    near[...] = jnp.concatenate(kept[0] + kept[1], axis=0)


def project_half_kernel(near, more, extra, send, mine, extra_out):
    R = D // 8
    got, tail = more[: 2 * R, :].astype(f32), more[2 * R :, :].astype(f32)
    count = mine.shape[0]
    low = count - R
    ex = extra[...] + unsplit(tail[2 * low :])
    extra_out[...] = ex
    mine[:R, :] = near[:R, :] + got[:R]
    mine[R:, :] = near[R:count, :] + tail[:low]
    send[:R, :] = (near[count : count + R, :] + got[R:]).astype(bf16)
    send[R:count, :] = (near[count + R :, :] + tail[low : 2 * low]).astype(bf16)
    send[count:, :] = split_rows(ex)


def project_plane_kernel(ids, own, more, extra, inner, s1, s2, s3, mine, extra_out, output, total, held):
    g = ids[0]
    R = D // 8
    RR = R // 4
    got = more[...].astype(f32)
    value = own[...] + got[: own.shape[0]]
    ex = extra[...] + unsplit(got[own.shape[0] :])
    extra_out[...] = ex
    output[...] = widen(value[R:])
    total[...] = value[:R].reshape(4, RR, 3 * CG)
    held[...] = inner[...].reshape(4, RR, D)
    high = ex.astype(bf16).astype(f32)
    low = ex - high
    tail = jnp.concatenate([high[:, : D // 2], low[:, : D // 2], jnp.zeros((8, 3 * CG), f32)], axis=1)
    for k, out in enumerate((mine, s1, s2, s3)):
        block = jnp.concatenate([total[g ^ k], held[g ^ k]], axis=1)
        out[...] = block if k == 0 else jnp.concatenate([block, tail], axis=0).astype(bf16)


def final_kernel(where, own, r1, r2, r3, extra, outer_in, query, key, value, inner, first, second, table, outer, slots, rows):
    g, at = where[0], where[1]
    RR = D // 32
    ex = extra[...][:, : D // 2]
    slots[g] = own[...]
    for k, r in ((1, r1), (2, r2), (3, r3)):
        got = r[...].astype(f32)
        slots[g ^ k] = got[:RR]
        ex = ex + got[RR:, : D // 2] + got[RR:, D // 2 : D]
    query[...] = jnp.concatenate([slots[a, :, 2 * CG : 3 * CG] for a in range(4)], axis=1)
    for part, out in enumerate((key, value)):
        starts = [128 * h + DH * part for h in range(HG)]
        out[...] = jnp.concatenate([slots[a, :, n : n + DH] for a in range(4) for n in starts], axis=1)
    base = 3 * CG
    for z in range(4):
        for e in range(2):
            n = base + (4 * e + z) * 4 * RR
            inner[:, (8 * z + 4 * e) * 4 * RR : (8 * z + 4 * e + 4) * 4 * RR] = jnp.concatenate(
                [slots[z ^ b, :, n : n + 4 * RR] for b in range(4)], axis=1
            )
    own_gain = first.shape[1]
    for r, out in ((0, second), (2, first)):
        whole = jnp.concatenate([ex[r : r + 1], ex[r + 1 : r + 2]], axis=1)
        count = D // own_gain
        rows[...] = jnp.concatenate([whole[:, own_gain * n : own_gain * (n + 1)] for n in range(count)], axis=0)
        out[...] = rows[pl.ds(at, 1), :]
    table[...] = jnp.concatenate([ex[4:5, 32 * h : 32 * (h + 1)] for h in range(H)], axis=0)
    outer[...] = outer_in[...].astype(f32)


def on_device(seqs, fsdps, *args):
    (
        activations,
        segments,
        cotangent,
        attention_gain,
        query_weight,
        key_weight,
        value_weight,
        output_weight,
        bias_table,
        feedforward_gain,
        inner_weight,
        outer_weight,
    ) = args
    T = activations.shape[1]
    C = seqs // GROUPS
    fast = C == 2 and not FORCE_GENERIC
    position = lax.axis_index("seq")
    f = lax.axis_index("fsdp")
    g, c = position // C, position % C
    half = c if fast else 0
    ids = jnp.stack([g, half, f, c]).astype(jnp.int32)
    R0 = query_weight.shape[0]
    RH = R0 // 2
    F0 = outer_weight.shape[0]

    def group_move(value, k):
        pairs = [(a * C + b, (a ^ k) * C + b) for a in range(GROUPS) for b in range(C)]
        return lax.ppermute(value, "seq", pairs)

    def plane_move(value, k):
        return lax.ppermute(value, "fsdp", [(i, i ^ k) for i in range(fsdps)])

    def core_move(value):
        return lax.ppermute(value, "seq", [(i, i ^ 1) for i in range(seqs)])

    def from_group(value):
        return [value] + [group_move(value, k) for k in (1, 2, 3)]

    def from_planes(value):
        return [value] + [plane_move(value, k) for k in (1, 2, 3)]

    def ids_for(side):
        return jnp.stack([g, jnp.asarray(side, jnp.int32), f, c]).astype(jnp.int32)

    def start(side):
        own = fast and side is half
        kernel = functools.partial(start_kernel, T, C)
        return call(
            functools.partial(kernel, None) if own else kernel,
            (shape((RH + 16, 3 * CG), bf16), shape((T + 16, D), bf16)),
            ([] if own else [ids_for(side)])
            + [
                query_weight,
                key_weight,
                value_weight,
                attention_gain,
                feedforward_gain,
                bias_table,
                activations,
                segments,
            ],
            scratch=[
                pltpu.VMEM((16, 3 * CG), f32),
                pltpu.VMEM((3, RH, 256), bf16),
                pltpu.VMEM((R0,), bf16),
                pltpu.VMEM((R0,), bf16),
                pltpu.VMEM(bias_table.shape, bf16),
                pltpu.VMEM((1, T), jnp.int32),
                pltpu.SemaphoreType.DMA((8,)),
            ],
            us=1,
            mib=60,
            scalars=0 if own else 1,
            far=range(9),
        )

    def middle_pack(side):
        return call(
            middle_pack_kernel,
            shape((3 * R0, D // 2), bf16),
            [ids_for(side), output_weight, inner_weight, outer_weight],
            scratch=[
                pltpu.VMEM((4, R0, 256), bf16),
                pltpu.VMEM((F0 // 8, D), bf16),
                pltpu.SemaphoreType.DMA((6,)),
            ],
            us=1,
            mib=60,
            far=(1, 2, 3),
        )

    def after(values, *earlier):
        return lax.optimization_barrier((values, earlier))[0]

    def ring(value):
        return lax.ppermute(value, "fsdp", [(i, (i + 1) % fsdps) for i in range(fsdps)])

    token_groups = [[a * C + b for a in range(GROUPS)] for b in range(C)]

    def gather(value):
        return lax.all_gather(value, "seq", axis=0, axis_index_groups=token_groups)

    w_pack, x_pack = start(half)
    m_pack = middle_pack(half)
    ws = from_planes(w_pack)
    ms = from_planes(m_pack)
    x_all = gather(after(x_pack, m_pack))
    cots = from_group(after(cotangent[0], x_all))
    if fast:
        xo = [core_move(after(x_all, *ws))]
        wo = [core_move(w) for w in ws]
    else:
        xo = []
        wo = from_planes(start(1)[0])

    wide_t = (8 if fast else 4) * T
    normed, kv, query, marks, gains, table = call(
        functools.partial(project_kernel, T, fast),
        (
            shape((wide_t, D), bf16),
            shape((HG, wide_t, 128), bf16),
            shape((HG, 4 * T, 128), bf16),
            shape((8, 128), f32),
            shape((8, D), f32),
            shape((32, 128), f32),
        ),
        [ids] + ws + wo + [x_all] + xo,
        scratch=[pltpu.VMEM((4, 2, RH, 3 * CG), bf16), pltpu.VMEM((4, 16, 3 * CG), f32)],
        us=1,
    )
    tiles = call(functools.partial(tiles_kernel, T), shape((HG, 5, T, T), f32), [ids, table], us=1)

    slot = jnp.arange(4, dtype=jnp.int32)
    q_at = slot * C + c
    seg_q = marks
    blocks = [kv]
    if fast:
        seg_k = marks
        k_at = jnp.concatenate([slot * C + c, slot * C + 1 - c])
    else:
        members = [[a * C + b for b in range(C)] for a in range(GROUPS)]
        blocks = [lax.all_gather(kv, "seq", axis=0, axis_index_groups=members)]
        seg_k = lax.all_gather(marks[:4].astype(bf16), "seq", axis=0, axis_index_groups=members)
        seg_k = seg_k.reshape(C * 4, T).astype(f32)
        k_at = (slot[None, :] * C + jnp.arange(C, dtype=jnp.int32)[:, None]).reshape(C * 4)
    context, lse = call(
        functools.partial(forward_kernel, T, C, fast),
        (shape((4 * T, CG), bf16), shape((2, 8, 2 * T), f32)),
        [ids, q_at, k_at, query, seg_q, seg_k, tiles] + blocks,
        scalars=3,
        scratch=[pltpu.VMEM((C * 4, T, 128), f32)],
        mib=16 if fast else 48,
        us=1,
    )
    ctx_all = gather(context)
    cots, ms = after((tuple(cots), tuple(ms)), ctx_all)
    if fast:
        mo = [core_move(m) for m in ms]
    else:
        mo = from_planes(middle_pack(1))

    FH = F0 // 2
    outs = call(
        functools.partial(middle_kernel, T),
        (shape((T, D), f32),)
        + (shape((T, D), bf16),) * 3
        + (shape((4 * T, CG), bf16),) * 4
        + (shape((4 * T, D), f32),)
        + (shape((4 * T, D), bf16),) * 4
        + (shape((4, T, D), bf16), shape((1, D), f32)),
        [ids, x_all, ctx_all, gains] + list(cots) + list(ms) + mo,
        scratch=[
            pltpu.VMEM((4, 2, R0, D // 2), bf16),
            pltpu.VMEM((2, 4, R0, FH), bf16),
            pltpu.VMEM((2, 4, F0 // 8, D), bf16),
            pltpu.VMEM((4, T, D), f32),
        ],
        mib=24,
        us=10,
    )
    res0, res_send, gcs = outs[0], outs[1:4], outs[4:8]
    grads, normed_ffn, active, ginner, branch, cot_all, second_gain = outs[8:15]
    got = [gcs[0]] + [group_move(gcs[k], k) for k in (1, 2, 3)]
    R = D // 8
    keep, send = call(
        functools.partial(weight_kernel, T),
        (shape((3, 4, R, D), f32), shape((3, 4, R, D), bf16)),
        [ids, normed_ffn, active, ginner, branch, cot_all, ctx_all],
        scratch=[
            pltpu.VMEM((4, 2, R, D), f32),
            pltpu.VMEM((2, 4, R, D), f32),
            pltpu.VMEM((4, 2, R, D), f32),
        ],
        mib=24,
        us=5,
    )

    RR = R // 4
    if fast:
        far, near, p1, p2, p3, wown = call(
            join_kernel,
            (shape((4 * R, D), bf16), shape((4 * R, D), f32)) + (shape((R, D), bf16),) * 3 + (shape((R, D), f32),),
            [ids, keep, core_move(send)],
            scratch=[pltpu.VMEM((4, 4, RR, D), f32)],
        )
        middle_more = plane_move(far, 1)
        got = list(after(tuple(got), far, p1))
        ps = [group_move(p, k) for k, p in ((1, p1), (2, p2), (3, p3))]
    if fast:
        back_outs = (
            shape((4 * T, CG), bf16),
            shape((HG, 4 * T, 128), bf16),
            shape((HG, 4 * T, 128), bf16),
            shape((HG, 5, T, T), f32),
        )
        back_scratch = [pltpu.VMEM((C * 4, T, 128), f32), pltpu.VMEM((HG, 8 * T, 128), f32)]
    else:
        back_outs = (
            shape((4 * T, CG), bf16),
            shape((C, HG, 4 * T, 128), f32),
            shape((HG, 5, T, T), f32),
        )
        back_scratch = [pltpu.VMEM((C * 4, T, 128), f32)]
    back = call(
        functools.partial(backward_kernel, T, C, fast),
        back_outs,
        [ids, q_at, k_at, query, seg_q, seg_k, tiles, lse] + got + blocks,
        scalars=3,
        scratch=back_scratch,
        mib=20 if fast else 56,
        us=30000,
    )
    if fast:
        dq, down, doth, sums = back
        doth = after(doth, *ps)
        middle_send, middle_mine = call(
            middle_half_kernel,
            (shape((2 * R + 16, D), bf16), shape((2 * R, D), f32)),
            [near, middle_more],
            scalars=0,
            us=1,
        )
        middle_last = plane_move(middle_send, 2)
        doth = after(doth, middle_send)
        dmore = core_move(doth)
        keep_p, send_p = call(
            functools.partial(project_grad_kernel, T),
            (shape((4, R, 3 * CG), f32), shape((4 * R, 3 * CG), bf16)),
            [ids, normed, dq, down, doth],
            scratch=[pltpu.VMEM((4, 2, R, 3 * CG), f32)],
        )
        RB = R + RR * D // (3 * CG)
        project_more = core_move(send_p)
    else:
        dq, dall, sums = back
        down = lax.psum_scatter(dall, "seq", scatter_dimension=0, axis_index_groups=members)
        down, dmore = down.astype(bf16), jnp.zeros((HG, 4 * T, 128), bf16)

    own, s1, s2, s3, joined, first_gain = call(
        functools.partial(tail_kernel, T),
        (shape((T, D), f32),)
        + (shape((2 * T, D), bf16),) * 3
        + (shape((4 * T, 3 * CG), bf16), shape((1, D), f32)),
        [ids, x_all, dq, down, dmore, grads, gains] + ws + wo + list(res_send),
        scratch=[pltpu.VMEM((4, 2, RH, 3 * CG), bf16), pltpu.VMEM((4, T, D), f32)],
    )
    table_row = call(functools.partial(table_kernel, T), shape((1, 32 * H), f32), [ids, sums])
    small = shape((8, 3 * CG), f32), shape((16, 3 * CG), bf16)
    extra, extra_send = call(extra_kernel, small, [second_gain, first_gain, table_row], scalars=0, us=1)
    if fast:
        RB = R + RR * D // (3 * CG)
        project_far, project_near, extra = call(
            project_join_kernel,
            (shape((2 * RB + 16, 3 * CG), bf16),)
            + (shape((2 * RB, 3 * CG), f32), shape((8, 3 * CG), f32)),
            [ids, keep_p, project_more, extra, core_move(extra_send), wown] + ps,
            scratch=[pltpu.VMEM((4, 4, RR, 3 * CG), f32), pltpu.VMEM((4, RR, D), f32)],
            us=1,
        )
        send, mine, extra = call(
            project_half_kernel,
            (shape((RB + 16, 3 * CG), bf16), shape((RB, 3 * CG), f32), shape((8, 3 * CG), f32)),
            [after(project_near, middle_last), plane_move(project_far, 1), extra],
            scalars=0,
            us=1,
        )
        more = plane_move(send, 2)
        s1, s2, s3 = after((s1, s2, s3), project_far)
    parts = [group_move(v, k) for k, v in ((1, s1), (2, s2), (3, s3))]
    input_gradient = own + parts[0][:T].astype(f32) + parts[1][:T].astype(f32) + parts[2][:T].astype(f32)
    result = res0 + parts[0][T:].astype(f32) + parts[1][T:].astype(f32) + parts[2][T:].astype(f32)
    if fast:
        inner_mine, outer_mine = call(
            middle_sum_kernel,
            (shape((R, D), f32), shape((R, D), bf16)),
            [middle_mine, middle_last],
            scalars=0,
            us=1,
        )
        pairs = []
        for a in range(GROUPS):
            for b in range(C):
                for z in range(fsdps):
                    pairs.append(((a * C + b) * fsdps + z, ((a ^ z) * C + b) * fsdps + z))
        outer_got = lax.ppermute(outer_mine, ("seq", "fsdp"), pairs)
        wide = 3 * CG + D
        t1, t2, t3, tmine, extra, output_grad = call(
            project_plane_kernel,
            (shape((RR + 8, wide), bf16),) * 3
            + (shape((RR, wide), f32), shape((8, 3 * CG), f32), shape((RR, D), f32)),
            [ids, mine, more, extra, inner_mine],
            scratch=[pltpu.VMEM((4, RR, 3 * CG), f32), pltpu.VMEM((4, RR, D), f32)],
            us=1,
        )
        ts = [group_move(t, k) for k, t in ((1, t1), (2, t2), (3, t3))]
        where = jnp.stack([g, position * fsdps + f]).astype(jnp.int32)
        count = D // (seqs * fsdps)
        query_grad, key_grad, value_grad, inner_grad, first_grad, second_grad, table_grad, outer_grad = call(
            final_kernel,
            (shape((RR, D), f32),) * 3
            + (shape((RR, 4 * F0), f32), shape((1, count), f32), shape((1, count), f32), shape((H, 32), f32))
            + (shape((R, D), f32),),
            [where, tmine] + ts + [extra, outer_got],
            scratch=[pltpu.VMEM((4, RR, wide), f32), pltpu.VMEM((D // count, count), f32)],
            us=1,
        )
        first_grad, second_grad = first_grad.reshape(count), second_grad.reshape(count)
        table_grad = table_grad.T
    else:
        FB = F0 // 8
        axes = ("seq", "fsdp")

        def product(left, right):
            return lax.optimization_barrier(mm(left, right, TN))

        def spread(whole, axis):
            blocks = []
            for z in range(4):
                for e in range(2):
                    block = lax.slice_in_dim(whole, (4 * e + z) * FB, (4 * e + z + 1) * FB, axis=axis)
                    blocks += [block * (b == (z ^ g)).astype(f32) for b in range(4)]
            return jnp.concatenate(blocks, axis=axis)

        inner_w = spread(product(normed_ffn, ginner), 1)
        outer_w = spread(product(active, cot_all.reshape(4 * T, D)), 0)
        out_w = jnp.zeros((4, CG, D), f32)
        for k in range(4):
            out_w = lax.dynamic_update_slice_in_dim(out_w, product(ctx_all[k], branch)[None], k, 0)
        joined_w = product(normed, joined)
        pairs_w = joined_w[:, : 2 * CG].reshape(D, HG, 2, DH)

        def whole(part):
            return lax.dynamic_update_slice(jnp.zeros((D, D), f32), part.reshape(D, CG), (0, g * CG))

        def scatter(part):
            return lax.psum_scatter(part, axes, scatter_dimension=0, tiled=True)

        query_grad = scatter(whole(joined_w[:, 2 * CG :]))
        key_grad = scatter(whole(pairs_w[:, :, 0]))
        value_grad = scatter(whole(pairs_w[:, :, 1]))
        output_grad = scatter(out_w.reshape(D, D))
        inner_grad = scatter(inner_w)
        outer_grad = scatter(outer_w)
        extra = lax.psum(extra, axes)
        at = position * fsdps + f
        count = D // (seqs * fsdps)
        second_vec = jnp.concatenate([extra[0, : D // 2], extra[1, : D // 2]])
        first_vec = jnp.concatenate([extra[2, : D // 2], extra[3, : D // 2]])
        second_grad = lax.dynamic_slice_in_dim(second_vec, at * count, count)
        first_grad = lax.dynamic_slice_in_dim(first_vec, at * count, count)
        table_grad = extra[4, : 32 * H].reshape(H, 32).T
    return (
        result[None],
        input_gradient[None],
        first_grad,
        query_grad,
        key_grad,
        value_grad,
        output_grad,
        table_grad,
        second_grad,
        inner_grad,
        outer_grad,
    )


def solution(mesh):
    return jax.shard_map(
        functools.partial(on_device, mesh.shape["seq"], mesh.shape["fsdp"]),
        mesh=mesh,
        in_specs=(
            P("fsdp", "seq", None),
            P("fsdp", "seq"),
            P("fsdp", "seq", None),
            P("fsdp"),
            P("fsdp", None),
            P("fsdp", None),
            P("fsdp", None),
            P("fsdp", None),
            P("fsdp", None),
            P("fsdp"),
            P("fsdp", None),
            P("fsdp", None),
        ),
        out_specs=(
            P("fsdp", "seq", None),
            P("fsdp", "seq", None),
            P(("seq", "fsdp")),
            P(("seq", "fsdp"), None),
            P(("seq", "fsdp"), None),
            P(("seq", "fsdp"), None),
            P(("seq", "fsdp"), None),
            P(),
            P(("seq", "fsdp")),
            P(("seq", "fsdp"), None),
            P(("seq", "fsdp"), None),
        ),
        check_vma=False,
    )
```

time: 244 us -> 158 us (0.65)
  waiting for transfers between devices: 109 us -> 46.8 us
  local copies, waits for them, and re-layouts: 31.8 us -> 0.02 us
  blocking collectives: 0 us -> 25.6 us
  starting transfers between devices: 50.2 us -> 37 us
  other arithmetic: 11.8 us -> 3.14 us
  Pallas kernels: 38.5 us -> 44 us
    ppermute x12 -> x10, waiting for transfers between devices: 68 us -> 27.4 us  [plane_move(): return lax.ppermute(value, 'fsdp', [(i, i ^ k) for i in range(fsdps)])]
    ppermute x24 -> x15, waiting for transfers between devices: 41.3 us -> 13.3 us  [group_move(): return lax.ppermute(value, 'seq', pairs)]
    all_gather x0 -> x2, blocking collectives: none -> 25.6 us  [gather(): return lax.all_gather(value, 'seq', axis=0, axis_index_groups=token_groups)]
    unnamed x66 -> x10, local copies, waits for them, and re-layouts: 17.8 us -> 0.02 us
    ppermute x24 -> x15, starting transfers between devices: 28.5 us -> 17.7 us  [group_move(): return lax.ppermute(value, 'seq', pairs)]
    ppermute x6 -> x13, waiting for transfers between devices: 0.02 us -> 6.08 us  [core_move(): return lax.ppermute(value, 'seq', [(i, i ^ 1) for i in range(seqs)])]
    pallas_call x9 -> x19, Pallas kernels: 38.5 us -> 44 us  [call(): pl.pallas_call(kernel, out_shape=outs, in_specs=[smem] * scalars + [hbm i...]
    dynamic_slice x9 -> x0, local copies, waits for them, and re-layouts: 5.39 us -> none  [the longest x3 2.96 us: part(): lax.dynamic_slice(weight, (side * RH, g * CG), (RH, CG)).reshape(RH, HG, DH)]
  transfers between devices with their start and end apart: 43 -> 39, of which waited for: 19 -> 18; matrix products, arithmetic and copies ran while one was open for 9% -> 2% of each run, Pallas kernels for 9% -> 17%
where the time goes in v2:
time: 158 us; the launch traced here: 157 us
  waiting for transfers between devices  46.8 us (30%)
  Pallas kernels  44 us (28%)
  starting transfers between devices  37 us (23%)
  blocking collectives  25.6 us (16%)
  other arithmetic  3.14 us (2%)
    pallas_call x19, Pallas kernels, call(): pl.pallas_call(kernel, out_shape=outs, in_specs=[smem] * scalars + [hbm i...  44 us
    ppermute x10, waiting for transfers between devices, plane_move(): return lax.ppermute(value, 'fsdp', [(i, i ^ k) for i in range(fsdps)])  27.4 us
    all_gather x2, blocking collectives, gather(): return lax.all_gather(value, 'seq', axis=0, axis_index_groups=token_groups)  25.6 us
    ppermute x15, starting transfers between devices, group_move(): return lax.ppermute(value, 'seq', pairs)  17.7 us
    ppermute x10, starting transfers between devices, plane_move(): return lax.ppermute(value, 'fsdp', [(i, i ^ k) for i in range(fsdps)])  15.9 us
    ppermute x15, waiting for transfers between devices, group_move(): return lax.ppermute(value, 'seq', pairs)  13.3 us
    ppermute x13, waiting for transfers between devices, core_move(): return lax.ppermute(value, 'seq', [(i, i ^ 1) for i in range(seqs)])  6.08 us
  transfers between devices with their start and end apart: 39, of which 18 were waited for; matrix products, arithmetic and copies ran while one was open for 2% of the time, Pallas kernels for 17%

profile of v2, /device:TPU:0, one launch (start us, length us, event | category | flops | bytes accessed | tf_op | source)
XLA Modules:
  0.0 157.4 jit_solution(17831368339089516161)
XLA Ops:
  0.6 2.0 %shard_map.203 = (bf16[112,576]{1,0:T(8,128)(2,1)}, bf16[144,768]{1,0:T(8,128)(2,1)}) custom-call(bf16[192,768]{1,0:T(8,128)(2,1)} %q.1, bf16[192,768]{1,0:T(8,128)(2,1)} %k.1, bf16[192,768]{1,0:T(8,128)(2,1)} %v.1, bf16[192]{0:T(256)(128)(2,1)} %first.1, bf16[192]{0:T(256)(128)(2,1)} %second.1, bf16[8,12]{1,0:T(8,128)(2,1)} %table.1, ...), custom_call_target="tpu_custom_call" | custom-call | flops 1000000 | bytes 1024 | tf_op jit(solution)/shard_map/pallas_call | solution.py:48
  2.7 5.1 %collective-permute-start.2 = (bf16[112,576]{1,0:T(8,128)(2,1)}, bf16[112,576]{1,0:T(8,128)(2,1)S(1)}, u32[]{:S(2)}, u32[]{:S(2)}) collective-permute-start(bf16[112,576]{1,0:T(8,128)(2,1)} %get-tuple-element.104.refs_0_), channel_id=1, source_target_pairs={{0,3},{1,2},{2,1},{3,0},{4,7},{5,6},{6,5},{7,4},{8,11},{9,10},{10,... | collective-permute-start | bytes 387080 | tf_op jit(solution)/shard_map/ppermute | solution.py:679
  9.0 2.9 %shard_map.204.refs_7_ = bf16[576,384]{1,0:T(8,128)(2,1)} custom-call(s32[4]{0:T(128)} %pad_add_fusion.ids, bf16[192,768]{1,0:T(8,128)(2,1)} %wo.1, bf16[192,3072]{1,0:T(8,128)(2,1)} %inner.1, bf16[768,768]{1,0:T(8,128)(2,1)} %outer.1), custom_call_target="tpu_custom_call" | custom-call | flops 1000000 | bytes 1024 | tf_op jit(solution)/shard_map/pallas_call | solution.py:48
  11.9 12.1 %all-gather = bf16[576,768]{1,0:T(8,128)(2,1)S(1)} all-gather(bf16[144,768]{1,0:T(8,128)(2,1)S(1)} %copy-done.4), channel_id=2, replica_groups={{0,8,16,24},{4,12,20,28},{1,9,17,25},{5,13,21,29},{2,10,18,26},{6,14,22..., dimensions={0}, use_global_device_ids=true | all-gather | bytes 1105920 | tf_op jit(solution)/shard_map/all_gather | solution.py:749
  24.1 1.5 collective-permute-start.10
  27.0 3.6 %collective-permute-start.13 = (bf16[576,384]{1,0:T(8,128)(2,1)}, bf16[576,384]{1,0:T(8,128)(2,1)S(1)}, u32[]{:S(2)}, u32[]{:S(2)}) collective-permute-start(bf16[576,384]{1,0:T(8,128)(2,1)} %shard_map.204.refs_7_), channel_id=1, source_target_pairs={{0,3},{1,2},{2,1},{3,0},{4,7},{5,6},{6,5},{7,4},{8,11},{9,10},{10,... | collective-permute-start | bytes 1327112 | tf_op jit(solution)/shard_map/ppermute | solution.py:679
  30.6 1.7 %collective-permute-done.10.refs_6_ = bf16[128,768]{1,0:T(8,128)(2,1)S(1)} collective-permute-done((bf16[128,768]{1,0:T(8,128)(2,1)S(1)}, bf16[128,768]{1,0:T(8,128)(2,1)S(1)}, u32[]{:S(2)}, u32[]{:S(2)}) %collective-permute-start.10) | collective-permute-done | bytes 196640 | tf_op jit(solution)/shard_map/ppermute | solution.py:676
  32.3 2.1 %collective-permute-start.12 = (bf16[576,384]{1,0:T(8,128)(2,1)}, bf16[576,384]{1,0:T(8,128)(2,1)S(1)}, u32[]{:S(2)}, u32[]{:S(2)}) collective-permute-start(bf16[576,384]{1,0:T(8,128)(2,1)} %shard_map.204.refs_7_), channel_id=1, source_target_pairs={{0,2},{1,3},{2,0},{3,1},{4,6},{5,7},{6,4},{7,5},{8,10},{9,11},{10,... | collective-permute-start | bytes 1327112 | tf_op jit(solution)/shard_map/ppermute | solution.py:679
  34.4 2.0 %collective-permute-start.11 = (bf16[576,384]{1,0:T(8,128)(2,1)}, bf16[576,384]{1,0:T(8,128)(2,1)S(1)}, u32[]{:S(2)}, u32[]{:S(2)}) collective-permute-start(bf16[576,384]{1,0:T(8,128)(2,1)} %shard_map.204.refs_7_), channel_id=1, source_target_pairs={{0,1},{1,0},{2,3},{3,2},{4,5},{5,4},{6,7},{7,6},{8,9},{9,8},{10,11... | collective-permute-start | bytes 1327112 | tf_op jit(solution)/shard_map/ppermute | solution.py:679
  37.8 2.1 %collective-permute-start.9 = (bf16[128,768]{1,0:T(8,128)(2,1)S(1)}, bf16[128,768]{1,0:T(8,128)(2,1)S(1)}, u32[]{:S(2)}, u32[]{:S(2)}) collective-permute-start(bf16[128,768]{1,0:T(8,128)(2,1)S(1)} %bitcast.21), channel_id=1, source_target_pairs={{0,16},{4,20},{8,24},{12,28},{16,0},{20,4},{24,8},{28,12},{1,17},{... | collective-permute-start | bytes 589832 | tf_op jit(solution)/shard_map/ppermute | solution.py:676
  40.0 2.2 %shard_map.205 = (bf16[1024,768]{1,0:T(8,128)(2,1)S(1)}, bf16[3,1024,128]{2,1,0:T(8,128)(2,1)S(1)}, bf16[3,512,128]{2,1,0:T(8,128)(2,1)S(1)}, f32[8,128]{1,0:T(8...) custom-call(s32[4]{0:T(128)S(1)} %copy-done.3, bf16[112,576]{1,0:T(8,128)(2,1)S(1)} %copy-done.1, ...), custom_call_target="tpu_custom_call" | custom-call | flops 1000000 | bytes 1024 | tf_op jit(solution)/shard_map/pallas_call | solution.py:48
  43.4 5.2 %shard_map.207 = (bf16[512,192]{1,0:T(8,128)(2,1)S(1)}, f32[2,8,256]{2,1,0:T(8,128)S(1)}) custom-call(s32[4]{0:T(128)S(1)} %copy-done.3, s32[4]{0:T(128)S(1)} %get-tuple-element.196.q_at, s32[8]{0:T(128)S(1)} %pad_add_fusion.1.k_at, bf16[3,512,128]{2,1,0:T(8,128)(2,1)S(1)} %get-tuple-element.106.query, f32[8,128]{1,0:T(8,128)S(1)} %get-tuple-element.107.seg_q.seg_k, ...), custom_call_target="tpu_custom_call" | custom-call | flops 1000000 | bytes 1024 | tf_op jit(solution)/shard_map/pallas_call | solution.py:48
  48.6 13.5 %all-gather.1 = bf16[2048,192]{1,0:T(8,128)(2,1)S(1)} all-gather(bf16[512,192]{1,0:T(8,128)(2,1)S(1)} %get-tuple-element.110), channel_id=3, replica_groups={{0,8,16,24},{4,12,20,28},{1,9,17,25},{5,13,21,29},{2,10,18,26},{6,14,22..., dimensions={0}, use_global_device_ids=true | all-gather | bytes 983040 | tf_op jit(solution)/shard_map/all_gather | solution.py:749
  62.1 6.4 %collective-permute-done.12.refs_9_ = bf16[576,384]{1,0:T(8,128)(2,1)S(1)} collective-permute-done((bf16[576,384]{1,0:T(8,128)(2,1)}, bf16[576,384]{1,0:T(8,128)(2,1)S(1)}, u32[]{:S(2)}, u32[]{:S(2)}) %collective-permute-start.12) | collective-permute-done | bytes 442400 | tf_op jit(solution)/shard_map/ppermute | solution.py:679
  72.2 8.5 %shard_map.208 = (f32[128,768]{1,0:T(8,128)S(1)}, bf16[128,768]{1,0:T(8,128)(2,1)S(1)}, bf16[128,768]{1,0:T(8,128)(2,1)S(1)}, bf16[128,768]{1,0:T(8,128)(2,1)S(1...) custom-call(s32[4]{0:T(128)S(1)} %copy-done.3, ...), custom_call_target="tpu_custom_call" | custom-call | flops 10000000 | bytes 1024 | tf_op jit(solution)/shard_map/pallas_call | solution.py:48
  80.7 3.0 %shard_map.209 = (f32[3,4,96,768]{3,2,1,0:T(8,128)S(1)}, bf16[3,4,96,768]{3,2,1,0:T(8,128)(2,1)S(1)}) custom-call(s32[4]{0:T(128)S(1)} %copy-done.3, bf16[512,768]{1,0:T(8,128)(2,1)S(1)} %get-tuple-element.127.normed, bf16[512,768]{1,0:T(8,128)(2,1)S(1)} %get-tuple-element.128.active, bf16[512,768]{1,0:T(8,128)(2,1)S(1)} %get-tuple-element.129.ginner, ...), custom_call_target="tpu_custom_call" | custom-call | flops 5000000 | bytes 1024 | tf_op jit(solution)/shard_map/pallas_call | solution.py:48
  88.5 1.5 collective-permute-start.22
  90.0 3.0 %collective-permute-done.18.g1 = bf16[512,192]{1,0:T(8,128)(2,1)S(1)} collective-permute-done((bf16[512,192]{1,0:T(8,128)(2,1)S(1)}, bf16[512,192]{1,0:T(8,128)(2,1)S(1)}, u32[]{:S(2)}, u32[]{:S(2)}) %collective-permute-start.18) | collective-permute-done | bytes 196640 | tf_op jit(solution)/shard_map/ppermute | solution.py:676
  93.0 5.9 %collective-permute-done.19.g2 = bf16[512,192]{1,0:T(8,128)(2,1)S(1)} collective-permute-done((bf16[512,192]{1,0:T(8,128)(2,1)S(1)}, bf16[512,192]{1,0:T(8,128)(2,1)S(1)}, u32[]{:S(2)}, u32[]{:S(2)}) %collective-permute-start.19) | collective-permute-done | bytes 196640 | tf_op jit(solution)/shard_map/ppermute | solution.py:676
  100.1 1.5 collective-permute-start.24
  101.6 7.5 %shard_map.211 = (bf16[512,192]{1,0:T(8,128)(2,1)S(1)}, bf16[3,512,128]{2,1,0:T(8,128)(2,1)S(1)}, bf16[3,512,128]{2,1,0:T(8,128)(2,1)S(1)}, f32[3,5,128,128]{3,2,1,0:T(8,128)S(1)}) custom-call(s32[4]{0:T(128)S(1)} %copy-done.3, s32[4]{0:T(128)S(1)} %get-tuple-element.196.q_at, s32[8]{0:T(128)S(1)} %pad_add_fusion.1.k_at, ...), custom_call_target="tpu_custom_call" | custom-call | flops 30000001024 | bytes 1024 | tf_op jit(solution)/shard_map/pallas_call | solution.py:48
  109.3 1.9 %shard_map.214 = (f32[4,96,576]{2,1,0:T(8,128)S(1)}, bf16[384,576]{1,0:T(8,128)(2,1)S(1)}) custom-call(s32[4]{0:T(128)S(1)} %copy-done.3, bf16[1024,768]{1,0:T(8,128)(2,1)S(1)} %get-tuple-element.156.normed, bf16[512,192]{1,0:T(8,128)(2,1)S(1)} %get-tuple-element.140.dq, bf16[3,512,128]{2,1,0:T(8,128)(2,1)S(1)} %get-tuple-element.141.down, ...), custom_call_target="tpu_custom_call" | custom-call | flops 2000000 | bytes 1024 | tf_op jit(solution)/shard_map/pallas_call | solution.py:48
  111.8 1.7 %shard_map.215.table = f32[1,384]{1,0:T(1,128)S(1)} custom-call(s32[4]{0:T(128)S(1)} %copy-done.3, f32[3,5,128,128]{3,2,1,0:T(8,128)S(1)} %get-tuple-element.161.sums), custom_call_target="tpu_custom_call" | custom-call | flops 2000000 | bytes 1024 | tf_op jit(solution)/shard_map/pallas_call | solution.py:48
  113.7 3.0 %shard_map.213 = (f32[128,768]{1,0:T(8,128)S(1)}, bf16[256,768]{1,0:T(8,128)(2,1)}, bf16[256,768]{1,0:T(8,128)(2,1)S(1)}, bf16[256,768]{1,0:T(8,128)(2,1)S(1)}, ...) custom-call(s32[4]{0:T(128)S(1)} %copy-done.3, bf16[4,144,768]{2,1,0:T(8,128)(2,1)S(1)} %bitcast.17, ...), custom_call_target="tpu_custom_call" | custom-call | flops 2000000 | bytes 1024 | tf_op jit(solution)/shard_map/pallas_call | solution.py:48
  118.8 2.0 %collective-permute-start.33 = (bf16[272,576]{1,0:T(8,128)(2,1)S(1)}, bf16[272,576]{1,0:T(8,128)(2,1)S(1)}, u32[]{:S(2)}, u32[]{:S(2)}) collective-permute-start(bf16[272,576]{1,0:T(8,128)(2,1)S(1)} %get-tuple-element.165), channel_id=1, source_target_pairs={{0,1},{1,0},{2,3},{3,2},{4,5},{5,4},{6,7},{7,6},{8,9},{9,8},{10,11... | collective-permute-start | bytes 940040 | tf_op jit(solution)/shard_map/ppermute | solution.py:679
  124.2 10.0 %collective-permute-done.32.more = bf16[208,768]{1,0:T(8,128)(2,1)S(1)} collective-permute-done((bf16[208,768]{1,0:T(8,128)(2,1)S(1)}, bf16[208,768]{1,0:T(8,128)(2,1)S(1)}, u32[]{:S(2)}, u32[]{:S(2)}) %collective-permute-start.32) | collective-permute-done | bytes 319520 | tf_op jit(solution)/shard_map/ppermute | solution.py:679
  134.2 1.6 %collective-permute-done.33.more = bf16[272,576]{1,0:T(8,128)(2,1)S(1)} collective-permute-done((bf16[272,576]{1,0:T(8,128)(2,1)S(1)}, bf16[272,576]{1,0:T(8,128)(2,1)S(1)}, u32[]{:S(2)}, u32[]{:S(2)}) %collective-permute-start.33) | collective-permute-done | bytes 313376 | tf_op jit(solution)/shard_map/ppermute | solution.py:679
  137.2 9.3 %collective-permute-done.34.more = bf16[144,576]{1,0:T(8,128)(2,1)S(1)} collective-permute-done((bf16[144,576]{1,0:T(8,128)(2,1)S(1)}, bf16[144,576]{1,0:T(8,128)(2,1)S(1)}, u32[]{:S(2)}, u32[]{:S(2)}) %collective-permute-start.34) | collective-permute-done | bytes 165920 | tf_op jit(solution)/shard_map/ppermute | solution.py:679
  149.9 1.5 collective-permute-start.37
  151.3 2.4 %add_bitcast_fusion = (f32[1,128,768]{2,1,0:T(8,128)}, f32[1,128,768]{2,1,0:T(8,128)}) fusion(f32[128,768]{1,0:T(8,128)S(1)} %get-tuple-element.169, bf16[256,768]{1,0:T(8,128)(2,1)} %collective-permute-done.31, bf16[256,768]{1,0:T(8,128)(2,1)} %collective-permute-done.30, bf16[256,768]{1,0:T(8,128)(2,1)} %collective-permute-done.29, ...), kind=kLoop, calls=%fused_computation | loop fusion | flops 1179648 | bytes 2752512 | tf_op jit(solution)/shard_map/broadcast_in_dim | solution.py:1022
  153.8 2.0 %collective-permute-done.36.r2 = bf16[32,1344]{1,0:T(8,128)(2,1)S(1)} collective-permute-done((bf16[32,1344]{1,0:T(8,128)(2,1)S(1)}, bf16[32,1344]{1,0:T(8,128)(2,1)S(1)}, u32[]{:S(2)}, u32[]{:S(2)}) %collective-permute-start.36) | collective-permute-done | bytes 86048 | tf_op jit(solution)/shard_map/ppermute | solution.py:676
  155.7 1.7 %shard_map.221 = (f32[24,768]{1,0:T(8,128)}, f32[24,768]{1,0:T(8,128)}, f32[24,768]{1,0:T(8,128)}, f32[24,3072]{1,0:T(8,128)}, f32[1,24]{1,0:T(1,128)}, /*index=...) custom-call(s32[2]{0:T(128)S(1)} %pad_add_fusion.2.where, f32[24,1344]{1,0:T(8,128)S(1)} %get-tuple-element.178.own, ...), custom_call_target="tpu_custom_call" | custom-call | flops 1000000 | bytes 1024 | tf_op jit(solution)/shard_map/pallas_call | solution.py:48
  (82 shorter events, 26.3 us)
Async XLA Ops:
  2.7 21.3 %collective-permute-start.2 = (bf16[112,576]{1,0:T(8,128)(2,1)}, bf16[112,576]{1,0:T(8,128)(2,1)S(1)}, u32[]{:S(2)}, u32[]{:S(2)}) collective-permute-start(bf16[112,576]{1,0:T(8,128)(2,1)} %get-tuple-element.104.refs_0_), channel_id=1, source_target_pairs={{0,3},{1,2},{2,1},{3,0},{4,7},{5,6},{6,5},{7,4},{8,11},{9,10},{10,... | collective-permute-start | bytes 387080 | tf_op jit(solution)/shard_map/ppermute | solution.py:679
  7.8 16.2 %collective-permute-start.1 = (bf16[112,576]{1,0:T(8,128)(2,1)}, bf16[112,576]{1,0:T(8,128)(2,1)S(1)}, u32[]{:S(2)}, u32[]{:S(2)}) collective-permute-start(bf16[112,576]{1,0:T(8,128)(2,1)} %get-tuple-element.104.refs_0_), channel_id=1, source_target_pairs={{0,2},{1,3},{2,0},{3,1},{4,6},{5,7},{6,4},{7,5},{8,10},{9,11},{10,... | collective-permute-start | bytes 387080 | tf_op jit(solution)/shard_map/ppermute | solution.py:679
  7.8 16.2 %collective-permute-start = (bf16[112,576]{1,0:T(8,128)(2,1)}, bf16[112,576]{1,0:T(8,128)(2,1)S(1)}, u32[]{:S(2)}, u32[]{:S(2)}) collective-permute-start(bf16[112,576]{1,0:T(8,128)(2,1)} %get-tuple-element.104.refs_0_), channel_id=1, source_target_pairs={{0,1},{1,0},{2,3},{3,2},{4,5},{5,4},{6,7},{7,6},{8,9},{9,8},{10,11... | collective-permute-start | bytes 387080 | tf_op jit(solution)/shard_map/ppermute | solution.py:679
  24.0 15.9 %collective-permute-start.7 = (bf16[4,144,768]{2,1,0:T(8,128)(2,1)S(1)}, bf16[4,144,768]{2,1,0:T(8,128)(2,1)S(1)}, u32[]{:S(2)}, u32[]{:S(2)}) collective-permute-start(bf16[4,144,768]{2,1,0:T(8,128)(2,1)S(1)} %bitcast.14), channel_id=1, source_target_pairs={{0,4},{4,0},{8,12},{12,8},{16,20},{20,16},{24,28},{28,24},{1,5},{5... | collective-permute-start | bytes 2654216 | tf_op jit(solution)/shard_map/ppermute | solution.py:682
  24.1 8.2 %collective-permute-start.10 = (bf16[128,768]{1,0:T(8,128)(2,1)S(1)}, bf16[128,768]{1,0:T(8,128)(2,1)S(1)}, u32[]{:S(2)}, u32[]{:S(2)}) collective-permute-start(bf16[128,768]{1,0:T(8,128)(2,1)S(1)} %bitcast.20), channel_id=1, source_target_pairs={{0,24},{4,28},{8,16},{12,20},{16,8},{20,12},{24,0},{28,4},{1,25},{... | collective-permute-start | bytes 589832 | tf_op jit(solution)/shard_map/ppermute | solution.py:676
  25.8 8.7 %collective-permute-start.6 = (bf16[112,576]{1,0:T(8,128)(2,1)S(1)}, bf16[112,576]{1,0:T(8,128)(2,1)S(1)}, u32[]{:S(2)}, u32[]{:S(2)}) collective-permute-start(bf16[112,576]{1,0:T(8,128)(2,1)S(1)} %collective-permute-done.2.refs_3_), channel_id=1, source_target_pairs={{0,4},{4,0},{8,12},{12,8},{16,20},{20,16},{24,28},{28,24},{1,5},{5... | collective-permute-start | bytes 387080 | tf_op jit(solution)/shard_map/ppermute | solution.py:682
  26.1 10.3 %collective-permute-start.5 = (bf16[112,576]{1,0:T(8,128)(2,1)S(1)}, bf16[112,576]{1,0:T(8,128)(2,1)S(1)}, u32[]{:S(2)}, u32[]{:S(2)}) collective-permute-start(bf16[112,576]{1,0:T(8,128)(2,1)S(1)} %collective-permute-done.1.refs_2_), channel_id=1, source_target_pairs={{0,4},{4,0},{8,12},{12,8},{16,20},{20,16},{24,28},{28,24},{1,5},{5... | collective-permute-start | bytes 387080 | tf_op jit(solution)/shard_map/ppermute | solution.py:682
  27.0 35.1 %collective-permute-start.13 = (bf16[576,384]{1,0:T(8,128)(2,1)}, bf16[576,384]{1,0:T(8,128)(2,1)S(1)}, u32[]{:S(2)}, u32[]{:S(2)}) collective-permute-start(bf16[576,384]{1,0:T(8,128)(2,1)} %shard_map.204.refs_7_), channel_id=1, source_target_pairs={{0,3},{1,2},{2,1},{3,0},{4,7},{5,6},{6,5},{7,4},{8,11},{9,10},{10,... | collective-permute-start | bytes 1327112 | tf_op jit(solution)/shard_map/ppermute | solution.py:679
  32.3 36.2 %collective-permute-start.12 = (bf16[576,384]{1,0:T(8,128)(2,1)}, bf16[576,384]{1,0:T(8,128)(2,1)S(1)}, u32[]{:S(2)}, u32[]{:S(2)}) collective-permute-start(bf16[576,384]{1,0:T(8,128)(2,1)} %shard_map.204.refs_7_), channel_id=1, source_target_pairs={{0,2},{1,3},{2,0},{3,1},{4,6},{5,7},{6,4},{7,5},{8,10},{9,11},{10,... | collective-permute-start | bytes 1327112 | tf_op jit(solution)/shard_map/ppermute | solution.py:679
  34.4 34.1 %collective-permute-start.11 = (bf16[576,384]{1,0:T(8,128)(2,1)}, bf16[576,384]{1,0:T(8,128)(2,1)S(1)}, u32[]{:S(2)}, u32[]{:S(2)}) collective-permute-start(bf16[576,384]{1,0:T(8,128)(2,1)} %shard_map.204.refs_7_), channel_id=1, source_target_pairs={{0,1},{1,0},{2,3},{3,2},{4,5},{5,4},{6,7},{7,6},{8,9},{9,8},{10,11... | collective-permute-start | bytes 1327112 | tf_op jit(solution)/shard_map/ppermute | solution.py:679
  37.8 24.3 %collective-permute-start.9 = (bf16[128,768]{1,0:T(8,128)(2,1)S(1)}, bf16[128,768]{1,0:T(8,128)(2,1)S(1)}, u32[]{:S(2)}, u32[]{:S(2)}) collective-permute-start(bf16[128,768]{1,0:T(8,128)(2,1)S(1)} %bitcast.21), channel_id=1, source_target_pairs={{0,16},{4,20},{8,24},{12,28},{16,0},{20,4},{24,8},{28,12},{1,17},{... | collective-permute-start | bytes 589832 | tf_op jit(solution)/shard_map/ppermute | solution.py:676
  39.9 22.2 %collective-permute-start.8 = (bf16[128,768]{1,0:T(8,128)(2,1)S(1)}, bf16[128,768]{1,0:T(8,128)(2,1)S(1)}, u32[]{:S(2)}, u32[]{:S(2)}) collective-permute-start(bf16[128,768]{1,0:T(8,128)(2,1)S(1)} %bitcast.22), channel_id=1, source_target_pairs={{0,8},{4,12},{8,0},{12,4},{16,24},{20,28},{24,16},{28,20},{1,9},{5... | collective-permute-start | bytes 589832 | tf_op jit(solution)/shard_map/ppermute | solution.py:676
  69.1 3.1 %collective-permute-start.17 = (bf16[576,384]{1,0:T(8,128)(2,1)S(1)}, bf16[576,384]{1,0:T(8,128)(2,1)S(1)}, u32[]{:S(2)}, u32[]{:S(2)}) collective-permute-start(bf16[576,384]{1,0:T(8,128)(2,1)S(1)} %collective-permute-done.13.refs_10_), channel_id=1, source_target_pairs={{0,4},{4,0},{8,12},{12,8},{16,20},{20,16},{24,28},{28,24},{1,5},{5... | collective-permute-start | bytes 1327112 | tf_op jit(solution)/shard_map/ppermute | solution.py:682
  83.7 3.8 %collective-permute-start.21 = (bf16[3,4,96,768]{3,2,1,0:T(8,128)(2,1)S(1)}, bf16[3,4,96,768]{3,2,1,0:T(8,128)(2,1)S(1)}, u32[]{:S(2)}, u32[]{:S(2)}) collective-permute-start(bf16[3,4,96,768]{3,2,1,0:T(8,128)(2,1)S(1)} %get-tuple-element.133), channel_id=1, source_target_pairs={{0,4},{4,0},{8,12},{12,8},{16,20},{20,16},{24,28},{28,24},{1,5},{5... | collective-permute-start | bytes 5308424 | tf_op jit(solution)/shard_map/ppermute | solution.py:682
  83.9 9.1 %collective-permute-start.18 = (bf16[512,192]{1,0:T(8,128)(2,1)S(1)}, bf16[512,192]{1,0:T(8,128)(2,1)S(1)}, u32[]{:S(2)}, u32[]{:S(2)}) collective-permute-start(bf16[512,192]{1,0:T(8,128)(2,1)S(1)} %get-tuple-element.124), channel_id=1, source_target_pairs={{0,8},{4,12},{8,0},{12,4},{16,24},{20,28},{24,16},{28,20},{1,9},{5... | collective-permute-start | bytes 589832 | tf_op jit(solution)/shard_map/ppermute | solution.py:676
  85.3 13.6 %collective-permute-start.19 = (bf16[512,192]{1,0:T(8,128)(2,1)S(1)}, bf16[512,192]{1,0:T(8,128)(2,1)S(1)}, u32[]{:S(2)}, u32[]{:S(2)}) collective-permute-start(bf16[512,192]{1,0:T(8,128)(2,1)S(1)} %get-tuple-element.125), channel_id=1, source_target_pairs={{0,16},{4,20},{8,24},{12,28},{16,0},{20,4},{24,8},{28,12},{1,17},{... | collective-permute-start | bytes 589832 | tf_op jit(solution)/shard_map/ppermute | solution.py:676
  85.9 13.6 %collective-permute-start.20 = (bf16[512,192]{1,0:T(8,128)(2,1)S(1)}, bf16[512,192]{1,0:T(8,128)(2,1)S(1)}, u32[]{:S(2)}, u32[]{:S(2)}) collective-permute-start(bf16[512,192]{1,0:T(8,128)(2,1)S(1)} %get-tuple-element.126), channel_id=1, source_target_pairs={{0,24},{4,28},{8,16},{12,20},{16,8},{20,12},{24,0},{28,4},{1,25},{... | collective-permute-start | bytes 589832 | tf_op jit(solution)/shard_map/ppermute | solution.py:676
  88.5 20.7 %collective-permute-start.22 = (bf16[96,768]{1,0:T(8,128)(2,1)S(1)}, bf16[96,768]{1,0:T(8,128)(2,1)S(1)}, u32[]{:S(2)}, u32[]{:S(2)}) collective-permute-start(bf16[96,768]{1,0:T(8,128)(2,1)S(1)} %get-tuple-element.135), channel_id=1, source_target_pairs={{0,8},{4,12},{8,0},{12,4},{16,24},{20,28},{24,16},{28,20},{1,9},{5... | collective-permute-start | bytes 442376 | tf_op jit(solution)/shard_map/ppermute | solution.py:676
  90.0 19.2 %collective-permute-start.25 = (bf16[384,768]{1,0:T(8,128)(2,1)S(1)}, bf16[384,768]{1,0:T(8,128)(2,1)S(1)}, u32[]{:S(2)}, u32[]{:S(2)}) collective-permute-start(bf16[384,768]{1,0:T(8,128)(2,1)S(1)} %get-tuple-element.134), channel_id=1, source_target_pairs={{0,1},{1,0},{2,3},{3,2},{4,5},{5,4},{6,7},{7,6},{8,9},{9,8},{10,11... | collective-permute-start | bytes 1769480 | tf_op jit(solution)/shard_map/ppermute | solution.py:679
  99.5 9.6 %collective-permute-start.23 = (bf16[96,768]{1,0:T(8,128)(2,1)S(1)}, bf16[96,768]{1,0:T(8,128)(2,1)S(1)}, u32[]{:S(2)}, u32[]{:S(2)}) collective-permute-start(bf16[96,768]{1,0:T(8,128)(2,1)S(1)} %get-tuple-element.143), channel_id=1, source_target_pairs={{0,16},{4,20},{8,24},{12,28},{16,0},{20,4},{24,8},{28,12},{1,17},{... | collective-permute-start | bytes 442376 | tf_op jit(solution)/shard_map/ppermute | solution.py:676
  100.1 9.0 %collective-permute-start.24 = (bf16[96,768]{1,0:T(8,128)(2,1)S(1)}, bf16[96,768]{1,0:T(8,128)(2,1)S(1)}, u32[]{:S(2)}, u32[]{:S(2)}) collective-permute-start(bf16[96,768]{1,0:T(8,128)(2,1)S(1)} %get-tuple-element.144), channel_id=1, source_target_pairs={{0,24},{4,28},{8,16},{12,20},{16,8},{20,12},{24,0},{28,4},{1,25},{... | collective-permute-start | bytes 442376 | tf_op jit(solution)/shard_map/ppermute | solution.py:676
  111.2 6.7 %collective-permute-start.27 = (bf16[384,576]{1,0:T(8,128)(2,1)S(1)}, bf16[384,576]{1,0:T(8,128)(2,1)S(1)}, u32[]{:S(2)}, u32[]{:S(2)}) collective-permute-start(bf16[384,576]{1,0:T(8,128)(2,1)S(1)} %get-tuple-element.158), channel_id=1, source_target_pairs={{0,4},{4,0},{8,12},{12,8},{16,20},{20,16},{24,28},{28,24},{1,5},{5... | collective-permute-start | bytes 1327112 | tf_op jit(solution)/shard_map/ppermute | solution.py:682
  116.9 17.4 %collective-permute-start.32 = (bf16[208,768]{1,0:T(8,128)(2,1)S(1)}, bf16[208,768]{1,0:T(8,128)(2,1)S(1)}, u32[]{:S(2)}, u32[]{:S(2)}) collective-permute-start(bf16[208,768]{1,0:T(8,128)(2,1)S(1)} %get-tuple-element.147), channel_id=1, source_target_pairs={{0,2},{1,3},{2,0},{3,1},{4,6},{5,7},{6,4},{7,5},{8,10},{9,11},{10,... | collective-permute-start | bytes 958472 | tf_op jit(solution)/shard_map/ppermute | solution.py:679
  118.8 17.1 %collective-permute-start.33 = (bf16[272,576]{1,0:T(8,128)(2,1)S(1)}, bf16[272,576]{1,0:T(8,128)(2,1)S(1)}, u32[]{:S(2)}, u32[]{:S(2)}) collective-permute-start(bf16[272,576]{1,0:T(8,128)(2,1)S(1)} %get-tuple-element.165), channel_id=1, source_target_pairs={{0,1},{1,0},{2,3},{3,2},{4,5},{5,4},{6,7},{7,6},{8,9},{9,8},{10,11... | collective-permute-start | bytes 940040 | tf_op jit(solution)/shard_map/ppermute | solution.py:679
  120.7 28.5 %collective-permute-start.29 = (bf16[256,768]{1,0:T(8,128)(2,1)}, bf16[256,768]{1,0:T(8,128)(2,1)}, u32[]{:S(2)}, u32[]{:S(2)}) collective-permute-start(bf16[256,768]{1,0:T(8,128)(2,1)} %get-tuple-element.166), channel_id=1, source_target_pairs={{0,8},{4,12},{8,0},{12,4},{16,24},{20,28},{24,16},{28,20},{1,9},{5... | collective-permute-start | bytes 1179656 | tf_op jit(solution)/shard_map/ppermute | solution.py:676
  122.1 27.7 %collective-permute-start.30 = (bf16[256,768]{1,0:T(8,128)(2,1)S(1)}, bf16[256,768]{1,0:T(8,128)(2,1)}, u32[]{:S(2)}, u32[]{:S(2)}) collective-permute-start(bf16[256,768]{1,0:T(8,128)(2,1)S(1)} %get-tuple-element.167), channel_id=1, source_target_pairs={{0,16},{4,20},{8,24},{12,28},{16,0},{20,4},{24,8},{28,12},{1,17},{... | collective-permute-start | bytes 1179656 | tf_op jit(solution)/shard_map/ppermute | solution.py:676
  122.7 28.6 %collective-permute-start.31 = (bf16[256,768]{1,0:T(8,128)(2,1)S(1)}, bf16[256,768]{1,0:T(8,128)(2,1)}, u32[]{:S(2)}, u32[]{:S(2)}) collective-permute-start(bf16[256,768]{1,0:T(8,128)(2,1)S(1)} %get-tuple-element.168), channel_id=1, source_target_pairs={{0,24},{4,28},{8,16},{12,20},{16,8},{20,12},{24,0},{28,4},{1,25},{... | collective-permute-start | bytes 1179656 | tf_op jit(solution)/shard_map/ppermute | solution.py:676
  135.9 10.6 %collective-permute-start.34 = (bf16[144,576]{1,0:T(8,128)(2,1)S(1)}, bf16[144,576]{1,0:T(8,128)(2,1)S(1)}, u32[]{:S(2)}, u32[]{:S(2)}) collective-permute-start(bf16[144,576]{1,0:T(8,128)(2,1)S(1)} %get-tuple-element.174), channel_id=1, source_target_pairs={{0,2},{1,3},{2,0},{3,1},{4,6},{5,7},{6,4},{7,5},{8,10},{9,11},{10,... | collective-permute-start | bytes 497672 | tf_op jit(solution)/shard_map/ppermute | solution.py:679
  136.5 17.2 %collective-permute-start.38 = (bf16[96,768]{1,0:T(8,128)(2,1)S(1)}, bf16[96,768]{1,0:T(8,128)(2,1)S(1)}, u32[]{:S(2)}, u32[]{:S(2)}) collective-permute-start(bf16[96,768]{1,0:T(8,128)(2,1)S(1)} %get-tuple-element.183), channel_id=1, source_target_pairs={{0,0},{1,9},{2,18},{3,27},{4,4},{5,13},{6,22},{7,31},{8,8},{9,1},{... | collective-permute-start | bytes 442376 | tf_op jit(solution)/shard_map/ppermute | solution.py:953
  147.8 5.9 %collective-permute-start.35 = (bf16[32,1344]{1,0:T(8,128)(2,1)S(1)}, bf16[32,1344]{1,0:T(8,128)(2,1)S(1)}, u32[]{:S(2)}, u32[]{:S(2)}) collective-permute-start(bf16[32,1344]{1,0:T(8,128)(2,1)S(1)} %get-tuple-element.179), channel_id=1, source_target_pairs={{0,8},{4,12},{8,0},{12,4},{16,24},{20,28},{24,16},{28,20},{1,9},{5... | collective-permute-start | bytes 258056 | tf_op jit(solution)/shard_map/ppermute | solution.py:676
  149.3 6.5 %collective-permute-start.36 = (bf16[32,1344]{1,0:T(8,128)(2,1)S(1)}, bf16[32,1344]{1,0:T(8,128)(2,1)S(1)}, u32[]{:S(2)}, u32[]{:S(2)}) collective-permute-start(bf16[32,1344]{1,0:T(8,128)(2,1)S(1)} %get-tuple-element.180), channel_id=1, source_target_pairs={{0,16},{4,20},{8,24},{12,28},{16,0},{20,4},{24,8},{28,12},{1,17},{... | collective-permute-start | bytes 258056 | tf_op jit(solution)/shard_map/ppermute | solution.py:676
  149.9 5.8 %collective-permute-start.37 = (bf16[32,1344]{1,0:T(8,128)(2,1)S(1)}, bf16[32,1344]{1,0:T(8,128)(2,1)S(1)}, u32[]{:S(2)}, u32[]{:S(2)}) collective-permute-start(bf16[32,1344]{1,0:T(8,128)(2,1)S(1)} %get-tuple-element.181), channel_id=1, source_target_pairs={{0,24},{4,28},{8,16},{12,20},{16,8},{20,12},{24,0},{28,4},{1,25},{... | collective-permute-start | bytes 258056 | tf_op jit(solution)/shard_map/ppermute | solution.py:676
  (12 other events, 104.4 us)

commit v3 on v2

--- a/solution.py
+++ b/solution.py
@@ -41,7 +41,7 @@
     return nearer + jnp.where(offset > 0, 16, 0)
 
 
-def call(kernel, outs, args, scalars=1, scratch=(), mib=16, us=2, far=()):
+def call(kernel, outs, args, scalars=1, scratch=(), mib=12, us=2, far=()):
     vmem = pl.BlockSpec(memory_space=pltpu.VMEM)
     smem = pl.BlockSpec(memory_space=pltpu.SMEM)
     hbm = pl.BlockSpec(memory_space=pltpu.HBM)
@@ -298,15 +298,14 @@
 def middle_kernel(T, ids, *refs):
     g, half, f = ids[0], ids[1], ids[2]
     x, ctx, gains = refs[0:3]
-    cots, ws, others = refs[3:7], refs[7:11], refs[11:15]
-    res0, sends, gcs = refs[15], refs[16:19], refs[19:23]
-    grads, normed, active, ginner, branch, cot_all, gain_grad = refs[23:30]
-    WO, W1, W2, held = refs[30:34]
+    cot_all, ws, others = refs[3], refs[4:8], refs[8:12]
+    res0, sends, gcs = refs[12], refs[13:16], refs[16:20]
+    grads, normed, active, ginner, branch = refs[20:25]
+    WO, W1, W2, held = refs[25:29]
     rows, low = WO.shape[2], WO.shape[2] // 2
     FH = W1.shape[3]
     for k in range(4):
         z = f ^ k
-        cot_all[g ^ k] = cots[k][...]
         for at, pieces in ((half, ws), (1 - half, others)):
             piece = pieces[k]
             WO[z, at] = piece[:rows]
@@ -314,7 +313,6 @@
             W2[at, z, :, 0 : D // 2] = piece[2 * rows : 2 * rows + low]
             W2[at, z, :, D // 2 :] = piece[2 * rows + low :]
     gain = gains[1:2, :]
-    gain_grad[...] = jnp.zeros_like(gain_grad)
 
     def out_rows(a):
         return jnp.concatenate([WO[a, 0], WO[a, 1]], axis=1)
@@ -355,7 +353,6 @@
                 held[m] += att[index * T : (index + 1) * T]
 
         u = gn * gain
-        gain_grad[...] += jnp.sum(gn * att * s, axis=0, keepdims=True)
         grad = 0.25 * cot.astype(f32) + s * u - att * (s * s * s) * jnp.mean(u * att, axis=-1, keepdims=True)
         grads[at, :] = grad
         gb = grad.astype(bf16)
@@ -387,7 +384,7 @@
 def tail_kernel(T, ids, x_all, dq, down, doth, grads, gains, *refs):
     g, half, f = ids[0], ids[1], ids[2]
     ws, os, rs = refs[0:4], refs[4:8], refs[8:11]
-    own, s1, s2, s3, joined, gain_grad, W, held = refs[11:]
+    own, s1, s2, s3, joined, W, held = refs[11:]
     rows = W.shape[2]
     sends = (s1, s2, s3)
     for k in range(4):
@@ -396,7 +393,6 @@
         W[z, 1 - half] = os[k][:rows, :]
     weight = W[...].reshape(D, 3 * CG)
     gain = gains[0:1, :]
-    gain_grad[...] = jnp.zeros_like(gain_grad)
     for i in range(2):
         at = slice(2 * i * T, (2 * i + 2) * T)
         parts = [(down[h, at, :].astype(f32) + doth[h, at, :].astype(f32)).astype(bf16) for h in range(HG)]
@@ -406,7 +402,6 @@
         x = jnp.concatenate([x_all[m, :T, :] for m in (2 * i, 2 * i + 1)], axis=0).astype(f32)
         s = lax.rsqrt(jnp.mean(x * x, axis=-1, keepdims=True) + epsilon)
         u = gn * gain
-        gain_grad[...] += jnp.sum(gn * x * s, axis=0, keepdims=True)
         total = grads[at, :] + s * u - x * (s * s * s) * jnp.mean(u * x, axis=-1, keepdims=True)
         for index, m in enumerate((2 * i, 2 * i + 1)):
             held[m] = total[index * T : (index + 1) * T]
@@ -434,11 +429,9 @@
         send[a * R : (a + 1) * R, :] = gw[a, 1 - c].astype(bf16)
 
 
-def extra_kernel(second, first, table, block, send):
-    wide = jnp.zeros((1, 3 * CG - D // 2), f32)
-    vectors = [second[:, : D // 2], second[:, D // 2 :], first[:, : D // 2], first[:, D // 2 :], table[...]]
-    rows = jnp.concatenate([jnp.concatenate([v, wide], axis=1) for v in vectors], axis=0)
-    rows = jnp.concatenate([rows, jnp.zeros((3, 3 * CG), f32)], axis=0)
+def extra_kernel(table, block, send):
+    rows = jnp.concatenate([table[...], jnp.zeros((1, 3 * CG - 32 * H), f32)], axis=1)
+    rows = jnp.concatenate([rows, jnp.zeros((7, 3 * CG), f32)], axis=0)
     block[...] = rows
     send[...] = split_rows(rows)
 
@@ -476,8 +469,10 @@
             out[:rows, :] = jnp.concatenate(pieces, axis=1)
 
 
-def middle_pack_kernel(ids, wo, inner, outer, out, held, block, sems):
-    g, side, f = ids[0], ids[1], ids[2]
+def middle_pack_kernel(C, ids, wo, inner, outer, out, held, block, sems):
+    place, f = lax.axis_index("seq"), lax.axis_index("fsdp")
+    g = lax.div(place, C)
+    side = lax.rem(place, C) if ids is None else ids[1]
     R0, F0 = wo.shape[0], outer.shape[0]
     FB, low = F0 // 8, R0 // 2
     half = F0 // 2
@@ -521,8 +516,8 @@
         right = keep[1, at ^ g] + more[1, at ^ g].astype(f32)
         return [total[a, at] for a in range(4)] + [right]
 
-    far[...] = jnp.concatenate(toward(f ^ 1) + toward(f ^ 3), axis=0).astype(bf16)
-    near[...] = jnp.concatenate(toward(f) + toward(f ^ 2), axis=0)
+    far[...] = jnp.concatenate(toward(f ^ 2) + toward(f ^ 3), axis=0).astype(bf16)
+    near[...] = jnp.concatenate(toward(f) + toward(f ^ 1), axis=0)
     for k, out in enumerate((wown, p1, p2, p3)):
         out[...] = (keep[2, g ^ k] + more[2, g ^ k].astype(f32)).astype(out.dtype)
 
@@ -531,15 +526,33 @@
     value = near[...] + more[...].astype(f32)
     count = mine.shape[0]
     mine[...] = value[:count]
-    send[:count, :] = value[count:].astype(bf16)
-    send[count:, :] = jnp.zeros((send.shape[0] - count, send.shape[1]), bf16)
-
-
-def middle_sum_kernel(own, more, inner, outer):
+    send[...] = value[count:].astype(bf16)
+
+
+def rows_kernel(ids, *refs):
+    qs, ws, os = refs[0:4], refs[4:8], refs[8:12]
+    first, second, narrow_rows, wide_rows = refs[12:16]
+    half, f, c = ids[1], ids[2], ids[3]
     R = D // 8
-    value = own[...] + more[: 2 * R, :].astype(f32)
+    RR, R0 = R // 4, D // 4
+    for k in range(4):
+        narrow_rows[f ^ k] = qs[k][:R, :].astype(f32)
+        for at, pieces in ((half, ws), (1 - half, os)):
+            wide_rows[f ^ k, at] = pieces[k][R0 : 2 * R0, :].astype(f32)
+    at = pl.ds(pl.multiple_of(RR * f, 8), RR)
+    there = pl.ds(pl.multiple_of(R * c + RR * f, 8), RR)
+    for a in range(4):
+        first[a * RR : (a + 1) * RR, :] = narrow_rows[a, at, :]
+        rows = jnp.concatenate([wide_rows[a, 0, there, :], wide_rows[a, 1, there, :]], axis=1)
+        second[a * RR : (a + 1) * RR, :] = rows
+
+
+def middle_sum_kernel(own, more, rows, inner, outer, sums):
+    R = D // 8
+    value = own[...] + more[...].astype(f32)
     inner[...] = value[:R]
     outer[...] = value[R:].astype(bf16)
+    sums[...] = jnp.sum(rows[...] * value[:R], axis=1, keepdims=True)
 
 
 def unsplit(block):
@@ -595,7 +608,7 @@
     send[count:, :] = split_rows(ex)
 
 
-def project_plane_kernel(ids, own, more, extra, inner, s1, s2, s3, mine, extra_out, output, total, held):
+def project_plane_kernel(ids, own, more, extra, inner, second, rows, s1, s2, s3, mine, extra_out, output, total, held, sums):
     g = ids[0]
     R = D // 8
     RR = R // 4
@@ -606,15 +619,27 @@
     output[...] = widen(value[R:])
     total[...] = value[:R].reshape(4, RR, 3 * CG)
     held[...] = inner[...].reshape(4, RR, D)
+    products = jnp.sum(rows[...] * value[:R], axis=1, keepdims=True)
+    lane = lax.broadcasted_iota(jnp.int32, (RR, 128), 1)
+    for a in range(4):
+        one = products[a * RR : (a + 1) * RR, :]
+        two = second[a * RR : (a + 1) * RR, :]
+        columns = jnp.zeros((RR, 128), f32)
+        for n, part in enumerate((one, two)):
+            high = part.astype(bf16).astype(f32)
+            columns = jnp.where(lane == 2 * n, high, columns)
+            columns = jnp.where(lane == 2 * n + 1, part - high, columns)
+        sums[a] = columns
     high = ex.astype(bf16).astype(f32)
     low = ex - high
-    tail = jnp.concatenate([high[:, : D // 2], low[:, : D // 2], jnp.zeros((8, 3 * CG), f32)], axis=1)
+    width = 3 * CG + D + 128
+    tail = jnp.concatenate([high[:, : D // 2], low[:, : D // 2], jnp.zeros((8, width - D), f32)], axis=1)
     for k, out in enumerate((mine, s1, s2, s3)):
-        block = jnp.concatenate([total[g ^ k], held[g ^ k]], axis=1)
+        block = jnp.concatenate([total[g ^ k], held[g ^ k], sums[g ^ k]], axis=1)
         out[...] = block if k == 0 else jnp.concatenate([block, tail], axis=0).astype(bf16)
 
 
-def final_kernel(where, own, r1, r2, r3, extra, outer_in, query, key, value, inner, first, second, table, outer, slots, rows):
+def final_kernel(where, own, r1, r2, r3, extra, outer_in, gains, query, key, value, inner, first, second, table, outer, slots, rows):
     g, at = where[0], where[1]
     RR = D // 32
     ex = extra[...][:, : D // 2]
@@ -634,13 +659,13 @@
             inner[:, (8 * z + 4 * e) * 4 * RR : (8 * z + 4 * e + 4) * 4 * RR] = jnp.concatenate(
                 [slots[z ^ b, :, n : n + 4 * RR] for b in range(4)], axis=1
             )
-    own_gain = first.shape[1]
-    for r, out in ((0, second), (2, first)):
-        whole = jnp.concatenate([ex[r : r + 1], ex[r + 1 : r + 2]], axis=1)
-        count = D // own_gain
-        rows[...] = jnp.concatenate([whole[:, own_gain * n : own_gain * (n + 1)] for n in range(count)], axis=0)
-        out[...] = rows[pl.ds(at, 1), :]
-    table[...] = jnp.concatenate([ex[4:5, 32 * h : 32 * (h + 1)] for h in range(H)], axis=0)
+    columns = slots[0, :, base + D :] + slots[1, :, base + D :] + slots[2, :, base + D :] + slots[3, :, base + D :]
+    square = jnp.concatenate([columns, jnp.zeros((128 - RR, 128), f32)], axis=0).T
+    for n, out in enumerate((first, second)):
+        whole = gains[n : n + 1, :]
+        rows[...] = jnp.concatenate([whole[:, RR * m : RR * (m + 1)] for m in range(D // RR)], axis=0)
+        out[...] = (square[2 * n : 2 * n + 1, :RR] + square[2 * n + 1 : 2 * n + 2, :RR]) / rows[pl.ds(at, 1), :]
+    table[...] = jnp.concatenate([ex[0:1, 32 * h : 32 * (h + 1)] for h in range(H)], axis=0)
     outer[...] = outer_in[...].astype(f32)
 
 
@@ -723,10 +748,12 @@
         )
 
     def middle_pack(side):
+        own = fast and side is half
+        kernel = functools.partial(middle_pack_kernel, C)
         return call(
-            middle_pack_kernel,
+            functools.partial(kernel, None) if own else kernel,
             shape((3 * R0, D // 2), bf16),
-            [ids_for(side), output_weight, inner_weight, outer_weight],
+            ([] if own else [ids_for(side)]) + [output_weight, inner_weight, outer_weight],
             scratch=[
                 pltpu.VMEM((4, R0, 256), bf16),
                 pltpu.VMEM((F0 // 8, D), bf16),
@@ -734,7 +761,8 @@
             ],
             us=1,
             mib=60,
-            far=(1, 2, 3),
+            scalars=0 if own else 1,
+            far=range(4),
         )
 
     def after(values, *earlier):
@@ -749,11 +777,13 @@
         return lax.all_gather(value, "seq", axis=0, axis_index_groups=token_groups)
 
     w_pack, x_pack = start(half)
+    output_weight, inner_weight, outer_weight, w_pack = after(
+        (output_weight, inner_weight, outer_weight, w_pack), w_pack
+    )
     m_pack = middle_pack(half)
     ws = from_planes(w_pack)
-    ms = from_planes(m_pack)
+    m1, m2 = plane_move(m_pack, 1), plane_move(m_pack, 2)
     x_all = gather(after(x_pack, m_pack))
-    cots = from_group(after(cotangent[0], x_all))
     if fast:
         xo = [core_move(after(x_all, *ws))]
         wo = [core_move(w) for w in ws]
@@ -800,12 +830,21 @@
         mib=16 if fast else 48,
         us=1,
     )
-    ctx_all = gather(context)
-    cots, ms = after((tuple(cots), tuple(ms)), ctx_all)
     if fast:
-        mo = [core_move(m) for m in ms]
+        mo = [core_move(m_pack)]
+        ctx_all = gather(after(context, *mo))
+        m1, m2 = after((m1, m2), ctx_all)
+        m3 = plane_move(m2, 1)
+        mo += [core_move(m1), core_move(m2)]
+        cot_all = gather(after(cotangent[0], ctx_all, *mo))
+        m3 = after(m3, cot_all)
+        mo.append(core_move(m3))
     else:
+        ctx_all = gather(context)
+        m3 = plane_move(m2, 1)
+        cot_all = gather(cotangent[0])
         mo = from_planes(middle_pack(1))
+    ms = (m_pack, m1, m2, m3)
 
     FH = F0 // 2
     outs = call(
@@ -814,9 +853,8 @@
         + (shape((T, D), bf16),) * 3
         + (shape((4 * T, CG), bf16),) * 4
         + (shape((4 * T, D), f32),)
-        + (shape((4 * T, D), bf16),) * 4
-        + (shape((4, T, D), bf16), shape((1, D), f32)),
-        [ids, x_all, ctx_all, gains] + list(cots) + list(ms) + mo,
+        + (shape((4 * T, D), bf16),) * 4,
+        [ids, x_all, ctx_all, gains, cot_all] + list(ms) + mo,
         scratch=[
             pltpu.VMEM((4, 2, R0, D // 2), bf16),
             pltpu.VMEM((2, 4, R0, FH), bf16),
@@ -827,7 +865,7 @@
         us=10,
     )
     res0, res_send, gcs = outs[0], outs[1:4], outs[4:8]
-    grads, normed_ffn, active, ginner, branch, cot_all, second_gain = outs[8:15]
+    grads, normed_ffn, active, ginner, branch = outs[8:13]
     got = [gcs[0]] + [group_move(gcs[k], k) for k in (1, 2, 3)]
     R = D // 8
     keep, send = call(
@@ -851,8 +889,15 @@
             [ids, keep, core_move(send)],
             scratch=[pltpu.VMEM((4, 4, RR, D), f32)],
         )
-        middle_more = plane_move(far, 1)
-        got = list(after(tuple(got), far, p1))
+        middle_more = plane_move(far, 2)
+        first_rows, second_rows = call(
+            rows_kernel,
+            (shape((R, 3 * CG), f32), shape((R, D), f32)),
+            [ids] + ws + list(ms) + mo,
+            scratch=[pltpu.VMEM((4, R, 3 * CG), f32), pltpu.VMEM((4, 2, R0, F0 // 2), f32)],
+            us=1,
+        )
+        got = list(after(tuple(got), far, p1, second_rows))
         ps = [group_move(p, k) for k, p in ((1, p1), (2, p2), (3, p3))]
     if fast:
         back_outs = (
@@ -881,15 +926,6 @@
     if fast:
         dq, down, doth, sums = back
         doth = after(doth, *ps)
-        middle_send, middle_mine = call(
-            middle_half_kernel,
-            (shape((2 * R + 16, D), bf16), shape((2 * R, D), f32)),
-            [near, middle_more],
-            scalars=0,
-            us=1,
-        )
-        middle_last = plane_move(middle_send, 2)
-        doth = after(doth, middle_send)
         dmore = core_move(doth)
         keep_p, send_p = call(
             functools.partial(project_grad_kernel, T),
@@ -904,19 +940,12 @@
         down = lax.psum_scatter(dall, "seq", scatter_dimension=0, axis_index_groups=members)
         down, dmore = down.astype(bf16), jnp.zeros((HG, 4 * T, 128), bf16)
 
-    own, s1, s2, s3, joined, first_gain = call(
-        functools.partial(tail_kernel, T),
-        (shape((T, D), f32),)
-        + (shape((2 * T, D), bf16),) * 3
-        + (shape((4 * T, 3 * CG), bf16), shape((1, D), f32)),
-        [ids, x_all, dq, down, dmore, grads, gains] + ws + wo + list(res_send),
-        scratch=[pltpu.VMEM((4, 2, RH, 3 * CG), bf16), pltpu.VMEM((4, T, D), f32)],
-    )
     table_row = call(functools.partial(table_kernel, T), shape((1, 32 * H), f32), [ids, sums])
     small = shape((8, 3 * CG), f32), shape((16, 3 * CG), bf16)
-    extra, extra_send = call(extra_kernel, small, [second_gain, first_gain, table_row], scalars=0, us=1)
+    extra, extra_send = call(extra_kernel, small, [table_row], scalars=0, us=1)
     if fast:
         RB = R + RR * D // (3 * CG)
+        extra, middle_more = after((extra, middle_more), middle_more)
         project_far, project_near, extra = call(
             project_join_kernel,
             (shape((2 * RB + 16, 3 * CG), bf16),)
@@ -925,10 +954,30 @@
             scratch=[pltpu.VMEM((4, 4, RR, 3 * CG), f32), pltpu.VMEM((4, RR, D), f32)],
             us=1,
         )
+        dmore = after(dmore, project_far)
+    own, s1, s2, s3, joined = call(
+        functools.partial(tail_kernel, T),
+        (shape((T, D), f32),)
+        + (shape((2 * T, D), bf16),) * 3
+        + (shape((4 * T, 3 * CG), bf16),),
+        [ids, x_all, dq, down, dmore, grads, gains] + ws + wo + list(res_send),
+        scratch=[pltpu.VMEM((4, 2, RH, 3 * CG), bf16), pltpu.VMEM((4, T, D), f32)],
+    )
+    if fast:
+        middle_send, middle_mine = call(
+            middle_half_kernel,
+            (shape((2 * R, D), bf16), shape((2 * R, D), f32)),
+            [near, middle_more],
+            scalars=0,
+            us=1,
+        )
+        project_more = plane_move(project_far, 1)
+        middle_send = after(middle_send, project_more)
+        middle_last = plane_move(middle_send, 1)
         send, mine, extra = call(
             project_half_kernel,
             (shape((RB + 16, 3 * CG), bf16), shape((RB, 3 * CG), f32), shape((8, 3 * CG), f32)),
-            [after(project_near, middle_last), plane_move(project_far, 1), extra],
+            [after(project_near, middle_send), project_more, extra],
             scalars=0,
             us=1,
         )
@@ -938,10 +987,10 @@
     input_gradient = own + parts[0][:T].astype(f32) + parts[1][:T].astype(f32) + parts[2][:T].astype(f32)
     result = res0 + parts[0][T:].astype(f32) + parts[1][T:].astype(f32) + parts[2][T:].astype(f32)
     if fast:
-        inner_mine, outer_mine = call(
+        inner_mine, outer_mine, second_sums = call(
             middle_sum_kernel,
-            (shape((R, D), f32), shape((R, D), bf16)),
-            [middle_mine, middle_last],
+            (shape((R, D), f32), shape((R, D), bf16), shape((R, 1), f32)),
+            [middle_mine, middle_last, second_rows],
             scalars=0,
             us=1,
         )
@@ -951,13 +1000,17 @@
                 for z in range(fsdps):
                     pairs.append(((a * C + b) * fsdps + z, ((a ^ z) * C + b) * fsdps + z))
         outer_got = lax.ppermute(outer_mine, ("seq", "fsdp"), pairs)
-        wide = 3 * CG + D
+        wide = 3 * CG + D + 128
         t1, t2, t3, tmine, extra, output_grad = call(
             project_plane_kernel,
             (shape((RR + 8, wide), bf16),) * 3
             + (shape((RR, wide), f32), shape((8, 3 * CG), f32), shape((RR, D), f32)),
-            [ids, mine, more, extra, inner_mine],
-            scratch=[pltpu.VMEM((4, RR, 3 * CG), f32), pltpu.VMEM((4, RR, D), f32)],
+            [ids, mine, more, extra, inner_mine, second_sums, first_rows],
+            scratch=[
+                pltpu.VMEM((4, RR, 3 * CG), f32),
+                pltpu.VMEM((4, RR, D), f32),
+                pltpu.VMEM((4, RR, 128), f32),
+            ],
             us=1,
         )
         ts = [group_move(t, k) for k, t in ((1, t1), (2, t2), (3, t3))]
@@ -968,7 +1021,7 @@
             (shape((RR, D), f32),) * 3
             + (shape((RR, 4 * F0), f32), shape((1, count), f32), shape((1, count), f32), shape((H, 32), f32))
             + (shape((R, D), f32),),
-            [where, tmine] + ts + [extra, outer_got],
+            [where, tmine] + ts + [extra, outer_got, gains],
             scratch=[pltpu.VMEM((4, RR, wide), f32), pltpu.VMEM((D // count, count), f32)],
             us=1,
         )
@@ -989,7 +1042,8 @@
                     blocks += [block * (b == (z ^ g)).astype(f32) for b in range(4)]
             return jnp.concatenate(blocks, axis=axis)
 
-        inner_w = spread(product(normed_ffn, ginner), 1)
+        inner_p = product(normed_ffn, ginner)
+        inner_w = spread(inner_p, 1)
         outer_w = spread(product(active, cot_all.reshape(4 * T, D)), 0)
         out_w = jnp.zeros((4, CG, D), f32)
         for k in range(4):
@@ -1010,13 +1064,22 @@
         inner_grad = scatter(inner_w)
         outer_grad = scatter(outer_w)
         extra = lax.psum(extra, axes)
+        order = f ^ jnp.arange(4)
+
+        def by_plane(slots, low, high):
+            return jnp.stack([v[low:high] for v in slots])[order].astype(f32)
+
+        pair = jnp.stack([by_plane(ws, 0, RH), by_plane(wo, 0, RH)], axis=1).reshape(D, 3 * CG)
+        first_vec = jnp.sum(pair * joined_w, axis=1)
+        wide = jnp.concatenate([by_plane(v, R0, 2 * R0).reshape(D, F0 // 2) for v in (ms, mo)], axis=1)
+        second_vec = jnp.sum(wide * inner_p, axis=1)
+        first_vec = lax.psum(first_vec, axes) / gains[0]
+        second_vec = lax.psum(second_vec, axes) / gains[1]
         at = position * fsdps + f
         count = D // (seqs * fsdps)
-        second_vec = jnp.concatenate([extra[0, : D // 2], extra[1, : D // 2]])
-        first_vec = jnp.concatenate([extra[2, : D // 2], extra[3, : D // 2]])
         second_grad = lax.dynamic_slice_in_dim(second_vec, at * count, count)
         first_grad = lax.dynamic_slice_in_dim(first_vec, at * count, count)
-        table_grad = extra[4, : 32 * H].reshape(H, 32).T
+        table_grad = extra[0, : 32 * H].reshape(H, 32).T
     return (
         result[None],
         input_gradient[None],

time: 158 us -> 151 us (0.956)
  waiting for transfers between devices: 46.8 us -> 34.8 us
  blocking collectives: 25.6 us -> 37.4 us
  starting transfers between devices: 37 us -> 28.8 us
    all_gather x2 -> x3, blocking collectives: 25.6 us -> 37.4 us  [gather(): return lax.all_gather(value, 'seq', axis=0, axis_index_groups=token_groups)]
    ppermute x10, waiting for transfers between devices: 27.4 us -> 19.4 us  [plane_move(): return lax.ppermute(value, 'fsdp', [(i, i ^ k) for i in range(fsdps)])]
    ppermute x10, starting transfers between devices: 15.9 us -> 11.4 us  [plane_move(): return lax.ppermute(value, 'fsdp', [(i, i ^ k) for i in range(fsdps)])]
    ppermute x15 -> x12, waiting for transfers between devices: 13.3 us -> 9.23 us  [group_move(): return lax.ppermute(value, 'seq', pairs)]
    ppermute x15 -> x12, starting transfers between devices: 17.7 us -> 14.1 us  [group_move(): return lax.ppermute(value, 'seq', pairs)]
    pallas_call x19 -> x20, Pallas kernels: 44 us -> 44.9 us  [call(): pl.pallas_call(kernel, out_shape=outs, in_specs=[smem] * scalars + [hbm i...]
  transfers between devices with their start and end apart: 39 -> 36, of which waited for: 18 -> 12; matrix products, arithmetic and copies ran while one was open for 2% -> 2% of each run, Pallas kernels for 17% -> 20%
where the time goes in v3:
time: 151 us; the launch traced here: 150 us
  Pallas kernels  44.9 us (30%)
  blocking collectives  37.4 us (25%)
  waiting for transfers between devices  34.8 us (23%)
  starting transfers between devices  28.8 us (19%)
  other arithmetic  2.6 us (2%)
    pallas_call x20, Pallas kernels, call(): pl.pallas_call(kernel, out_shape=outs, in_specs=[smem] * scalars + [hbm i...  44.9 us
    all_gather x3, blocking collectives, gather(): return lax.all_gather(value, 'seq', axis=0, axis_index_groups=token_groups)  37.4 us
    ppermute x10, waiting for transfers between devices, plane_move(): return lax.ppermute(value, 'fsdp', [(i, i ^ k) for i in range(fsdps)])  19.4 us
    ppermute x12, starting transfers between devices, group_move(): return lax.ppermute(value, 'seq', pairs)  14.1 us
    ppermute x10, starting transfers between devices, plane_move(): return lax.ppermute(value, 'fsdp', [(i, i ^ k) for i in range(fsdps)])  11.4 us
    ppermute x12, waiting for transfers between devices, group_move(): return lax.ppermute(value, 'seq', pairs)  9.23 us
    ppermute x13, waiting for transfers between devices, core_move(): return lax.ppermute(value, 'seq', [(i, i ^ 1) for i in range(seqs)])  6.23 us
  transfers between devices with their start and end apart: 36, of which 12 were waited for; matrix products, arithmetic and copies ran while one was open for 2% of the time, Pallas kernels for 20%

profile of v3, /device:TPU:0, one launch (start us, length us, event | category | flops | bytes accessed | tf_op | source)
XLA Modules:
  0.0 150.4 jit_solution(11351815523696533286)
XLA Ops:
  0.6 2.0 %shard_map.203 = (bf16[112,576]{1,0:T(8,128)(2,1)}, bf16[144,768]{1,0:T(8,128)(2,1)}) custom-call(bf16[192,768]{1,0:T(8,128)(2,1)} %q.1, bf16[192,768]{1,0:T(8,128)(2,1)} %k.1, bf16[192,768]{1,0:T(8,128)(2,1)} %v.1, bf16[192]{0:T(256)(128)(2,1)} %first.1, bf16[192]{0:T(256)(128)(2,1)} %second.1, bf16[8,12]{1,0:T(8,128)(2,1)} %table.1, ...), custom_call_target="tpu_custom_call" | custom-call | flops 1000000 | bytes 1024 | tf_op jit(solution)/shard_map/pallas_call | solution.py:48
  2.7 5.1 %collective-permute-start.2 = (bf16[112,576]{1,0:T(8,128)(2,1)}, bf16[112,576]{1,0:T(8,128)(2,1)S(1)}, u32[]{:S(2)}, u32[]{:S(2)}) collective-permute-start(bf16[112,576]{1,0:T(8,128)(2,1)} %get-tuple-element.111.refs_0_), channel_id=1, source_target_pairs={{0,3},{1,2},{2,1},{3,0},{4,7},{5,6},{6,5},{7,4},{8,11},{9,10},{10,... | collective-permute-start | bytes 387080 | tf_op jit(solution)/shard_map/ppermute | solution.py:704
  8.4 2.1 %shard_map.204.refs_4_ = bf16[576,384]{1,0:T(8,128)(2,1)} custom-call(bf16[192,768]{1,0:T(8,128)(2,1)} %wo, bf16[192,3072]{1,0:T(8,128)(2,1)} %inner, bf16[768,768]{1,0:T(8,128)(2,1)} %outer), custom_call_target="tpu_custom_call" | custom-call | flops 1000000 | bytes 1024 | tf_op jit(solution)/shard_map/pallas_call | solution.py:48
  10.5 12.1 %all-gather = bf16[576,768]{1,0:T(8,128)(2,1)S(1)} all-gather(bf16[144,768]{1,0:T(8,128)(2,1)S(1)} %copy-done.8), channel_id=2, replica_groups={{0,8,16,24},{4,12,20,28},{1,9,17,25},{5,13,21,29},{2,10,18,26},{6,14,22..., dimensions={0}, use_global_device_ids=true | all-gather | bytes 1105920 | tf_op jit(solution)/shard_map/all_gather | solution.py:777
  25.1 2.2 %collective-permute-start.10 = (bf16[576,384]{1,0:T(8,128)(2,1)}, bf16[576,384]{1,0:T(8,128)(2,1)S(1)}, u32[]{:S(2)}, u32[]{:S(2)}) collective-permute-start(bf16[576,384]{1,0:T(8,128)(2,1)} %shard_map.204.refs_4_), channel_id=1, source_target_pairs={{0,2},{1,3},{2,0},{3,1},{4,6},{5,7},{6,4},{7,5},{8,10},{9,11},{10,... | collective-permute-start | bytes 1327112 | tf_op jit(solution)/shard_map/ppermute | solution.py:704
  27.3 2.0 %collective-permute-start.9 = (bf16[576,384]{1,0:T(8,128)(2,1)}, bf16[576,384]{1,0:T(8,128)(2,1)S(1)}, u32[]{:S(2)}, u32[]{:S(2)}) collective-permute-start(bf16[576,384]{1,0:T(8,128)(2,1)} %shard_map.204.refs_4_), channel_id=1, source_target_pairs={{0,1},{1,0},{2,3},{3,2},{4,5},{5,4},{6,7},{7,6},{8,9},{9,8},{10,11... | collective-permute-start | bytes 1327112 | tf_op jit(solution)/shard_map/ppermute | solution.py:704
  30.7 2.8 %shard_map.205 = (bf16[1024,768]{1,0:T(8,128)(2,1)S(1)}, bf16[3,1024,128]{2,1,0:T(8,128)(2,1)S(1)}, bf16[3,512,128]{2,1,0:T(8,128)(2,1)S(1)}, f32[8,128]{1,0:T(8...) custom-call(s32[4]{0:T(128)S(1)} %pad_add_fusion.ids, bf16[112,576]{1,0:T(8,128)(2,1)S(1)} %copy-done.1, ...), custom_call_target="tpu_custom_call" | custom-call | flops 1000000 | bytes 1024 | tf_op jit(solution)/shard_map/pallas_call | solution.py:48
  34.7 5.4 %shard_map.207 = (bf16[512,192]{1,0:T(8,128)(2,1)S(1)}, f32[2,8,256]{2,1,0:T(8,128)S(1)}) custom-call(s32[4]{0:T(128)S(1)} %pad_add_fusion.ids, s32[4]{0:T(128)S(1)} %get-tuple-element.202.q_at, s32[8]{0:T(128)S(1)} %pad_add_fusion.1.k_at, bf16[3,512,128]{2,1,0:T(8,128)(2,1)S(1)} %get-tuple-element.113.query, f32[8,128]{1,0:T(8,128)S(1)} %get-tuple-element.114.seg_q.seg_k, ...), custom_call_target="tpu_custom_call" | custom-call | flops 1000000 | bytes 1024 | tf_op jit(solution)/shard_map/pallas_call | solution.py:48
  40.1 14.5 %all-gather.1 = bf16[2048,192]{1,0:T(8,128)(2,1)S(1)} all-gather(bf16[512,192]{1,0:T(8,128)(2,1)S(1)} %get-tuple-element.118), channel_id=3, replica_groups={{0,8,16,24},{4,12,20,28},{1,9,17,25},{5,13,21,29},{2,10,18,26},{6,14,22..., dimensions={0}, use_global_device_ids=true | all-gather | bytes 983040 | tf_op jit(solution)/shard_map/all_gather | solution.py:777
  57.2 10.8 %all-gather.2 = bf16[512,768]{1,0:T(8,128)(2,1)S(1)} all-gather(bf16[128,768]{1,0:T(8,128)(2,1)S(1)} %bitcast.23), channel_id=4, replica_groups={{0,8,16,24},{4,12,20,28},{1,9,17,25},{5,13,21,29},{2,10,18,26},{6,14,22..., dimensions={0}, use_global_device_ids=true | all-gather | bytes 983040 | tf_op jit(solution)/shard_map/all_gather | solution.py:777
  68.1 1.8 %collective-permute-done.14.refs_11_ = bf16[576,384]{1,0:T(8,128)(2,1)S(1)} collective-permute-done((bf16[576,384]{1,0:T(8,128)(2,1)S(1)}, bf16[576,384]{1,0:T(8,128)(2,1)S(1)}, u32[]{:S(2)}, u32[]{:S(2)}) %collective-permute-start.14) | collective-permute-done | bytes 442400 | tf_op jit(solution)/shard_map/ppermute | solution.py:707
  69.8 8.1 %shard_map.208 = (f32[128,768]{1,0:T(8,128)S(1)}, bf16[128,768]{1,0:T(8,128)(2,1)S(1)}, bf16[128,768]{1,0:T(8,128)(2,1)S(1)}, bf16[128,768]{1,0:T(8,128)(2,1)S(1...) custom-call(s32[4]{0:T(128)S(1)} %pad_add_fusion.ids, ...), custom_call_target="tpu_custom_call" | custom-call | flops 10000000 | bytes 1024 | tf_op jit(solution)/shard_map/pallas_call | solution.py:48
  78.7 3.0 %shard_map.209 = (f32[3,4,96,768]{3,2,1,0:T(8,128)S(1)}, bf16[3,4,96,768]{3,2,1,0:T(8,128)(2,1)S(1)}) custom-call(s32[4]{0:T(128)S(1)} %pad_add_fusion.ids, bf16[512,768]{1,0:T(8,128)(2,1)S(1)} %get-tuple-element.130.normed, bf16[512,768]{1,0:T(8,128)(2,1)S(1)} %get-tuple-element.131.active, bf16[512,768]{1,0:T(8,128)(2,1)S(1)} %get-tuple-element.132.ginner, ...), custom_call_target="tpu_custom_call" | custom-call | flops 5000000 | bytes 1024 | tf_op jit(solution)/shard_map/pallas_call | solution.py:48
  81.9 1.8 %collective-permute-start.15 = (bf16[512,192]{1,0:T(8,128)(2,1)S(1)}, bf16[512,192]{1,0:T(8,128)(2,1)S(1)}, u32[]{:S(2)}, u32[]{:S(2)}) collective-permute-start(bf16[512,192]{1,0:T(8,128)(2,1)S(1)} %get-tuple-element.127), channel_id=1, source_target_pairs={{0,8},{4,12},{8,0},{12,4},{16,24},{20,28},{24,16},{28,20},{1,9},{5... | collective-permute-start | bytes 589832 | tf_op jit(solution)/shard_map/ppermute | solution.py:701
  83.9 1.4 collective-permute-start.17
  87.3 1.8 %collective-permute-start.19 = (bf16[96,768]{1,0:T(8,128)(2,1)S(1)}, bf16[96,768]{1,0:T(8,128)(2,1)S(1)}, u32[]{:S(2)}, u32[]{:S(2)}) collective-permute-start(bf16[96,768]{1,0:T(8,128)(2,1)S(1)} %get-tuple-element.137), channel_id=1, source_target_pairs={{0,8},{4,12},{8,0},{12,4},{16,24},{20,28},{24,16},{28,20},{1,9},{5... | collective-permute-start | bytes 442376 | tf_op jit(solution)/shard_map/ppermute | solution.py:701
  89.6 1.4 collective-permute-done.15.g1
  91.0 6.2 %collective-permute-done.16.g2 = bf16[512,192]{1,0:T(8,128)(2,1)S(1)} collective-permute-done((bf16[512,192]{1,0:T(8,128)(2,1)S(1)}, bf16[512,192]{1,0:T(8,128)(2,1)S(1)}, u32[]{:S(2)}, u32[]{:S(2)}) %collective-permute-start.16) | collective-permute-done | bytes 196640 | tf_op jit(solution)/shard_map/ppermute | solution.py:701
  98.1 1.5 collective-permute-start.21
  99.6 7.6 %shard_map.212 = (bf16[512,192]{1,0:T(8,128)(2,1)S(1)}, bf16[3,512,128]{2,1,0:T(8,128)(2,1)S(1)}, bf16[3,512,128]{2,1,0:T(8,128)(2,1)S(1)}, f32[3,5,128,128]{3,2,1,0:T(8,128)S(1)}) custom-call(s32[4]{0:T(128)S(1)} %pad_add_fusion.ids, s32[4]{0:T(128)S(1)} %get-tuple-element.202.q_at, s32[8]{0:T(128)S(1)} %pad_add_fusion.1.k_at, ...), custom_call_target="tpu_custom_call" | custom-call | flops 30000001024 | bytes 1024 | tf_op jit(solution)/shard_map/pallas_call | solution.py:48
  107.3 1.9 %shard_map.213 = (f32[4,96,576]{2,1,0:T(8,128)S(1)}, bf16[384,576]{1,0:T(8,128)(2,1)S(1)}) custom-call(s32[4]{0:T(128)S(1)} %pad_add_fusion.ids, bf16[1024,768]{1,0:T(8,128)(2,1)S(1)} %get-tuple-element.149.normed, bf16[512,192]{1,0:T(8,128)(2,1)S(1)} %get-tuple-element.143.dq, bf16[3,512,128]{2,1,0:T(8,128)(2,1)S(1)} %get-tuple-element.144.down, ...), custom_call_target="tpu_custom_call" | custom-call | flops 2000000 | bytes 1024 | tf_op jit(solution)/shard_map/pallas_call | solution.py:48
  109.8 1.7 %shard_map.214.table = f32[1,384]{1,0:T(1,128)S(1)} custom-call(s32[4]{0:T(128)S(1)} %pad_add_fusion.ids, f32[3,5,128,128]{3,2,1,0:T(8,128)S(1)} %get-tuple-element.152.sums), custom_call_target="tpu_custom_call" | custom-call | flops 2000000 | bytes 1024 | tf_op jit(solution)/shard_map/pallas_call | solution.py:48
  111.6 4.9 %collective-permute-done.24.more = bf16[384,768]{1,0:T(8,128)(2,1)S(1)} collective-permute-done((bf16[384,768]{1,0:T(8,128)(2,1)S(1)}, bf16[384,768]{1,0:T(8,128)(2,1)S(1)}, u32[]{:S(2)}, u32[]{:S(2)}) %collective-permute-start.24) | collective-permute-done | bytes 589856 | tf_op jit(solution)/shard_map/ppermute | solution.py:704
  117.5 3.1 %shard_map.217 = (f32[128,768]{1,0:T(8,128)S(1)}, bf16[256,768]{1,0:T(8,128)(2,1)}, bf16[256,768]{1,0:T(8,128)(2,1)}, bf16[256,768]{1,0:T(8,128)(2,1)}, bf16[512,576]{1,0:T(8,128)(2,1)}) custom-call(s32[4]{0:T(128)S(1)} %pad_add_fusion.ids, bf16[4,144,768]{2,1,0:T(8,128)(2,1)S(1)} %bitcast.18, bf16[512,192]{1,0:T(8,128)(2,1)S(1)} %get-tuple-element.143.dq, ...), custom_call_target="tpu_custom_call" | custom-call | flops 2000000 | bytes 1024 | tf_op jit(solution)/shard_map/pallas_call | solution.py:48
  120.9 1.7 %collective-permute-start.27 = (bf16[256,768]{1,0:T(8,128)(2,1)}, bf16[256,768]{1,0:T(8,128)(2,1)}, u32[]{:S(2)}, u32[]{:S(2)}) collective-permute-start(bf16[256,768]{1,0:T(8,128)(2,1)} %get-tuple-element.167), channel_id=1, source_target_pairs={{0,16},{4,20},{8,24},{12,28},{16,0},{20,4},{24,8},{28,12},{1,17},{... | collective-permute-start | bytes 1179656 | tf_op jit(solution)/shard_map/ppermute | solution.py:701
  122.6 1.5 collective-permute-start.28
  124.2 3.3 %collective-permute-done.29.more = bf16[272,576]{1,0:T(8,128)(2,1)S(1)} collective-permute-done((bf16[272,576]{1,0:T(8,128)(2,1)S(1)}, bf16[272,576]{1,0:T(8,128)(2,1)S(1)}, u32[]{:S(2)}, u32[]{:S(2)}) %collective-permute-start.29) | collective-permute-done | bytes 313376 | tf_op jit(solution)/shard_map/ppermute | solution.py:704
  128.5 11.2 %collective-permute-done.31.more = bf16[192,768]{1,0:T(8,128)(2,1)S(1)} collective-permute-done((bf16[192,768]{1,0:T(8,128)(2,1)S(1)}, bf16[192,768]{1,0:T(8,128)(2,1)S(1)}, u32[]{:S(2)}, u32[]{:S(2)}) %collective-permute-start.31) | collective-permute-done | bytes 294944 | tf_op jit(solution)/shard_map/ppermute | solution.py:704
  141.5 1.7 %collective-permute-start.33 = (bf16[32,1472]{1,0:T(8,128)(2,1)S(1)}, bf16[32,1472]{1,0:T(8,128)(2,1)S(1)}, u32[]{:S(2)}, u32[]{:S(2)}) collective-permute-start(bf16[32,1472]{1,0:T(8,128)(2,1)S(1)} %get-tuple-element.186), channel_id=1, source_target_pairs={{0,16},{4,20},{8,24},{12,28},{16,0},{20,4},{24,8},{28,12},{1,17},{... | collective-permute-start | bytes 282632 | tf_op jit(solution)/shard_map/ppermute | solution.py:701
  143.2 1.5 collective-permute-start.34
  145.3 2.4 %add_bitcast_fusion = (f32[1,128,768]{2,1,0:T(8,128)}, f32[1,128,768]{2,1,0:T(8,128)}) fusion(f32[128,768]{1,0:T(8,128)S(1)} %get-tuple-element.169, bf16[256,768]{1,0:T(8,128)(2,1)} %collective-permute-done.28, bf16[256,768]{1,0:T(8,128)(2,1)} %collective-permute-done.27, bf16[256,768]{1,0:T(8,128)(2,1)} %collective-permute-done.26, f32[128,768]{1,0:T(8,128)S(1)} %copy-done.3), kind=kLoop, calls=%fused_computation | loop fusion | flops 1179648 | bytes 2752512 | tf_op jit(solution)/shard_map/broadcast_in_dim | solution.py:1085
  148.7 1.8 %shard_map.222 = (f32[24,768]{1,0:T(8,128)}, f32[24,768]{1,0:T(8,128)}, f32[24,768]{1,0:T(8,128)}, f32[24,3072]{1,0:T(8,128)}, f32[1,24]{1,0:T(1,128)}, /*index=...) custom-call(s32[2]{0:T(128)S(1)} %pad_add_fusion.2.where, f32[24,1472]{1,0:T(8,128)S(1)} %get-tuple-element.184.own, ...), custom_call_target="tpu_custom_call" | custom-call | flops 1000000 | bytes 1024 | tf_op jit(solution)/shard_map/pallas_call | solution.py:48
  (88 shorter events, 19.5 us)
Async XLA Ops:
  2.7 19.9 %collective-permute-start.2 = (bf16[112,576]{1,0:T(8,128)(2,1)}, bf16[112,576]{1,0:T(8,128)(2,1)S(1)}, u32[]{:S(2)}, u32[]{:S(2)}) collective-permute-start(bf16[112,576]{1,0:T(8,128)(2,1)} %get-tuple-element.111.refs_0_), channel_id=1, source_target_pairs={{0,3},{1,2},{2,1},{3,0},{4,7},{5,6},{6,5},{7,4},{8,11},{9,10},{10,... | collective-permute-start | bytes 387080 | tf_op jit(solution)/shard_map/ppermute | solution.py:704
  7.8 14.8 %collective-permute-start.1 = (bf16[112,576]{1,0:T(8,128)(2,1)}, bf16[112,576]{1,0:T(8,128)(2,1)S(1)}, u32[]{:S(2)}, u32[]{:S(2)}) collective-permute-start(bf16[112,576]{1,0:T(8,128)(2,1)} %get-tuple-element.111.refs_0_), channel_id=1, source_target_pairs={{0,2},{1,3},{2,0},{3,1},{4,6},{5,7},{6,4},{7,5},{8,10},{9,11},{10,... | collective-permute-start | bytes 387080 | tf_op jit(solution)/shard_map/ppermute | solution.py:704
  7.8 14.8 %collective-permute-start = (bf16[112,576]{1,0:T(8,128)(2,1)}, bf16[112,576]{1,0:T(8,128)(2,1)S(1)}, u32[]{:S(2)}, u32[]{:S(2)}) collective-permute-start(bf16[112,576]{1,0:T(8,128)(2,1)} %get-tuple-element.111.refs_0_), channel_id=1, source_target_pairs={{0,1},{1,0},{2,3},{3,2},{4,5},{5,4},{6,7},{7,6},{8,9},{9,8},{10,11... | collective-permute-start | bytes 387080 | tf_op jit(solution)/shard_map/ppermute | solution.py:704
  22.6 8.1 %collective-permute-start.7 = (bf16[4,144,768]{2,1,0:T(8,128)(2,1)S(1)}, bf16[4,144,768]{2,1,0:T(8,128)(2,1)}, u32[]{:S(2)}, u32[]{:S(2)}) collective-permute-start(bf16[4,144,768]{2,1,0:T(8,128)(2,1)S(1)} %bitcast.15), channel_id=1, source_target_pairs={{0,4},{4,0},{8,12},{12,8},{16,20},{20,16},{24,28},{28,24},{1,5},{5... | collective-permute-start | bytes 2654216 | tf_op jit(solution)/shard_map/ppermute | solution.py:707
  22.7 2.4 %collective-permute-start.3 = (bf16[112,576]{1,0:T(8,128)(2,1)S(1)}, bf16[112,576]{1,0:T(8,128)(2,1)S(1)}, u32[]{:S(2)}, u32[]{:S(2)}) collective-permute-start(bf16[112,576]{1,0:T(8,128)(2,1)S(1)} %copy-done.1), channel_id=1, source_target_pairs={{0,4},{4,0},{8,12},{12,8},{16,20},{20,16},{24,28},{28,24},{1,5},{5... | collective-permute-start | bytes 387080 | tf_op jit(solution)/shard_map/ppermute | solution.py:707
  23.2 4.1 %collective-permute-start.6 = (bf16[112,576]{1,0:T(8,128)(2,1)S(1)}, bf16[112,576]{1,0:T(8,128)(2,1)S(1)}, u32[]{:S(2)}, u32[]{:S(2)}) collective-permute-start(bf16[112,576]{1,0:T(8,128)(2,1)S(1)} %collective-permute-done.2.refs_3_), channel_id=1, source_target_pairs={{0,4},{4,0},{8,12},{12,8},{16,20},{20,16},{24,28},{28,24},{1,5},{5... | collective-permute-start | bytes 387080 | tf_op jit(solution)/shard_map/ppermute | solution.py:707
  23.3 16.8 %collective-permute-start.8 = (bf16[576,384]{1,0:T(8,128)(2,1)}, bf16[576,384]{1,0:T(8,128)(2,1)S(1)}, u32[]{:S(2)}, u32[]{:S(2)}) collective-permute-start(bf16[576,384]{1,0:T(8,128)(2,1)} %shard_map.204.refs_4_), channel_id=1, source_target_pairs={{0,4},{4,0},{8,12},{12,8},{16,20},{20,16},{24,28},{28,24},{1,5},{5... | collective-permute-start | bytes 1327112 | tf_op jit(solution)/shard_map/ppermute | solution.py:707
  23.7 5.6 %collective-permute-start.5 = (bf16[112,576]{1,0:T(8,128)(2,1)S(1)}, bf16[112,576]{1,0:T(8,128)(2,1)S(1)}, u32[]{:S(2)}, u32[]{:S(2)}) collective-permute-start(bf16[112,576]{1,0:T(8,128)(2,1)S(1)} %collective-permute-done.1.refs_2_), channel_id=1, source_target_pairs={{0,4},{4,0},{8,12},{12,8},{16,20},{20,16},{24,28},{28,24},{1,5},{5... | collective-permute-start | bytes 387080 | tf_op jit(solution)/shard_map/ppermute | solution.py:707
  25.1 29.5 %collective-permute-start.10 = (bf16[576,384]{1,0:T(8,128)(2,1)}, bf16[576,384]{1,0:T(8,128)(2,1)S(1)}, u32[]{:S(2)}, u32[]{:S(2)}) collective-permute-start(bf16[576,384]{1,0:T(8,128)(2,1)} %shard_map.204.refs_4_), channel_id=1, source_target_pairs={{0,2},{1,3},{2,0},{3,1},{4,6},{5,7},{6,4},{7,5},{8,10},{9,11},{10,... | collective-permute-start | bytes 1327112 | tf_op jit(solution)/shard_map/ppermute | solution.py:704
  27.3 27.4 %collective-permute-start.9 = (bf16[576,384]{1,0:T(8,128)(2,1)}, bf16[576,384]{1,0:T(8,128)(2,1)S(1)}, u32[]{:S(2)}, u32[]{:S(2)}) collective-permute-start(bf16[576,384]{1,0:T(8,128)(2,1)} %shard_map.204.refs_4_), channel_id=1, source_target_pairs={{0,1},{1,0},{2,3},{3,2},{4,5},{5,4},{6,7},{7,6},{8,9},{9,8},{10,11... | collective-permute-start | bytes 1327112 | tf_op jit(solution)/shard_map/ppermute | solution.py:704
  55.3 12.7 %collective-permute-start.13 = (bf16[576,384]{1,0:T(8,128)(2,1)S(1)}, bf16[576,384]{1,0:T(8,128)(2,1)S(1)}, u32[]{:S(2)}, u32[]{:S(2)}) collective-permute-start(bf16[576,384]{1,0:T(8,128)(2,1)S(1)} %collective-permute-done.10.refs_6_), channel_id=1, source_target_pairs={{0,1},{1,0},{2,3},{3,2},{4,5},{5,4},{6,7},{7,6},{8,9},{9,8},{10,11... | collective-permute-start | bytes 1327112 | tf_op jit(solution)/shard_map/ppermute | solution.py:704
  81.7 4.5 %collective-permute-start.18 = (bf16[3,4,96,768]{3,2,1,0:T(8,128)(2,1)S(1)}, bf16[3,4,96,768]{3,2,1,0:T(8,128)(2,1)S(1)}, u32[]{:S(2)}, u32[]{:S(2)}) collective-permute-start(bf16[3,4,96,768]{3,2,1,0:T(8,128)(2,1)S(1)} %get-tuple-element.135), channel_id=1, source_target_pairs={{0,4},{4,0},{8,12},{12,8},{16,20},{20,16},{24,28},{28,24},{1,5},{5... | collective-permute-start | bytes 5308424 | tf_op jit(solution)/shard_map/ppermute | solution.py:707
  81.9 9.1 %collective-permute-start.15 = (bf16[512,192]{1,0:T(8,128)(2,1)S(1)}, bf16[512,192]{1,0:T(8,128)(2,1)S(1)}, u32[]{:S(2)}, u32[]{:S(2)}) collective-permute-start(bf16[512,192]{1,0:T(8,128)(2,1)S(1)} %get-tuple-element.127), channel_id=1, source_target_pairs={{0,8},{4,12},{8,0},{12,4},{16,24},{20,28},{24,16},{28,20},{1,9},{5... | collective-permute-start | bytes 589832 | tf_op jit(solution)/shard_map/ppermute | solution.py:701
  83.7 13.6 %collective-permute-start.16 = (bf16[512,192]{1,0:T(8,128)(2,1)S(1)}, bf16[512,192]{1,0:T(8,128)(2,1)S(1)}, u32[]{:S(2)}, u32[]{:S(2)}) collective-permute-start(bf16[512,192]{1,0:T(8,128)(2,1)S(1)} %get-tuple-element.128), channel_id=1, source_target_pairs={{0,16},{4,20},{8,24},{12,28},{16,0},{20,4},{24,8},{28,12},{1,17},{... | collective-permute-start | bytes 589832 | tf_op jit(solution)/shard_map/ppermute | solution.py:701
  83.9 13.9 %collective-permute-start.17 = (bf16[512,192]{1,0:T(8,128)(2,1)S(1)}, bf16[512,192]{1,0:T(8,128)(2,1)S(1)}, u32[]{:S(2)}, u32[]{:S(2)}) collective-permute-start(bf16[512,192]{1,0:T(8,128)(2,1)S(1)} %get-tuple-element.129), channel_id=1, source_target_pairs={{0,24},{4,28},{8,16},{12,20},{16,8},{20,12},{24,0},{28,4},{1,25},{... | collective-permute-start | bytes 589832 | tf_op jit(solution)/shard_map/ppermute | solution.py:701
  87.3 20.0 %collective-permute-start.19 = (bf16[96,768]{1,0:T(8,128)(2,1)S(1)}, bf16[96,768]{1,0:T(8,128)(2,1)S(1)}, u32[]{:S(2)}, u32[]{:S(2)}) collective-permute-start(bf16[96,768]{1,0:T(8,128)(2,1)S(1)} %get-tuple-element.137), channel_id=1, source_target_pairs={{0,8},{4,12},{8,0},{12,4},{16,24},{20,28},{24,16},{28,20},{1,9},{5... | collective-permute-start | bytes 442376 | tf_op jit(solution)/shard_map/ppermute | solution.py:701
  89.1 27.4 %collective-permute-start.24 = (bf16[384,768]{1,0:T(8,128)(2,1)S(1)}, bf16[384,768]{1,0:T(8,128)(2,1)S(1)}, u32[]{:S(2)}, u32[]{:S(2)}) collective-permute-start(bf16[384,768]{1,0:T(8,128)(2,1)S(1)} %get-tuple-element.136), channel_id=1, source_target_pairs={{0,2},{1,3},{2,0},{3,1},{4,6},{5,7},{6,4},{7,5},{8,10},{9,11},{10,... | collective-permute-start | bytes 1769480 | tf_op jit(solution)/shard_map/ppermute | solution.py:704
  97.9 9.4 %collective-permute-start.20 = (bf16[96,768]{1,0:T(8,128)(2,1)S(1)}, bf16[96,768]{1,0:T(8,128)(2,1)S(1)}, u32[]{:S(2)}, u32[]{:S(2)}) collective-permute-start(bf16[96,768]{1,0:T(8,128)(2,1)S(1)} %get-tuple-element.146), channel_id=1, source_target_pairs={{0,16},{4,20},{8,24},{12,28},{16,0},{20,4},{24,8},{28,12},{1,17},{... | collective-permute-start | bytes 442376 | tf_op jit(solution)/shard_map/ppermute | solution.py:701
  98.1 9.1 %collective-permute-start.21 = (bf16[96,768]{1,0:T(8,128)(2,1)S(1)}, bf16[96,768]{1,0:T(8,128)(2,1)S(1)}, u32[]{:S(2)}, u32[]{:S(2)}) collective-permute-start(bf16[96,768]{1,0:T(8,128)(2,1)S(1)} %get-tuple-element.147), channel_id=1, source_target_pairs={{0,24},{4,28},{8,16},{12,20},{16,8},{20,12},{24,0},{28,4},{1,25},{... | collective-permute-start | bytes 442376 | tf_op jit(solution)/shard_map/ppermute | solution.py:701
  109.2 7.3 %collective-permute-start.23 = (bf16[384,576]{1,0:T(8,128)(2,1)S(1)}, bf16[384,576]{1,0:T(8,128)(2,1)S(1)}, u32[]{:S(2)}, u32[]{:S(2)}) collective-permute-start(bf16[384,576]{1,0:T(8,128)(2,1)S(1)} %get-tuple-element.151), channel_id=1, source_target_pairs={{0,4},{4,0},{8,12},{12,8},{16,20},{20,16},{24,28},{28,24},{1,5},{5... | collective-permute-start | bytes 1327112 | tf_op jit(solution)/shard_map/ppermute | solution.py:707
  109.3 8.2 %collective-permute-start.22 = (bf16[3,512,128]{2,1,0:T(8,128)(2,1)S(1)}, bf16[3,512,128]{2,1,0:T(8,128)(2,1)S(1)}, u32[]{:S(2)}, u32[]{:S(2)}) collective-permute-start(bf16[3,512,128]{2,1,0:T(8,128)(2,1)S(1)} %get-tuple-element.148.doth), channel_id=1, source_target_pairs={{0,4},{4,0},{8,12},{12,8},{16,20},{20,16},{24,28},{28,24},{1,5},{5... | collective-permute-start | bytes 1179656 | tf_op jit(solution)/shard_map/ppermute | solution.py:707
  111.5 5.0 %collective-permute-start.25 = (bf16[16,576]{1,0:T(8,128)(2,1)S(1)}, bf16[16,576]{1,0:T(8,128)(2,1)S(1)}, u32[]{:S(2)}, u32[]{:S(2)}) collective-permute-start(bf16[16,576]{1,0:T(8,128)(2,1)S(1)} %get-tuple-element.155), channel_id=1, source_target_pairs={{0,4},{4,0},{8,12},{12,8},{16,20},{20,16},{24,28},{28,24},{1,5},{5... | collective-permute-start | bytes 55304 | tf_op jit(solution)/shard_map/ppermute | solution.py:707
  117.4 10.1 %collective-permute-start.29 = (bf16[272,576]{1,0:T(8,128)(2,1)S(1)}, bf16[272,576]{1,0:T(8,128)(2,1)S(1)}, u32[]{:S(2)}, u32[]{:S(2)}) collective-permute-start(bf16[272,576]{1,0:T(8,128)(2,1)S(1)} %get-tuple-element.157), channel_id=1, source_target_pairs={{0,1},{1,0},{2,3},{3,2},{4,5},{5,4},{6,7},{7,6},{8,9},{9,8},{10,11... | collective-permute-start | bytes 940040 | tf_op jit(solution)/shard_map/ppermute | solution.py:704
  120.6 22.6 %collective-permute-start.26 = (bf16[256,768]{1,0:T(8,128)(2,1)}, bf16[256,768]{1,0:T(8,128)(2,1)}, u32[]{:S(2)}, u32[]{:S(2)}) collective-permute-start(bf16[256,768]{1,0:T(8,128)(2,1)} %get-tuple-element.166), channel_id=1, source_target_pairs={{0,8},{4,12},{8,0},{12,4},{16,24},{20,28},{24,16},{28,20},{1,9},{5... | collective-permute-start | bytes 1179656 | tf_op jit(solution)/shard_map/ppermute | solution.py:701
  120.9 23.7 %collective-permute-start.27 = (bf16[256,768]{1,0:T(8,128)(2,1)}, bf16[256,768]{1,0:T(8,128)(2,1)}, u32[]{:S(2)}, u32[]{:S(2)}) collective-permute-start(bf16[256,768]{1,0:T(8,128)(2,1)} %get-tuple-element.167), channel_id=1, source_target_pairs={{0,16},{4,20},{8,24},{12,28},{16,0},{20,4},{24,8},{28,12},{1,17},{... | collective-permute-start | bytes 1179656 | tf_op jit(solution)/shard_map/ppermute | solution.py:701
  122.6 22.7 %collective-permute-start.28 = (bf16[256,768]{1,0:T(8,128)(2,1)}, bf16[256,768]{1,0:T(8,128)(2,1)}, u32[]{:S(2)}, u32[]{:S(2)}) collective-permute-start(bf16[256,768]{1,0:T(8,128)(2,1)} %get-tuple-element.168), channel_id=1, source_target_pairs={{0,24},{4,28},{8,16},{12,20},{16,8},{20,12},{24,0},{28,4},{1,25},{... | collective-permute-start | bytes 1179656 | tf_op jit(solution)/shard_map/ppermute | solution.py:701
  127.5 12.1 %collective-permute-start.31 = (bf16[192,768]{1,0:T(8,128)(2,1)S(1)}, bf16[192,768]{1,0:T(8,128)(2,1)S(1)}, u32[]{:S(2)}, u32[]{:S(2)}) collective-permute-start(bf16[192,768]{1,0:T(8,128)(2,1)S(1)} %get-tuple-element.174), channel_id=1, source_target_pairs={{0,1},{1,0},{2,3},{3,2},{4,5},{5,4},{6,7},{7,6},{8,9},{9,8},{10,11... | collective-permute-start | bytes 884744 | tf_op jit(solution)/shard_map/ppermute | solution.py:704
  127.9 11.9 %collective-permute-start.30 = (bf16[144,576]{1,0:T(8,128)(2,1)S(1)}, bf16[144,576]{1,0:T(8,128)(2,1)S(1)}, u32[]{:S(2)}, u32[]{:S(2)}) collective-permute-start(bf16[144,576]{1,0:T(8,128)(2,1)S(1)} %get-tuple-element.178), channel_id=1, source_target_pairs={{0,2},{1,3},{2,0},{3,1},{4,6},{5,7},{6,4},{7,5},{8,10},{9,11},{10,... | collective-permute-start | bytes 497672 | tf_op jit(solution)/shard_map/ppermute | solution.py:704
  141.1 6.6 %collective-permute-start.32 = (bf16[32,1472]{1,0:T(8,128)(2,1)S(1)}, bf16[32,1472]{1,0:T(8,128)(2,1)S(1)}, u32[]{:S(2)}, u32[]{:S(2)}) collective-permute-start(bf16[32,1472]{1,0:T(8,128)(2,1)S(1)} %get-tuple-element.185), channel_id=1, source_target_pairs={{0,8},{4,12},{8,0},{12,4},{16,24},{20,28},{24,16},{28,20},{1,9},{5... | collective-permute-start | bytes 282632 | tf_op jit(solution)/shard_map/ppermute | solution.py:701
  141.5 6.2 %collective-permute-start.33 = (bf16[32,1472]{1,0:T(8,128)(2,1)S(1)}, bf16[32,1472]{1,0:T(8,128)(2,1)S(1)}, u32[]{:S(2)}, u32[]{:S(2)}) collective-permute-start(bf16[32,1472]{1,0:T(8,128)(2,1)S(1)} %get-tuple-element.186), channel_id=1, source_target_pairs={{0,16},{4,20},{8,24},{12,28},{16,0},{20,4},{24,8},{28,12},{1,17},{... | collective-permute-start | bytes 282632 | tf_op jit(solution)/shard_map/ppermute | solution.py:701
  143.2 5.5 %collective-permute-start.34 = (bf16[32,1472]{1,0:T(8,128)(2,1)S(1)}, bf16[32,1472]{1,0:T(8,128)(2,1)S(1)}, u32[]{:S(2)}, u32[]{:S(2)}) collective-permute-start(bf16[32,1472]{1,0:T(8,128)(2,1)S(1)} %get-tuple-element.187), channel_id=1, source_target_pairs={{0,24},{4,28},{8,16},{12,20},{16,8},{20,12},{24,0},{28,4},{1,25},{... | collective-permute-start | bytes 282632 | tf_op jit(solution)/shard_map/ppermute | solution.py:701
  144.6 4.0 %collective-permute-start.35 = (bf16[96,768]{1,0:T(8,128)(2,1)S(1)}, bf16[96,768]{1,0:T(8,128)(2,1)S(1)}, u32[]{:S(2)}, u32[]{:S(2)}) collective-permute-start(bf16[96,768]{1,0:T(8,128)(2,1)S(1)} %get-tuple-element.189), channel_id=1, source_target_pairs={{0,0},{1,9},{2,18},{3,27},{4,4},{5,13},{6,22},{7,31},{8,8},{9,1},{... | collective-permute-start | bytes 442376 | tf_op jit(solution)/shard_map/ppermute | solution.py:1002
  (14 other events, 142.8 us)

commit v4 on v3

--- a/solution.py
+++ b/solution.py
@@ -66,7 +66,7 @@
     xs = [refs[8].at[k] for k in range(4)]
     if fast:
         xs += [refs[9].at[k] for k in range(4)]
-    normed, kv, query, marks, gains, table, W, small = refs[-8:]
+    normed, kv, query, marks, gains, W, small = refs[-7:]
     rows = W.shape[2]
     for k in range(4):
         z = f ^ k
@@ -76,7 +76,6 @@
     gain = jnp.concatenate([small[z, 0:1, 0 : D // 4] for z in range(4)], axis=1)
     gains[0:1, :] = gain
     gains[1:2, :] = jnp.concatenate([small[z, 1:2, 0 : D // 4] for z in range(4)], axis=1)
-    table[...] = jnp.concatenate([small[z, 8:16, 0:128] for z in range(4)], axis=0)
     weight = W[...].reshape(D, 3 * CG)
     count = len(xs)
     seg = [xs[k][T:, :].astype(f32)[0:1, :128] for k in range(count)]
@@ -100,13 +99,17 @@
                 query[h, at, :] = jnp.concatenate([q, blank], axis=1).astype(bf16)
 
 
-def tiles_kernel(T, ids, table, tiles):
-    g = ids[0]
+def tiles_kernel(T, ids, w0, w1, w2, w3, tiles, small):
+    g, f = ids[0], ids[2]
+    rows = w0.shape[0] - 16
+    for k, w in enumerate((w0, w1, w2, w3)):
+        small[f ^ k] = w[rows:, :].astype(f32)
+    table = jnp.concatenate([small[z, 8:16, 0:128] for z in range(4)], axis=0)
     lane = lax.broadcasted_iota(jnp.int32, (32, 128), 1)
     m = lax.broadcasted_iota(jnp.int32, (32, 2 * T), 1)
     label = lax.broadcasted_iota(jnp.int32, (32, 2 * T), 0)
     for h in range(HG):
-        column = jnp.sum(jnp.where(lane == HG * g + h, table[...], 0.0), axis=1, keepdims=True)
+        column = jnp.sum(jnp.where(lane == HG * g + h, table, 0.0), axis=1, keepdims=True)
         for d in range(5):
             if d in (0, 4):
                 one = column[15 if d == 0 else 31 :][:1, :]
@@ -298,10 +301,12 @@
 def middle_kernel(T, ids, *refs):
     g, half, f = ids[0], ids[1], ids[2]
     x, ctx, gains = refs[0:3]
-    cot_all, ws, others = refs[3], refs[4:8], refs[8:12]
-    res0, sends, gcs = refs[12], refs[13:16], refs[16:20]
-    grads, normed, active, ginner, branch = refs[20:25]
-    WO, W1, W2, held = refs[25:29]
+    cots, ws, others = refs[3:7], refs[7:11], refs[11:15]
+    res0, sends, gcs = refs[15], refs[16:19], refs[19:23]
+    grads, normed, active, ginner, branch, cot_all = refs[23:29]
+    WO, W1, W2, held = refs[29:33]
+    for k in range(4):
+        cot_all[g ^ k] = cots[k][...]
     rows, low = WO.shape[2], WO.shape[2] // 2
     FH = W1.shape[3]
     for k in range(4):
@@ -416,7 +421,7 @@
     return jnp.concatenate([high, (value - high.astype(f32)).astype(bf16)], axis=0)
 
 
-def project_grad_kernel(T, ids, normed, dq, down, doth, keep, send, gw):
+def project_grad_kernel(T, ids, normed, dq, down, doth, keep, e0, e1, gw):
     c = ids[3]
     R = D // 8
     own = jnp.concatenate([down[h] for h in range(HG)], axis=1)
@@ -426,7 +431,7 @@
     gw[...] = jnp.concatenate([pairs, single], axis=1).reshape(4, 2, R, 3 * CG)
     for a in range(4):
         keep[a] = gw[a, c]
-        send[a * R : (a + 1) * R, :] = gw[a, 1 - c].astype(bf16)
+        (e0, e1)[a // 2][a % 2] = gw[a, 1 - c].astype(bf16)
 
 
 def extra_kernel(table, block, send):
@@ -436,7 +441,7 @@
     send[...] = split_rows(rows)
 
 
-def start_kernel(T, C, ids, q, k, v, first, second, table, x, seg, out, x_out, small, held, gain1, gain2, rows8, marks, sems):
+def start_steps(T, C, ids, q, k, v, first, second, table, x, seg, out, x_out, small, held, gain1, gain2, rows8, marks, sems):
     place = lax.axis_index("seq")
     g = lax.div(place, C)
     side = lax.rem(place, C) if ids is None else ids[1]
@@ -449,6 +454,7 @@
     for copy in copies:
         copy.start()
     small[...] = jnp.zeros_like(small)
+    yield
     for copy in copies:
         copy.wait()
     mark = jnp.concatenate([marks[...].astype(f32), jnp.zeros((15, T), f32)], axis=0)
@@ -469,7 +475,7 @@
             out[:rows, :] = jnp.concatenate(pieces, axis=1)
 
 
-def middle_pack_kernel(C, ids, wo, inner, outer, out, held, block, sems):
+def middle_steps(C, ids, wo, inner, outer, out, held, block, sems):
     place, f = lax.axis_index("seq"), lax.axis_index("fsdp")
     g = lax.div(place, C)
     side = lax.rem(place, C) if ids is None else ids[1]
@@ -486,6 +492,7 @@
     copies = [pltpu.make_async_copy(a, b, sems.at[n]) for n, (a, b) in enumerate(pairs)]
     for copy in copies:
         copy.start()
+    yield
     for copy in copies:
         copy.wait()
     for a in range(GROUPS):
@@ -498,6 +505,18 @@
 
     out[2 * R0 : 2 * R0 + low, :] = block[:, : D // 2]
     out[2 * R0 + low :, :] = block[:, D // 2 :]
+
+
+def start_kernel(T, C, ids, *refs):
+    inputs, outputs, scratch = refs[:11], refs[11:14], refs[14:]
+    steps = [
+        start_steps(T, C, ids, *inputs[:8], *outputs[:2], *scratch[:7]),
+        middle_steps(C, ids, *inputs[8:], outputs[2], *scratch[7:]),
+    ]
+    for step in steps:
+        next(step)
+    for step in steps:
+        next(step, None)
 
 
 def added(refs):
@@ -575,10 +594,11 @@
     return jnp.concatenate([block[:rows], right], axis=1)
 
 
-def project_join_kernel(ids, keep, more, extra, extra_more, wown, p1, p2, p3, far, near, extra_out, total, out_total):
+def project_join_kernel(ids, keep, m0, m1, extra, extra_more, wown, p1, p2, p3, far, near, extra_out, total, out_total):
     f = ids[2]
     R = D // 8
-    total[...] = (keep[...] + more[...].astype(f32).reshape(4, R, 3 * CG)).reshape(4, 4, R // 4, 3 * CG)
+    for a in range(4):
+        total[a] = (keep[a] + (m0, m1)[a // 2][a % 2].astype(f32)).reshape(4, R // 4, 3 * CG)
     out_total[...] = added((wown, p1, p2, p3)).reshape(4, R // 4, D)
     ex = extra[...] + unsplit(extra_more[...].astype(f32))
     extra_out[...] = ex
@@ -720,7 +740,7 @@
         kernel = functools.partial(start_kernel, T, C)
         return call(
             functools.partial(kernel, None) if own else kernel,
-            (shape((RH + 16, 3 * CG), bf16), shape((T + 16, D), bf16)),
+            (shape((RH + 16, 3 * CG), bf16), shape((T + 16, D), bf16), shape((3 * R0, D // 2), bf16)),
             ([] if own else [ids_for(side)])
             + [
                 query_weight,
@@ -731,6 +751,9 @@
                 bias_table,
                 activations,
                 segments,
+                output_weight,
+                inner_weight,
+                outer_weight,
             ],
             scratch=[
                 pltpu.VMEM((16, 3 * CG), f32),
@@ -740,21 +763,6 @@
                 pltpu.VMEM(bias_table.shape, bf16),
                 pltpu.VMEM((1, T), jnp.int32),
                 pltpu.SemaphoreType.DMA((8,)),
-            ],
-            us=1,
-            mib=60,
-            scalars=0 if own else 1,
-            far=range(9),
-        )
-
-    def middle_pack(side):
-        own = fast and side is half
-        kernel = functools.partial(middle_pack_kernel, C)
-        return call(
-            functools.partial(kernel, None) if own else kernel,
-            shape((3 * R0, D // 2), bf16),
-            ([] if own else [ids_for(side)]) + [output_weight, inner_weight, outer_weight],
-            scratch=[
                 pltpu.VMEM((4, R0, 256), bf16),
                 pltpu.VMEM((F0 // 8, D), bf16),
                 pltpu.SemaphoreType.DMA((6,)),
@@ -762,7 +770,7 @@
             us=1,
             mib=60,
             scalars=0 if own else 1,
-            far=range(4),
+            far=range(12),
         )
 
     def after(values, *earlier):
@@ -776,14 +784,10 @@
     def gather(value):
         return lax.all_gather(value, "seq", axis=0, axis_index_groups=token_groups)
 
-    w_pack, x_pack = start(half)
-    output_weight, inner_weight, outer_weight, w_pack = after(
-        (output_weight, inner_weight, outer_weight, w_pack), w_pack
-    )
-    m_pack = middle_pack(half)
+    w_pack, x_pack, m_pack = start(half)
     ws = from_planes(w_pack)
     m1, m2 = plane_move(m_pack, 1), plane_move(m_pack, 2)
-    x_all = gather(after(x_pack, m_pack))
+    x_all = gather(x_pack)
     if fast:
         xo = [core_move(after(x_all, *ws))]
         wo = [core_move(w) for w in ws]
@@ -791,8 +795,16 @@
         xo = []
         wo = from_planes(start(1)[0])
 
+    tiles = call(
+        functools.partial(tiles_kernel, T),
+        shape((HG, 5, T, T), f32),
+        [ids] + ws,
+        scratch=[pltpu.VMEM((4, 16, 3 * CG), f32)],
+        us=1,
+    )
+    x_all, tiles = after((x_all, tiles), tiles)
     wide_t = (8 if fast else 4) * T
-    normed, kv, query, marks, gains, table = call(
+    normed, kv, query, marks, gains = call(
         functools.partial(project_kernel, T, fast),
         (
             shape((wide_t, D), bf16),
@@ -800,14 +812,13 @@
             shape((HG, 4 * T, 128), bf16),
             shape((8, 128), f32),
             shape((8, D), f32),
-            shape((32, 128), f32),
         ),
         [ids] + ws + wo + [x_all] + xo,
         scratch=[pltpu.VMEM((4, 2, RH, 3 * CG), bf16), pltpu.VMEM((4, 16, 3 * CG), f32)],
         us=1,
     )
-    tiles = call(functools.partial(tiles_kernel, T), shape((HG, 5, T, T), f32), [ids, table], us=1)
-
+
+    cots = from_group(after(cotangent[0], kv))
     slot = jnp.arange(4, dtype=jnp.int32)
     q_at = slot * C + c
     seg_q = marks
@@ -831,19 +842,17 @@
         us=1,
     )
     if fast:
-        mo = [core_move(m_pack)]
-        ctx_all = gather(after(context, *mo))
-        m1, m2 = after((m1, m2), ctx_all)
+        context, m1, m2, cots = after((context, m1, m2, tuple(cots)), context)
+        mo = [core_move(m_pack), core_move(m1)]
+        m2 = after(m2, *mo)
         m3 = plane_move(m2, 1)
-        mo += [core_move(m1), core_move(m2)]
-        cot_all = gather(after(cotangent[0], ctx_all, *mo))
-        m3 = after(m3, cot_all)
-        mo.append(core_move(m3))
+        ctx_all = gather(after(context, *mo, *cots))
+        m2, m3 = after((m2, m3), ctx_all)
+        mo += [core_move(m2), core_move(m3)]
     else:
         ctx_all = gather(context)
         m3 = plane_move(m2, 1)
-        cot_all = gather(cotangent[0])
-        mo = from_planes(middle_pack(1))
+        mo = from_planes(start(1)[2])
     ms = (m_pack, m1, m2, m3)
 
     FH = F0 // 2
@@ -853,8 +862,9 @@
         + (shape((T, D), bf16),) * 3
         + (shape((4 * T, CG), bf16),) * 4
         + (shape((4 * T, D), f32),)
-        + (shape((4 * T, D), bf16),) * 4,
-        [ids, x_all, ctx_all, gains, cot_all] + list(ms) + mo,
+        + (shape((4 * T, D), bf16),) * 4
+        + (shape((4, T, D), bf16),),
+        [ids, x_all, ctx_all, gains] + list(cots) + list(ms) + mo,
         scratch=[
             pltpu.VMEM((4, 2, R0, D // 2), bf16),
             pltpu.VMEM((2, 4, R0, FH), bf16),
@@ -865,7 +875,7 @@
         us=10,
     )
     res0, res_send, gcs = outs[0], outs[1:4], outs[4:8]
-    grads, normed_ffn, active, ginner, branch = outs[8:13]
+    grads, normed_ffn, active, ginner, branch, cot_all = outs[8:14]
     got = [gcs[0]] + [group_move(gcs[k], k) for k in (1, 2, 3)]
     R = D // 8
     keep, send = call(
@@ -927,14 +937,14 @@
         dq, down, doth, sums = back
         doth = after(doth, *ps)
         dmore = core_move(doth)
-        keep_p, send_p = call(
+        keep_p, *send_p = call(
             functools.partial(project_grad_kernel, T),
-            (shape((4, R, 3 * CG), f32), shape((4 * R, 3 * CG), bf16)),
+            (shape((4, R, 3 * CG), f32),) + (shape((2, R, 3 * CG), bf16),) * 2,
             [ids, normed, dq, down, doth],
             scratch=[pltpu.VMEM((4, 2, R, 3 * CG), f32)],
         )
         RB = R + RR * D // (3 * CG)
-        project_more = core_move(send_p)
+        project_more = [core_move(v) for v in send_p]
     else:
         dq, dall, sums = back
         down = lax.psum_scatter(dall, "seq", scatter_dimension=0, axis_index_groups=members)
@@ -945,12 +955,11 @@
     extra, extra_send = call(extra_kernel, small, [table_row], scalars=0, us=1)
     if fast:
         RB = R + RR * D // (3 * CG)
-        extra, middle_more = after((extra, middle_more), middle_more)
         project_far, project_near, extra = call(
             project_join_kernel,
             (shape((2 * RB + 16, 3 * CG), bf16),)
             + (shape((2 * RB, 3 * CG), f32), shape((8, 3 * CG), f32)),
-            [ids, keep_p, project_more, extra, core_move(extra_send), wown] + ps,
+            [ids, keep_p] + project_more + [extra, core_move(extra_send), wown] + ps,
             scratch=[pltpu.VMEM((4, 4, RR, 3 * CG), f32), pltpu.VMEM((4, RR, D), f32)],
             us=1,
         )

time: 151 us -> 144 us (0.954)
  blocking collectives: 37.4 us -> 25.2 us
  starting transfers between devices: 28.8 us -> 39.9 us
  waiting for transfers between devices: 34.8 us -> 28 us
    all_gather x3 -> x2, blocking collectives: 37.4 us -> 25.2 us  [gather(): return lax.all_gather(value, 'seq', axis=0, axis_index_groups=token_groups)]
    ppermute x10, starting transfers between devices: 11.4 us -> 18.1 us  [plane_move(): return lax.ppermute(value, 'fsdp', [(i, i ^ k) for i in range(fsdps)])]
    ppermute x12 -> x15, starting transfers between devices: 14.1 us -> 17.6 us  [group_move(): return lax.ppermute(value, 'seq', pairs)]
    ppermute x12 -> x15, waiting for transfers between devices: 9.23 us -> 6.21 us  [group_move(): return lax.ppermute(value, 'seq', pairs)]
    ppermute x10, waiting for transfers between devices: 19.4 us -> 17.2 us  [plane_move(): return lax.ppermute(value, 'fsdp', [(i, i ^ k) for i in range(fsdps)])]
    ppermute x13 -> x14, waiting for transfers between devices: 6.23 us -> 4.61 us  [core_move(): return lax.ppermute(value, 'seq', [(i, i ^ 1) for i in range(seqs)])]
    pallas_call x20 -> x19, Pallas kernels: 44.9 us -> 43.6 us  [call(): pl.pallas_call(kernel, out_shape=outs, in_specs=[smem] * scalars + [hbm i...]
    ppermute x13 -> x14, starting transfers between devices: 2.72 us -> 3.54 us  [core_move(): return lax.ppermute(value, 'seq', [(i, i ^ 1) for i in range(seqs)])]
  transfers between devices with their start and end apart: 36 -> 40, of which waited for: 12 -> 12; matrix products, arithmetic and copies ran while one was open for 2% -> 2% of each run, Pallas kernels for 20% -> 20%
where the time goes in v4:
time: 144 us; the launch traced here: 142 us
  Pallas kernels  43.6 us (30%)
  starting transfers between devices  39.9 us (28%)
  waiting for transfers between devices  28 us (19%)
  blocking collectives  25.2 us (18%)
  other arithmetic  2.64 us (2%)
  local copies, waits for them, and re-layouts  1.63 us (1%)
    pallas_call x19, Pallas kernels, call(): pl.pallas_call(kernel, out_shape=outs, in_specs=[smem] * scalars + [hbm i...  43.6 us
    all_gather x2, blocking collectives, gather(): return lax.all_gather(value, 'seq', axis=0, axis_index_groups=token_groups)  25.2 us
    ppermute x10, starting transfers between devices, plane_move(): return lax.ppermute(value, 'fsdp', [(i, i ^ k) for i in range(fsdps)])  18.1 us
    ppermute x15, starting transfers between devices, group_move(): return lax.ppermute(value, 'seq', pairs)  17.6 us
    ppermute x10, waiting for transfers between devices, plane_move(): return lax.ppermute(value, 'fsdp', [(i, i ^ k) for i in range(fsdps)])  17.2 us
    ppermute x15, waiting for transfers between devices, group_move(): return lax.ppermute(value, 'seq', pairs)  6.21 us
    ppermute x14, waiting for transfers between devices, core_move(): return lax.ppermute(value, 'seq', [(i, i ^ 1) for i in range(seqs)])  4.61 us
    ppermute x14, starting transfers between devices, core_move(): return lax.ppermute(value, 'seq', [(i, i ^ 1) for i in range(seqs)])  3.54 us
  transfers between devices with their start and end apart: 40, of which 12 were waited for; matrix products, arithmetic and copies ran while one was open for 2% of the time, Pallas kernels for 20%

profile of v4, /device:TPU:0, one launch (start us, length us, event | category | flops | bytes accessed | tf_op | source)
XLA Modules:
  0.0 142.0 jit_solution(4411818403242113782)
XLA Ops:
  0.6 2.5 %shard_map.203 = (bf16[112,576]{1,0:T(8,128)(2,1)}, bf16[144,768]{1,0:T(8,128)(2,1)}, bf16[576,384]{1,0:T(8,128)(2,1)}) custom-call(bf16[192,768]{1,0:T(8,128)(2,1)} %refs_0_.1, bf16[192,768]{1,0:T(8,128)(2,1)} %refs_1_.1, bf16[192,768]{1,0:T(8,128)(2,1)} %refs_2_.1, bf16[192]{0:T(256)(128)(2,1)} %refs_3_.1, bf16[192]{0:T(256)(128)(2,1)} %refs_4_.1, ...), custom_call_target="tpu_custom_call" | custom-call | flops 1000000 | bytes 1024 | tf_op jit(solution)/shard_map/pallas_call | solution.py:48
  3.2 5.1 %collective-permute-start.2 = (bf16[112,576]{1,0:T(8,128)(2,1)}, bf16[112,576]{1,0:T(8,128)(2,1)S(1)}, u32[]{:S(2)}, u32[]{:S(2)}) collective-permute-start(bf16[112,576]{1,0:T(8,128)(2,1)} %get-tuple-element.110.w0.refs_0_), channel_id=1, source_target_pairs={{0,3},{1,2},{2,1},{3,0},{4,7},{5,6},{6,5},{7,4},{8,11},{9,10},{10,... | collective-permute-start | bytes 387080 | tf_op jit(solution)/shard_map/ppermute | solution.py:724
  8.9 12.4 %all-gather = bf16[576,768]{1,0:T(8,128)(2,1)S(1)} all-gather(bf16[144,768]{1,0:T(8,128)(2,1)} %get-tuple-element.109), channel_id=2, replica_groups={{0,8,16,24},{4,12,20,28},{1,9,17,25},{5,13,21,29},{2,10,18,26},{6,14,22..., dimensions={0}, use_global_device_ids=true | all-gather | bytes 1105920 | tf_op jit(solution)/shard_map/all_gather | solution.py:785
  22.0 2.3 %collective-permute-start.9 = (bf16[576,384]{1,0:T(8,128)(2,1)}, bf16[576,384]{1,0:T(8,128)(2,1)S(1)}, u32[]{:S(2)}, u32[]{:S(2)}) collective-permute-start(bf16[576,384]{1,0:T(8,128)(2,1)} %get-tuple-element.118.refs_7_.refs_4_), channel_id=1, source_target_pairs={{0,2},{1,3},{2,0},{3,1},{4,6},{5,7},{6,4},{7,5},{8,10},{9,11},{10,... | collective-permute-start | bytes 1327112 | tf_op jit(solution)/shard_map/ppermute | solution.py:724
  24.3 1.7 %collective-permute-start.8 = (bf16[576,384]{1,0:T(8,128)(2,1)}, bf16[576,384]{1,0:T(8,128)(2,1)S(1)}, u32[]{:S(2)}, u32[]{:S(2)}) collective-permute-start(bf16[576,384]{1,0:T(8,128)(2,1)} %get-tuple-element.118.refs_7_.refs_4_), channel_id=1, source_target_pairs={{0,1},{1,0},{2,3},{3,2},{4,5},{5,4},{6,7},{7,6},{8,9},{9,8},{10,11... | collective-permute-start | bytes 1327112 | tf_op jit(solution)/shard_map/ppermute | solution.py:724
  28.8 2.6 %shard_map.205 = (bf16[1024,768]{1,0:T(8,128)(2,1)S(1)}, bf16[3,1024,128]{2,1,0:T(8,128)(2,1)S(1)}, bf16[3,512,128]{2,1,0:T(8,128)(2,1)S(1)}, f32[8,128]{1,0:T(8,128)S(1)}, f32[8,768]{1,0:T(8,128)S(1)}) custom-call(s32[4]{0:T(128)S(1)} %pad_add_fusion.ids, bf16[112,576]{1,0:T(8,128)(2,1)S(1)} %copy-done, ...), custom_call_target="tpu_custom_call" | custom-call | flops 1000000 | bytes 1024 | tf_op jit(solution)/shard_map/pallas_call | solution.py:48
  31.4 1.5 %collective-permute-start.12 = (bf16[128,768]{1,0:T(8,128)(2,1)S(1)}, bf16[128,768]{1,0:T(8,128)(2,1)S(1)}, u32[]{:S(2)}, u32[]{:S(2)}) collective-permute-start(bf16[128,768]{1,0:T(8,128)(2,1)S(1)} %bitcast.20), channel_id=1, source_target_pairs={{0,24},{4,28},{8,16},{12,20},{16,8},{20,12},{24,0},{28,4},{1,25},{... | collective-permute-start | bytes 589832 | tf_op jit(solution)/shard_map/ppermute | solution.py:721
  35.1 5.4 %shard_map.206 = (bf16[512,192]{1,0:T(8,128)(2,1)S(1)}, f32[2,8,256]{2,1,0:T(8,128)S(1)}) custom-call(s32[4]{0:T(128)S(1)} %pad_add_fusion.ids, s32[4]{0:T(128)S(1)} %get-tuple-element.210.q_at, s32[8]{0:T(128)S(1)} %pad_add_fusion.1.k_at, bf16[3,512,128]{2,1,0:T(8,128)(2,1)S(1)} %get-tuple-element.113.query, f32[8,128]{1,0:T(8,128)S(1)} %get-tuple-element.114.seg_q.seg_k, ...), custom_call_target="tpu_custom_call" | custom-call | flops 1000000 | bytes 1024 | tf_op jit(solution)/shard_map/pallas_call | solution.py:48
  40.4 4.8 %collective-permute-done.9.refs_9_.refs_6_ = bf16[576,384]{1,0:T(8,128)(2,1)S(1)} collective-permute-done((bf16[576,384]{1,0:T(8,128)(2,1)}, bf16[576,384]{1,0:T(8,128)(2,1)S(1)}, u32[]{:S(2)}, u32[]{:S(2)}) %collective-permute-start.9) | collective-permute-done | bytes 442400 | tf_op jit(solution)/shard_map/ppermute | solution.py:724
  48.4 12.9 %all-gather.1 = bf16[2048,192]{1,0:T(8,128)(2,1)S(1)} all-gather(bf16[512,192]{1,0:T(8,128)(2,1)S(1)} %get-tuple-element.126), channel_id=3, replica_groups={{0,8,16,24},{4,12,20,28},{1,9,17,25},{5,13,21,29},{2,10,18,26},{6,14,22..., dimensions={0}, use_global_device_ids=true | all-gather | bytes 983040 | tf_op jit(solution)/shard_map/all_gather | solution.py:785
  61.8 1.3 collective-permute-done.16.refs_13_.refs_10_
  63.8 8.2 %shard_map.207 = (f32[128,768]{1,0:T(8,128)S(1)}, bf16[128,768]{1,0:T(8,128)(2,1)S(1)}, bf16[128,768]{1,0:T(8,128)(2,1)S(1)}, bf16[128,768]{1,0:T(8,128)(2,1)S(1...) custom-call(s32[4]{0:T(128)S(1)} %pad_add_fusion.ids, ...), custom_call_target="tpu_custom_call" | custom-call | flops 10000000 | bytes 1024 | tf_op jit(solution)/shard_map/pallas_call | solution.py:48
  72.0 3.0 %shard_map.208 = (f32[3,4,96,768]{3,2,1,0:T(8,128)S(1)}, bf16[3,4,96,768]{3,2,1,0:T(8,128)(2,1)S(1)}) custom-call(s32[4]{0:T(128)S(1)} %pad_add_fusion.ids, bf16[512,768]{1,0:T(8,128)(2,1)S(1)} %get-tuple-element.138.normed, bf16[512,768]{1,0:T(8,128)(2,1)S(1)} %get-tuple-element.139.active, bf16[512,768]{1,0:T(8,128)(2,1)S(1)} %get-tuple-element.140.ginner, ...), custom_call_target="tpu_custom_call" | custom-call | flops 5000000 | bytes 1024 | tf_op jit(solution)/shard_map/pallas_call | solution.py:48
  77.2 1.5 %collective-permute-start.20 = (bf16[512,192]{1,0:T(8,128)(2,1)S(1)}, bf16[512,192]{1,0:T(8,128)(2,1)S(1)}, u32[]{:S(2)}, u32[]{:S(2)}) collective-permute-start(bf16[512,192]{1,0:T(8,128)(2,1)S(1)} %get-tuple-element.137), channel_id=1, source_target_pairs={{0,24},{4,28},{8,16},{12,20},{16,8},{20,12},{24,0},{28,4},{1,25},{... | collective-permute-start | bytes 589832 | tf_op jit(solution)/shard_map/ppermute | solution.py:721
  82.5 2.9 %collective-permute-start.32 = (bf16[384,768]{1,0:T(8,128)(2,1)S(1)}, bf16[384,768]{1,0:T(8,128)(2,1)S(1)}, u32[]{:S(2)}, u32[]{:S(2)}) collective-permute-start(bf16[384,768]{1,0:T(8,128)(2,1)S(1)} %get-tuple-element.145), channel_id=1, source_target_pairs={{0,2},{1,3},{2,0},{3,1},{4,6},{5,7},{6,4},{7,5},{8,10},{9,11},{10,... | collective-permute-start | bytes 1769480 | tf_op jit(solution)/shard_map/ppermute | solution.py:724
  85.3 4.6 %collective-permute-done.19.g2 = bf16[512,192]{1,0:T(8,128)(2,1)S(1)} collective-permute-done((bf16[512,192]{1,0:T(8,128)(2,1)S(1)}, bf16[512,192]{1,0:T(8,128)(2,1)S(1)}, u32[]{:S(2)}, u32[]{:S(2)}) %collective-permute-start.19) | collective-permute-done | bytes 196640 | tf_op jit(solution)/shard_map/ppermute | solution.py:721
  91.4 1.5 %collective-permute-start.24 = (bf16[96,768]{1,0:T(8,128)(2,1)S(1)}, bf16[96,768]{1,0:T(8,128)(2,1)S(1)}, u32[]{:S(2)}, u32[]{:S(2)}) collective-permute-start(bf16[96,768]{1,0:T(8,128)(2,1)S(1)} %get-tuple-element.156), channel_id=1, source_target_pairs={{0,24},{4,28},{8,16},{12,20},{16,8},{20,12},{24,0},{28,4},{1,25},{... | collective-permute-start | bytes 442376 | tf_op jit(solution)/shard_map/ppermute | solution.py:721
  92.9 7.6 %shard_map.211 = (bf16[512,192]{1,0:T(8,128)(2,1)S(1)}, bf16[3,512,128]{2,1,0:T(8,128)(2,1)S(1)}, bf16[3,512,128]{2,1,0:T(8,128)(2,1)S(1)}, f32[3,5,128,128]{3,2,1,0:T(8,128)S(1)}) custom-call(s32[4]{0:T(128)S(1)} %pad_add_fusion.ids, s32[4]{0:T(128)S(1)} %get-tuple-element.210.q_at, s32[8]{0:T(128)S(1)} %pad_add_fusion.1.k_at, ...), custom_call_target="tpu_custom_call" | custom-call | flops 30000001024 | bytes 1024 | tf_op jit(solution)/shard_map/pallas_call | solution.py:48
  100.5 1.9 %shard_map.212 = (f32[4,96,576]{2,1,0:T(8,128)S(1)}, bf16[2,96,576]{2,1,0:T(8,128)(2,1)S(1)}, bf16[2,96,576]{2,1,0:T(8,128)(2,1)S(1)}) custom-call(s32[4]{0:T(128)S(1)} %pad_add_fusion.ids, bf16[1024,768]{1,0:T(8,128)(2,1)S(1)} %get-tuple-element.158.normed, bf16[512,192]{1,0:T(8,128)(2,1)S(1)} %get-tuple-element.152.dq, ...), custom_call_target="tpu_custom_call" | custom-call | flops 2000000 | bytes 1024 | tf_op jit(solution)/shard_map/pallas_call | solution.py:48
  103.1 1.7 %shard_map.213.table = f32[1,384]{1,0:T(1,128)S(1)} custom-call(s32[4]{0:T(128)S(1)} %pad_add_fusion.ids, f32[3,5,128,128]{3,2,1,0:T(8,128)S(1)} %get-tuple-element.162.sums), custom_call_target="tpu_custom_call" | custom-call | flops 2000000 | bytes 1024 | tf_op jit(solution)/shard_map/pallas_call | solution.py:48
  107.0 1.4 collective-permute-start.33
  108.3 3.5 %shard_map.216 = (f32[128,768]{1,0:T(8,128)S(1)}, bf16[256,768]{1,0:T(8,128)(2,1)}, bf16[256,768]{1,0:T(8,128)(2,1)}, bf16[256,768]{1,0:T(8,128)(2,1)}, bf16[512,576]{1,0:T(8,128)(2,1)}) custom-call(s32[4]{0:T(128)S(1)} %pad_add_fusion.ids, bf16[4,144,768]{2,1,0:T(8,128)(2,1)S(1)} %bitcast.17, bf16[512,192]{1,0:T(8,128)(2,1)S(1)} %get-tuple-element.152.dq, ...), custom_call_target="tpu_custom_call" | custom-call | flops 2000000 | bytes 1024 | tf_op jit(solution)/shard_map/pallas_call | solution.py:48
  111.8 1.5 %collective-permute-start.29 = (bf16[256,768]{1,0:T(8,128)(2,1)}, bf16[256,768]{1,0:T(8,128)(2,1)}, u32[]{:S(2)}, u32[]{:S(2)}) collective-permute-start(bf16[256,768]{1,0:T(8,128)(2,1)} %get-tuple-element.175), channel_id=1, source_target_pairs={{0,8},{4,12},{8,0},{12,4},{16,24},{20,28},{24,16},{28,20},{1,9},{5... | collective-permute-start | bytes 1179656 | tf_op jit(solution)/shard_map/ppermute | solution.py:721
  113.8 1.5 %collective-permute-start.31 = (bf16[256,768]{1,0:T(8,128)(2,1)}, bf16[256,768]{1,0:T(8,128)(2,1)}, u32[]{:S(2)}, u32[]{:S(2)}) collective-permute-start(bf16[256,768]{1,0:T(8,128)(2,1)} %get-tuple-element.177), channel_id=1, source_target_pairs={{0,24},{4,28},{8,16},{12,20},{16,8},{20,12},{24,0},{28,4},{1,25},{... | collective-permute-start | bytes 1179656 | tf_op jit(solution)/shard_map/ppermute | solution.py:721
  115.4 2.7 %collective-permute-done.33.more = bf16[272,576]{1,0:T(8,128)(2,1)S(1)} collective-permute-done((bf16[272,576]{1,0:T(8,128)(2,1)S(1)}, bf16[272,576]{1,0:T(8,128)(2,1)S(1)}, u32[]{:S(2)}, u32[]{:S(2)}) %collective-permute-start.33) | collective-permute-done | bytes 313376 | tf_op jit(solution)/shard_map/ppermute | solution.py:724
  118.8 2.7 %collective-permute-start.34 = (bf16[144,576]{1,0:T(8,128)(2,1)S(1)}, bf16[144,576]{1,0:T(8,128)(2,1)S(1)}, u32[]{:S(2)}, u32[]{:S(2)}) collective-permute-start(bf16[144,576]{1,0:T(8,128)(2,1)S(1)} %get-tuple-element.186), channel_id=1, source_target_pairs={{0,2},{1,3},{2,0},{3,1},{4,6},{5,7},{6,4},{7,5},{8,10},{9,11},{10,... | collective-permute-start | bytes 497672 | tf_op jit(solution)/shard_map/ppermute | solution.py:724
  121.6 9.5 %collective-permute-done.35.more = bf16[192,768]{1,0:T(8,128)(2,1)S(1)} collective-permute-done((bf16[192,768]{1,0:T(8,128)(2,1)S(1)}, bf16[192,768]{1,0:T(8,128)(2,1)S(1)}, u32[]{:S(2)}, u32[]{:S(2)}) %collective-permute-start.35) | collective-permute-done | bytes 294944 | tf_op jit(solution)/shard_map/ppermute | solution.py:724
  131.3 1.4 shard_map.220
  133.3 1.4 collective-permute-start.37
  134.7 1.5 %collective-permute-start.38 = (bf16[32,1472]{1,0:T(8,128)(2,1)S(1)}, bf16[32,1472]{1,0:T(8,128)(2,1)S(1)}, u32[]{:S(2)}, u32[]{:S(2)}) collective-permute-start(bf16[32,1472]{1,0:T(8,128)(2,1)S(1)} %get-tuple-element.195), channel_id=1, source_target_pairs={{0,24},{4,28},{8,16},{12,20},{16,8},{20,12},{24,0},{28,4},{1,25},{... | collective-permute-start | bytes 282632 | tf_op jit(solution)/shard_map/ppermute | solution.py:721
  136.8 2.4 %add_bitcast_fusion = (f32[1,128,768]{2,1,0:T(8,128)}, f32[1,128,768]{2,1,0:T(8,128)}) fusion(f32[128,768]{1,0:T(8,128)S(1)} %get-tuple-element.178, bf16[256,768]{1,0:T(8,128)(2,1)} %collective-permute-done.31, bf16[256,768]{1,0:T(8,128)(2,1)} %collective-permute-done.30, bf16[256,768]{1,0:T(8,128)(2,1)} %collective-permute-done.29, ...), kind=kLoop, calls=%fused_computation | loop fusion | flops 1179648 | bytes 2752512 | tf_op jit(solution)/shard_map/broadcast_in_dim | solution.py:1094
  140.2 1.8 %shard_map.221 = (f32[24,768]{1,0:T(8,128)}, f32[24,768]{1,0:T(8,128)}, f32[24,768]{1,0:T(8,128)}, f32[24,3072]{1,0:T(8,128)}, f32[1,24]{1,0:T(1,128)}, /*index=...) custom-call(s32[2]{0:T(128)S(1)} %pad_add_fusion.2.where, f32[24,1472]{1,0:T(8,128)S(1)} %get-tuple-element.192.own, ...), custom_call_target="tpu_custom_call" | custom-call | flops 1000000 | bytes 1024 | tf_op jit(solution)/shard_map/pallas_call | solution.py:48
  (90 shorter events, 24.7 us)
Async XLA Ops:
  3.2 18.1 %collective-permute-start.2 = (bf16[112,576]{1,0:T(8,128)(2,1)}, bf16[112,576]{1,0:T(8,128)(2,1)S(1)}, u32[]{:S(2)}, u32[]{:S(2)}) collective-permute-start(bf16[112,576]{1,0:T(8,128)(2,1)} %get-tuple-element.110.w0.refs_0_), channel_id=1, source_target_pairs={{0,3},{1,2},{2,1},{3,0},{4,7},{5,6},{6,5},{7,4},{8,11},{9,10},{10,... | collective-permute-start | bytes 387080 | tf_op jit(solution)/shard_map/ppermute | solution.py:724
  8.3 13.0 %collective-permute-start.1 = (bf16[112,576]{1,0:T(8,128)(2,1)}, bf16[112,576]{1,0:T(8,128)(2,1)S(1)}, u32[]{:S(2)}, u32[]{:S(2)}) collective-permute-start(bf16[112,576]{1,0:T(8,128)(2,1)} %get-tuple-element.110.w0.refs_0_), channel_id=1, source_target_pairs={{0,2},{1,3},{2,0},{3,1},{4,6},{5,7},{6,4},{7,5},{8,10},{9,11},{10,... | collective-permute-start | bytes 387080 | tf_op jit(solution)/shard_map/ppermute | solution.py:724
  8.3 13.0 %collective-permute-start = (bf16[112,576]{1,0:T(8,128)(2,1)}, bf16[112,576]{1,0:T(8,128)(2,1)S(1)}, u32[]{:S(2)}, u32[]{:S(2)}) collective-permute-start(bf16[112,576]{1,0:T(8,128)(2,1)} %get-tuple-element.110.w0.refs_0_), channel_id=1, source_target_pairs={{0,1},{1,0},{2,3},{3,2},{4,5},{5,4},{6,7},{7,6},{8,9},{9,8},{10,11... | collective-permute-start | bytes 387080 | tf_op jit(solution)/shard_map/ppermute | solution.py:724
  21.3 7.5 %collective-permute-start.7 = (bf16[4,144,768]{2,1,0:T(8,128)(2,1)S(1)}, bf16[4,144,768]{2,1,0:T(8,128)(2,1)S(1)}, u32[]{:S(2)}, u32[]{:S(2)}) collective-permute-start(bf16[4,144,768]{2,1,0:T(8,128)(2,1)S(1)} %bitcast.14), channel_id=1, source_target_pairs={{0,4},{4,0},{8,12},{12,8},{16,20},{20,16},{24,28},{28,24},{1,5},{5... | collective-permute-start | bytes 2654216 | tf_op jit(solution)/shard_map/ppermute | solution.py:727
  21.4 4.6 %collective-permute-start.3 = (bf16[112,576]{1,0:T(8,128)(2,1)}, bf16[112,576]{1,0:T(8,128)(2,1)S(1)}, u32[]{:S(2)}, u32[]{:S(2)}) collective-permute-start(bf16[112,576]{1,0:T(8,128)(2,1)} %get-tuple-element.110.w0.refs_0_), channel_id=1, source_target_pairs={{0,4},{4,0},{8,12},{12,8},{16,20},{20,16},{24,28},{28,24},{1,5},{5... | collective-permute-start | bytes 387080 | tf_op jit(solution)/shard_map/ppermute | solution.py:727
  21.9 4.1 %collective-permute-start.6 = (bf16[112,576]{1,0:T(8,128)(2,1)S(1)}, bf16[112,576]{1,0:T(8,128)(2,1)S(1)}, u32[]{:S(2)}, u32[]{:S(2)}) collective-permute-start(bf16[112,576]{1,0:T(8,128)(2,1)S(1)} %collective-permute-done.2.w3.refs_3_), channel_id=1, source_target_pairs={{0,4},{4,0},{8,12},{12,8},{16,20},{20,16},{24,28},{28,24},{1,5},{5... | collective-permute-start | bytes 387080 | tf_op jit(solution)/shard_map/ppermute | solution.py:727
  22.0 23.2 %collective-permute-start.9 = (bf16[576,384]{1,0:T(8,128)(2,1)}, bf16[576,384]{1,0:T(8,128)(2,1)S(1)}, u32[]{:S(2)}, u32[]{:S(2)}) collective-permute-start(bf16[576,384]{1,0:T(8,128)(2,1)} %get-tuple-element.118.refs_7_.refs_4_), channel_id=1, source_target_pairs={{0,2},{1,3},{2,0},{3,1},{4,6},{5,7},{6,4},{7,5},{8,10},{9,11},{10,... | collective-permute-start | bytes 1327112 | tf_op jit(solution)/shard_map/ppermute | solution.py:724
  24.3 21.0 %collective-permute-start.8 = (bf16[576,384]{1,0:T(8,128)(2,1)}, bf16[576,384]{1,0:T(8,128)(2,1)S(1)}, u32[]{:S(2)}, u32[]{:S(2)}) collective-permute-start(bf16[576,384]{1,0:T(8,128)(2,1)} %get-tuple-element.118.refs_7_.refs_4_), channel_id=1, source_target_pairs={{0,1},{1,0},{2,3},{3,2},{4,5},{5,4},{6,7},{7,6},{8,9},{9,8},{10,11... | collective-permute-start | bytes 1327112 | tf_op jit(solution)/shard_map/ppermute | solution.py:724
  31.4 13.9 %collective-permute-start.12 = (bf16[128,768]{1,0:T(8,128)(2,1)S(1)}, bf16[128,768]{1,0:T(8,128)(2,1)S(1)}, u32[]{:S(2)}, u32[]{:S(2)}) collective-permute-start(bf16[128,768]{1,0:T(8,128)(2,1)S(1)} %bitcast.20), channel_id=1, source_target_pairs={{0,24},{4,28},{8,16},{12,20},{16,8},{20,12},{24,0},{28,4},{1,25},{... | collective-permute-start | bytes 589832 | tf_op jit(solution)/shard_map/ppermute | solution.py:721
  32.9 12.4 %collective-permute-start.11 = (bf16[128,768]{1,0:T(8,128)(2,1)S(1)}, bf16[128,768]{1,0:T(8,128)(2,1)S(1)}, u32[]{:S(2)}, u32[]{:S(2)}) collective-permute-start(bf16[128,768]{1,0:T(8,128)(2,1)S(1)} %bitcast.21), channel_id=1, source_target_pairs={{0,16},{4,20},{8,24},{12,28},{16,0},{20,4},{24,8},{28,12},{1,17},{... | collective-permute-start | bytes 589832 | tf_op jit(solution)/shard_map/ppermute | solution.py:721
  34.0 11.4 %collective-permute-start.10 = (bf16[128,768]{1,0:T(8,128)(2,1)S(1)}, bf16[128,768]{1,0:T(8,128)(2,1)S(1)}, u32[]{:S(2)}, u32[]{:S(2)}) collective-permute-start(bf16[128,768]{1,0:T(8,128)(2,1)S(1)} %bitcast.22), channel_id=1, source_target_pairs={{0,8},{4,12},{8,0},{12,4},{16,24},{20,28},{24,16},{28,20},{1,9},{5... | collective-permute-start | bytes 589832 | tf_op jit(solution)/shard_map/ppermute | solution.py:721
  47.6 13.6 %collective-permute-start.15 = (bf16[576,384]{1,0:T(8,128)(2,1)S(1)}, bf16[576,384]{1,0:T(8,128)(2,1)S(1)}, u32[]{:S(2)}, u32[]{:S(2)}) collective-permute-start(bf16[576,384]{1,0:T(8,128)(2,1)S(1)} %collective-permute-done.9.refs_9_.refs_6_), channel_id=1, source_target_pairs={{0,1},{1,0},{2,3},{3,2},{4,5},{5,4},{6,7},{7,6},{8,9},{9,8},{10,11... | collective-permute-start | bytes 1327112 | tf_op jit(solution)/shard_map/ppermute | solution.py:724
  74.9 5.2 %collective-permute-start.21 = (bf16[3,4,96,768]{3,2,1,0:T(8,128)(2,1)S(1)}, bf16[3,4,96,768]{3,2,1,0:T(8,128)(2,1)S(1)}, u32[]{:S(2)}, u32[]{:S(2)}) collective-permute-start(bf16[3,4,96,768]{3,2,1,0:T(8,128)(2,1)S(1)} %get-tuple-element.144), channel_id=1, source_target_pairs={{0,4},{4,0},{8,12},{12,8},{16,20},{20,16},{24,28},{28,24},{1,5},{5... | collective-permute-start | bytes 5308424 | tf_op jit(solution)/shard_map/ppermute | solution.py:727
  75.1 10.2 %collective-permute-start.18 = (bf16[512,192]{1,0:T(8,128)(2,1)S(1)}, bf16[512,192]{1,0:T(8,128)(2,1)S(1)}, u32[]{:S(2)}, u32[]{:S(2)}) collective-permute-start(bf16[512,192]{1,0:T(8,128)(2,1)S(1)} %get-tuple-element.135), channel_id=1, source_target_pairs={{0,8},{4,12},{8,0},{12,4},{16,24},{20,28},{24,16},{28,20},{1,9},{5... | collective-permute-start | bytes 589832 | tf_op jit(solution)/shard_map/ppermute | solution.py:721
  76.4 13.6 %collective-permute-start.19 = (bf16[512,192]{1,0:T(8,128)(2,1)S(1)}, bf16[512,192]{1,0:T(8,128)(2,1)S(1)}, u32[]{:S(2)}, u32[]{:S(2)}) collective-permute-start(bf16[512,192]{1,0:T(8,128)(2,1)S(1)} %get-tuple-element.136), channel_id=1, source_target_pairs={{0,16},{4,20},{8,24},{12,28},{16,0},{20,4},{24,8},{28,12},{1,17},{... | collective-permute-start | bytes 589832 | tf_op jit(solution)/shard_map/ppermute | solution.py:721
  77.2 13.4 %collective-permute-start.20 = (bf16[512,192]{1,0:T(8,128)(2,1)S(1)}, bf16[512,192]{1,0:T(8,128)(2,1)S(1)}, u32[]{:S(2)}, u32[]{:S(2)}) collective-permute-start(bf16[512,192]{1,0:T(8,128)(2,1)S(1)} %get-tuple-element.137), channel_id=1, source_target_pairs={{0,24},{4,28},{8,16},{12,20},{16,8},{20,12},{24,0},{28,4},{1,25},{... | collective-permute-start | bytes 589832 | tf_op jit(solution)/shard_map/ppermute | solution.py:721
  81.2 19.3 %collective-permute-start.22 = (bf16[96,768]{1,0:T(8,128)(2,1)S(1)}, bf16[96,768]{1,0:T(8,128)(2,1)S(1)}, u32[]{:S(2)}, u32[]{:S(2)}) collective-permute-start(bf16[96,768]{1,0:T(8,128)(2,1)S(1)} %get-tuple-element.146), channel_id=1, source_target_pairs={{0,8},{4,12},{8,0},{12,4},{16,24},{20,28},{24,16},{28,20},{1,9},{5... | collective-permute-start | bytes 442376 | tf_op jit(solution)/shard_map/ppermute | solution.py:721
  82.5 32.8 %collective-permute-start.32 = (bf16[384,768]{1,0:T(8,128)(2,1)S(1)}, bf16[384,768]{1,0:T(8,128)(2,1)S(1)}, u32[]{:S(2)}, u32[]{:S(2)}) collective-permute-start(bf16[384,768]{1,0:T(8,128)(2,1)S(1)} %get-tuple-element.145), channel_id=1, source_target_pairs={{0,2},{1,3},{2,0},{3,1},{4,6},{5,7},{6,4},{7,5},{8,10},{9,11},{10,... | collective-permute-start | bytes 1769480 | tf_op jit(solution)/shard_map/ppermute | solution.py:724
  90.6 9.9 %collective-permute-start.23 = (bf16[96,768]{1,0:T(8,128)(2,1)S(1)}, bf16[96,768]{1,0:T(8,128)(2,1)S(1)}, u32[]{:S(2)}, u32[]{:S(2)}) collective-permute-start(bf16[96,768]{1,0:T(8,128)(2,1)S(1)} %get-tuple-element.155), channel_id=1, source_target_pairs={{0,16},{4,20},{8,24},{12,28},{16,0},{20,4},{24,8},{28,12},{1,17},{... | collective-permute-start | bytes 442376 | tf_op jit(solution)/shard_map/ppermute | solution.py:721
  91.4 9.1 %collective-permute-start.24 = (bf16[96,768]{1,0:T(8,128)(2,1)S(1)}, bf16[96,768]{1,0:T(8,128)(2,1)S(1)}, u32[]{:S(2)}, u32[]{:S(2)}) collective-permute-start(bf16[96,768]{1,0:T(8,128)(2,1)S(1)} %get-tuple-element.156), channel_id=1, source_target_pairs={{0,24},{4,28},{8,16},{12,20},{16,8},{20,12},{24,0},{28,4},{1,25},{... | collective-permute-start | bytes 442376 | tf_op jit(solution)/shard_map/ppermute | solution.py:721
  102.4 3.7 %collective-permute-start.26 = (bf16[2,96,576]{2,1,0:T(8,128)(2,1)S(1)}, bf16[2,96,576]{2,1,0:T(8,128)(2,1)S(1)}, u32[]{:S(2)}, u32[]{:S(2)}) collective-permute-start(bf16[2,96,576]{2,1,0:T(8,128)(2,1)S(1)} %get-tuple-element.160), channel_id=1, source_target_pairs={{0,4},{4,0},{8,12},{12,8},{16,20},{20,16},{24,28},{28,24},{1,5},{5... | collective-permute-start | bytes 663560 | tf_op jit(solution)/shard_map/ppermute | solution.py:727
  103.0 5.3 %collective-permute-start.25 = (bf16[3,512,128]{2,1,0:T(8,128)(2,1)S(1)}, bf16[3,512,128]{2,1,0:T(8,128)(2,1)S(1)}, u32[]{:S(2)}, u32[]{:S(2)}) collective-permute-start(bf16[3,512,128]{2,1,0:T(8,128)(2,1)S(1)} %get-tuple-element.157.doth), channel_id=1, source_target_pairs={{0,4},{4,0},{8,12},{12,8},{16,20},{20,16},{24,28},{28,24},{1,5},{5... | collective-permute-start | bytes 1179656 | tf_op jit(solution)/shard_map/ppermute | solution.py:727
  107.0 11.2 %collective-permute-start.33 = (bf16[272,576]{1,0:T(8,128)(2,1)S(1)}, bf16[272,576]{1,0:T(8,128)(2,1)S(1)}, u32[]{:S(2)}, u32[]{:S(2)}) collective-permute-start(bf16[272,576]{1,0:T(8,128)(2,1)S(1)} %get-tuple-element.166), channel_id=1, source_target_pairs={{0,1},{1,0},{2,3},{3,2},{4,5},{5,4},{6,7},{7,6},{8,9},{9,8},{10,11... | collective-permute-start | bytes 940040 | tf_op jit(solution)/shard_map/ppermute | solution.py:724
  111.8 22.9 %collective-permute-start.29 = (bf16[256,768]{1,0:T(8,128)(2,1)}, bf16[256,768]{1,0:T(8,128)(2,1)}, u32[]{:S(2)}, u32[]{:S(2)}) collective-permute-start(bf16[256,768]{1,0:T(8,128)(2,1)} %get-tuple-element.175), channel_id=1, source_target_pairs={{0,8},{4,12},{8,0},{12,4},{16,24},{20,28},{24,16},{28,20},{1,9},{5... | collective-permute-start | bytes 1179656 | tf_op jit(solution)/shard_map/ppermute | solution.py:721
  113.3 22.9 %collective-permute-start.30 = (bf16[256,768]{1,0:T(8,128)(2,1)}, bf16[256,768]{1,0:T(8,128)(2,1)}, u32[]{:S(2)}, u32[]{:S(2)}) collective-permute-start(bf16[256,768]{1,0:T(8,128)(2,1)} %get-tuple-element.176), channel_id=1, source_target_pairs={{0,16},{4,20},{8,24},{12,28},{16,0},{20,4},{24,8},{28,12},{1,17},{... | collective-permute-start | bytes 1179656 | tf_op jit(solution)/shard_map/ppermute | solution.py:721
  113.8 23.0 %collective-permute-start.31 = (bf16[256,768]{1,0:T(8,128)(2,1)}, bf16[256,768]{1,0:T(8,128)(2,1)}, u32[]{:S(2)}, u32[]{:S(2)}) collective-permute-start(bf16[256,768]{1,0:T(8,128)(2,1)} %get-tuple-element.177), channel_id=1, source_target_pairs={{0,24},{4,28},{8,16},{12,20},{16,8},{20,12},{24,0},{28,4},{1,25},{... | collective-permute-start | bytes 1179656 | tf_op jit(solution)/shard_map/ppermute | solution.py:721
  118.2 13.0 %collective-permute-start.35 = (bf16[192,768]{1,0:T(8,128)(2,1)S(1)}, bf16[192,768]{1,0:T(8,128)(2,1)S(1)}, u32[]{:S(2)}, u32[]{:S(2)}) collective-permute-start(bf16[192,768]{1,0:T(8,128)(2,1)S(1)} %get-tuple-element.182), channel_id=1, source_target_pairs={{0,1},{1,0},{2,3},{3,2},{4,5},{5,4},{6,7},{7,6},{8,9},{9,8},{10,11... | collective-permute-start | bytes 884744 | tf_op jit(solution)/shard_map/ppermute | solution.py:724
  118.8 12.5 %collective-permute-start.34 = (bf16[144,576]{1,0:T(8,128)(2,1)S(1)}, bf16[144,576]{1,0:T(8,128)(2,1)S(1)}, u32[]{:S(2)}, u32[]{:S(2)}) collective-permute-start(bf16[144,576]{1,0:T(8,128)(2,1)S(1)} %get-tuple-element.186), channel_id=1, source_target_pairs={{0,2},{1,3},{2,0},{3,1},{4,6},{5,7},{6,4},{7,5},{8,10},{9,11},{10,... | collective-permute-start | bytes 497672 | tf_op jit(solution)/shard_map/ppermute | solution.py:724
  132.7 6.6 %collective-permute-start.36 = (bf16[32,1472]{1,0:T(8,128)(2,1)S(1)}, bf16[32,1472]{1,0:T(8,128)(2,1)S(1)}, u32[]{:S(2)}, u32[]{:S(2)}) collective-permute-start(bf16[32,1472]{1,0:T(8,128)(2,1)S(1)} %get-tuple-element.193), channel_id=1, source_target_pairs={{0,8},{4,12},{8,0},{12,4},{16,24},{20,28},{24,16},{28,20},{1,9},{5... | collective-permute-start | bytes 282632 | tf_op jit(solution)/shard_map/ppermute | solution.py:721
  133.3 6.0 %collective-permute-start.37 = (bf16[32,1472]{1,0:T(8,128)(2,1)S(1)}, bf16[32,1472]{1,0:T(8,128)(2,1)S(1)}, u32[]{:S(2)}, u32[]{:S(2)}) collective-permute-start(bf16[32,1472]{1,0:T(8,128)(2,1)S(1)} %get-tuple-element.194), channel_id=1, source_target_pairs={{0,16},{4,20},{8,24},{12,28},{16,0},{20,4},{24,8},{28,12},{1,17},{... | collective-permute-start | bytes 282632 | tf_op jit(solution)/shard_map/ppermute | solution.py:721
  134.7 5.5 %collective-permute-start.38 = (bf16[32,1472]{1,0:T(8,128)(2,1)S(1)}, bf16[32,1472]{1,0:T(8,128)(2,1)S(1)}, u32[]{:S(2)}, u32[]{:S(2)}) collective-permute-start(bf16[32,1472]{1,0:T(8,128)(2,1)S(1)} %get-tuple-element.195), channel_id=1, source_target_pairs={{0,24},{4,28},{8,16},{12,20},{16,8},{20,12},{24,0},{28,4},{1,25},{... | collective-permute-start | bytes 282632 | tf_op jit(solution)/shard_map/ppermute | solution.py:721
  136.2 4.0 %collective-permute-start.39 = (bf16[96,768]{1,0:T(8,128)(2,1)S(1)}, bf16[96,768]{1,0:T(8,128)(2,1)S(1)}, u32[]{:S(2)}, u32[]{:S(2)}) collective-permute-start(bf16[96,768]{1,0:T(8,128)(2,1)S(1)} %get-tuple-element.197), channel_id=1, source_target_pairs={{0,0},{1,9},{2,18},{3,27},{4,4},{5,13},{6,22},{7,31},{8,8},{9,1},{... | collective-permute-start | bytes 442376 | tf_op jit(solution)/shard_map/ppermute | solution.py:1011
  (16 other events, 80.0 us)

commit v5 on v4

--- a/solution.py
+++ b/solution.py
@@ -154,8 +154,8 @@
     mark_columns(T, nb * 4, seg_k, columns)
 
     def pair_step(pair, carry):
-        at = pl.ds(pl.multiple_of(pair * 2 * T, 2 * T), 2 * T)
-        seg = jnp.concatenate([seg_q[pl.ds(2 * pair + j, 1), :] for j in range(2)], axis=1)
+        at = slice(pair * 2 * T, (pair + 1) * 2 * T)
+        seg = jnp.concatenate([seg_q[2 * pair + j : 2 * pair + j + 1, :] for j in range(2)], axis=1)
         out = []
         for h in range(HG):
             q = query[h, at, :]
@@ -186,7 +186,8 @@
         context[at, :] = joined.T.astype(bf16)
         return carry
 
-    lax.fori_loop(0, 2, pair_step, 0)
+    for pair in range(2):
+        pair_step(pair, 0)
 
 
 def backward_kernel(T, nb, fast, ids, q_at, k_at, query, seg_q, seg_k, tiles, lse, g0, g1, g2, g3, *rest):
@@ -351,12 +352,8 @@
             active[at, columns] = act
             ginner[at, columns] = gi
         for index, m in enumerate(slots):
-            held[m] = result[index * T : (index + 1) * T]
-
-            @pl.when(g == m)
-            def _():
-                held[m] += att[index * T : (index + 1) * T]
-
+            share = (g == m).astype(f32)
+            held[m] = result[index * T : (index + 1) * T] + share * att[index * T : (index + 1) * T]
         u = gn * gain
         grad = 0.25 * cot.astype(f32) + s * u - att * (s * s * s) * jnp.mean(u * att, axis=-1, keepdims=True)
         grads[at, :] = grad
@@ -802,7 +799,8 @@
         scratch=[pltpu.VMEM((4, 16, 3 * CG), f32)],
         us=1,
     )
-    x_all, tiles = after((x_all, tiles), tiles)
+    m_other = core_move(m_pack) if fast else None
+    x_all, tiles, m_other = after((x_all, tiles, m_other), tiles)
     wide_t = (8 if fast else 4) * T
     normed, kv, query, marks, gains = call(
         functools.partial(project_kernel, T, fast),
@@ -842,13 +840,11 @@
         us=1,
     )
     if fast:
-        context, m1, m2, cots = after((context, m1, m2, tuple(cots)), context)
-        mo = [core_move(m_pack), core_move(m1)]
-        m2 = after(m2, *mo)
+        context, m2, cots = after((context, m2, tuple(cots)), context)
         m3 = plane_move(m2, 1)
-        ctx_all = gather(after(context, *mo, *cots))
-        m2, m3 = after((m2, m3), ctx_all)
-        mo += [core_move(m2), core_move(m3)]
+        ctx_all = gather(after(context, *cots))
+        m1, m2, m3 = after((m1, m2, m3), ctx_all)
+        mo = [m_other, core_move(m1), core_move(m2), core_move(m3)]
     else:
         ctx_all = gather(context)
         m3 = plane_move(m2, 1)
@@ -981,7 +977,6 @@
             us=1,
         )
         project_more = plane_move(project_far, 1)
-        middle_send = after(middle_send, project_more)
         middle_last = plane_move(middle_send, 1)
         send, mine, extra = call(
             project_half_kernel,

time: 144 us -> 141 us (0.979)
  the two profiles are of different devices: /device:TPU:0 before, /device:TPU:24 now
where the time goes in v5:
time: 141 us; the launch traced here: 140 us
  Pallas kernels  43.5 us (31%)
  waiting for transfers between devices  34.1 us (24%)
  starting transfers between devices  31.8 us (23%)
  blocking collectives  25.1 us (18%)
  other arithmetic  2.64 us (2%)
  local copies, waits for them, and re-layouts  2.28 us (2%)
    pallas_call x19, Pallas kernels, call(): pl.pallas_call(kernel, out_shape=outs, in_specs=[smem] * scalars + [hbm i...  43.5 us
    all_gather x2, blocking collectives, gather(): return lax.all_gather(value, 'seq', axis=0, axis_index_groups=token_groups)  25.1 us
    ppermute x10, waiting for transfers between devices, plane_move(): return lax.ppermute(value, 'fsdp', [(i, i ^ k) for i in range(fsdps)])  17.8 us
    ppermute x15, starting transfers between devices, group_move(): return lax.ppermute(value, 'seq', pairs)  17.6 us
    ppermute x15, waiting for transfers between devices, group_move(): return lax.ppermute(value, 'seq', pairs)  8.15 us
    ppermute x10, starting transfers between devices, plane_move(): return lax.ppermute(value, 'fsdp', [(i, i ^ k) for i in range(fsdps)])  7.54 us
    ppermute x14, waiting for transfers between devices, core_move(): return lax.ppermute(value, 'seq', [(i, i ^ 1) for i in range(seqs)])  6.05 us
    ppermute x1, starting transfers between devices, on_device(): outer_got = lax.ppermute(outer_mine, ('seq', 'fsdp'), pairs)  3.41 us
  transfers between devices with their start and end apart: 40, of which 14 were waited for; matrix products, arithmetic and copies ran while one was open for 2% of the time, Pallas kernels for 20%

profile of v5, /device:TPU:24, one launch (start us, length us, event | category | flops | bytes accessed | tf_op | source)
XLA Modules:
  0.0 140.3 jit_solution(4007491617870538538)
XLA Ops:
  0.6 2.5 %shard_map.203 = (bf16[112,576]{1,0:T(8,128)(2,1)}, bf16[144,768]{1,0:T(8,128)(2,1)}, bf16[576,384]{1,0:T(8,128)(2,1)}) custom-call(bf16[192,768]{1,0:T(8,128)(2,1)} %refs_0_.1, bf16[192,768]{1,0:T(8,128)(2,1)} %refs_1_.1, bf16[192,768]{1,0:T(8,128)(2,1)} %refs_2_.1, bf16[192]{0:T(256)(128)(2,1)} %refs_3_.1, bf16[192]{0:T(256)(128)(2,1)} %refs_4_.1, ...), custom_call_target="tpu_custom_call" | custom-call | flops 1000000 | bytes 1024 | tf_op jit(solution)/shard_map/pallas_call | solution.py:48
  3.3 1.9 %collective-permute-start.1 = (bf16[112,576]{1,0:T(8,128)(2,1)}, bf16[112,576]{1,0:T(8,128)(2,1)S(1)}, u32[]{:S(2)}, u32[]{:S(2)}) collective-permute-start(bf16[112,576]{1,0:T(8,128)(2,1)} %get-tuple-element.109.w0.refs_0_), channel_id=1, source_target_pairs={{0,2},{1,3},{2,0},{3,1},{4,6},{5,7},{6,4},{7,5},{8,10},{9,11},{10,... | collective-permute-start | bytes 387080 | tf_op jit(solution)/shard_map/ppermute | solution.py:721
  5.2 2.5 %collective-permute-start = (bf16[112,576]{1,0:T(8,128)(2,1)}, bf16[112,576]{1,0:T(8,128)(2,1)S(1)}, u32[]{:S(2)}, u32[]{:S(2)}) collective-permute-start(bf16[112,576]{1,0:T(8,128)(2,1)} %get-tuple-element.109.w0.refs_0_), channel_id=1, source_target_pairs={{0,1},{1,0},{2,3},{3,2},{4,5},{5,4},{6,7},{7,6},{8,9},{9,8},{10,11... | collective-permute-start | bytes 387080 | tf_op jit(solution)/shard_map/ppermute | solution.py:721
  7.6 12.1 %all-gather = bf16[576,768]{1,0:T(8,128)(2,1)S(1)} all-gather(bf16[144,768]{1,0:T(8,128)(2,1)} %get-tuple-element.108), channel_id=2, replica_groups={{0,8,16,24},{4,12,20,28},{1,9,17,25},{5,13,21,29},{2,10,18,26},{6,14,22..., dimensions={0}, use_global_device_ids=true | all-gather | bytes 1105920 | tf_op jit(solution)/shard_map/all_gather | solution.py:782
  20.9 2.6 %collective-permute-done.4.refs_4_ = bf16[112,576]{1,0:T(8,128)(2,1)S(1)} collective-permute-done((bf16[112,576]{1,0:T(8,128)(2,1)}, bf16[112,576]{1,0:T(8,128)(2,1)S(1)}, u32[]{:S(2)}, u32[]{:S(2)}) %collective-permute-start.4) | collective-permute-done | bytes 129056 | tf_op jit(solution)/shard_map/ppermute | solution.py:724
  27.3 2.7 %shard_map.205 = (bf16[1024,768]{1,0:T(8,128)(2,1)S(1)}, bf16[3,1024,128]{2,1,0:T(8,128)(2,1)S(1)}, bf16[3,512,128]{2,1,0:T(8,128)(2,1)S(1)}, f32[8,128]{1,0:T(8,128)S(1)}, f32[8,768]{1,0:T(8,128)S(1)}) custom-call(s32[4]{0:T(128)S(1)} %pad_add_fusion.ids, bf16[112,576]{1,0:T(8,128)(2,1)S(1)} %copy-done, ...), custom_call_target="tpu_custom_call" | custom-call | flops 1000000 | bytes 1024 | tf_op jit(solution)/shard_map/pallas_call | solution.py:48
  30.0 1.5 %collective-permute-start.12 = (bf16[128,768]{1,0:T(8,128)(2,1)S(1)}, bf16[128,768]{1,0:T(8,128)(2,1)S(1)}, u32[]{:S(2)}, u32[]{:S(2)}) collective-permute-start(bf16[128,768]{1,0:T(8,128)(2,1)S(1)} %bitcast.20), channel_id=1, source_target_pairs={{0,24},{4,28},{8,16},{12,20},{16,8},{20,12},{24,0},{28,4},{1,25},{... | collective-permute-start | bytes 589832 | tf_op jit(solution)/shard_map/ppermute | solution.py:718
  33.7 5.2 %shard_map.206 = (bf16[512,192]{1,0:T(8,128)(2,1)S(1)}, f32[2,8,256]{2,1,0:T(8,128)S(1)}) custom-call(s32[4]{0:T(128)S(1)} %pad_add_fusion.ids, s32[4]{0:T(128)S(1)} %get-tuple-element.208.q_at, s32[8]{0:T(128)S(1)} %pad_add_fusion.1.k_at, bf16[3,512,128]{2,1,0:T(8,128)(2,1)S(1)} %get-tuple-element.113.query, f32[8,128]{1,0:T(8,128)S(1)} %get-tuple-element.114.seg_q.seg_k, ...), custom_call_target="tpu_custom_call" | custom-call | flops 1000000 | bytes 1024 | tf_op jit(solution)/shard_map/pallas_call | solution.py:48
  38.9 4.5 %collective-permute-done.9.refs_9_.refs_6_ = bf16[576,384]{1,0:T(8,128)(2,1)S(1)} collective-permute-done((bf16[576,384]{1,0:T(8,128)(2,1)}, bf16[576,384]{1,0:T(8,128)(2,1)S(1)}, u32[]{:S(2)}, u32[]{:S(2)}) %collective-permute-start.9) | collective-permute-done | bytes 442400 | tf_op jit(solution)/shard_map/ppermute | solution.py:721
  43.6 13.0 %all-gather.1 = bf16[2048,192]{1,0:T(8,128)(2,1)S(1)} all-gather(bf16[512,192]{1,0:T(8,128)(2,1)S(1)} %get-tuple-element.124), channel_id=3, replica_groups={{0,8,16,24},{4,12,20,28},{1,9,17,25},{5,13,21,29},{2,10,18,26},{6,14,22..., dimensions={0}, use_global_device_ids=true | all-gather | bytes 983040 | tf_op jit(solution)/shard_map/all_gather | solution.py:782
  56.6 1.5 %collective-permute-done.14.refs_10_.refs_7_ = bf16[576,384]{1,0:T(8,128)(2,1)S(1)} collective-permute-done((bf16[576,384]{1,0:T(8,128)(2,1)S(1)}, bf16[576,384]{1,0:T(8,128)(2,1)S(1)}, u32[]{:S(2)}, u32[]{:S(2)}) %collective-permute-start.14) | collective-permute-done | bytes 442400 | tf_op jit(solution)/shard_map/ppermute | solution.py:721
  61.1 7.7 %shard_map.207 = (f32[128,768]{1,0:T(8,128)S(1)}, bf16[128,768]{1,0:T(8,128)(2,1)S(1)}, bf16[128,768]{1,0:T(8,128)(2,1)S(1)}, bf16[128,768]{1,0:T(8,128)(2,1)S(1...) custom-call(s32[4]{0:T(128)S(1)} %pad_add_fusion.ids, ...), custom_call_target="tpu_custom_call" | custom-call | flops 10000000 | bytes 1024 | tf_op jit(solution)/shard_map/pallas_call | solution.py:48
  68.9 3.0 %shard_map.208 = (f32[3,4,96,768]{3,2,1,0:T(8,128)S(1)}, bf16[3,4,96,768]{3,2,1,0:T(8,128)(2,1)S(1)}) custom-call(s32[4]{0:T(128)S(1)} %pad_add_fusion.ids, bf16[512,768]{1,0:T(8,128)(2,1)S(1)} %get-tuple-element.137.normed, bf16[512,768]{1,0:T(8,128)(2,1)S(1)} %get-tuple-element.138.active, bf16[512,768]{1,0:T(8,128)(2,1)S(1)} %get-tuple-element.139.ginner, ...), custom_call_target="tpu_custom_call" | custom-call | flops 5000000 | bytes 1024 | tf_op jit(solution)/shard_map/pallas_call | solution.py:48
  74.1 1.5 %collective-permute-start.20 = (bf16[512,192]{1,0:T(8,128)(2,1)S(1)}, bf16[512,192]{1,0:T(8,128)(2,1)S(1)}, u32[]{:S(2)}, u32[]{:S(2)}) collective-permute-start(bf16[512,192]{1,0:T(8,128)(2,1)S(1)} %get-tuple-element.136), channel_id=1, source_target_pairs={{0,24},{4,28},{8,16},{12,20},{16,8},{20,12},{24,0},{28,4},{1,25},{... | collective-permute-start | bytes 589832 | tf_op jit(solution)/shard_map/ppermute | solution.py:718
  79.2 2.0 %collective-permute-done.18.g1 = bf16[512,192]{1,0:T(8,128)(2,1)S(1)} collective-permute-done((bf16[512,192]{1,0:T(8,128)(2,1)S(1)}, bf16[512,192]{1,0:T(8,128)(2,1)S(1)}, u32[]{:S(2)}, u32[]{:S(2)}) %collective-permute-start.18) | collective-permute-done | bytes 196640 | tf_op jit(solution)/shard_map/ppermute | solution.py:718
  81.2 5.5 %collective-permute-done.19.g2 = bf16[512,192]{1,0:T(8,128)(2,1)S(1)} collective-permute-done((bf16[512,192]{1,0:T(8,128)(2,1)S(1)}, bf16[512,192]{1,0:T(8,128)(2,1)S(1)}, u32[]{:S(2)}, u32[]{:S(2)}) %collective-permute-start.19) | collective-permute-done | bytes 196640 | tf_op jit(solution)/shard_map/ppermute | solution.py:718
  88.3 1.5 %collective-permute-start.24 = (bf16[96,768]{1,0:T(8,128)(2,1)S(1)}, bf16[96,768]{1,0:T(8,128)(2,1)S(1)}, u32[]{:S(2)}, u32[]{:S(2)}) collective-permute-start(bf16[96,768]{1,0:T(8,128)(2,1)S(1)} %get-tuple-element.155), channel_id=1, source_target_pairs={{0,24},{4,28},{8,16},{12,20},{16,8},{20,12},{24,0},{28,4},{1,25},{... | collective-permute-start | bytes 442376 | tf_op jit(solution)/shard_map/ppermute | solution.py:718
  89.8 7.9 %shard_map.211 = (bf16[512,192]{1,0:T(8,128)(2,1)S(1)}, bf16[3,512,128]{2,1,0:T(8,128)(2,1)S(1)}, bf16[3,512,128]{2,1,0:T(8,128)(2,1)S(1)}, f32[3,5,128,128]{3,2,1,0:T(8,128)S(1)}) custom-call(s32[4]{0:T(128)S(1)} %pad_add_fusion.ids, s32[4]{0:T(128)S(1)} %get-tuple-element.208.q_at, s32[8]{0:T(128)S(1)} %pad_add_fusion.1.k_at, ...), custom_call_target="tpu_custom_call" | custom-call | flops 30000001024 | bytes 1024 | tf_op jit(solution)/shard_map/pallas_call | solution.py:48
  97.8 1.9 %shard_map.212 = (f32[4,96,576]{2,1,0:T(8,128)S(1)}, bf16[2,96,576]{2,1,0:T(8,128)(2,1)S(1)}, bf16[2,96,576]{2,1,0:T(8,128)(2,1)S(1)}) custom-call(s32[4]{0:T(128)S(1)} %pad_add_fusion.ids, bf16[1024,768]{1,0:T(8,128)(2,1)S(1)} %get-tuple-element.157.normed, bf16[512,192]{1,0:T(8,128)(2,1)S(1)} %get-tuple-element.151.dq, ...), custom_call_target="tpu_custom_call" | custom-call | flops 2000000 | bytes 1024 | tf_op jit(solution)/shard_map/pallas_call | solution.py:48
  100.3 1.7 %shard_map.213.table = f32[1,384]{1,0:T(1,128)S(1)} custom-call(s32[4]{0:T(128)S(1)} %pad_add_fusion.ids, f32[3,5,128,128]{3,2,1,0:T(8,128)S(1)} %get-tuple-element.161.sums), custom_call_target="tpu_custom_call" | custom-call | flops 2000000 | bytes 1024 | tf_op jit(solution)/shard_map/pallas_call | solution.py:48
  104.5 3.6 %shard_map.216 = (f32[128,768]{1,0:T(8,128)S(1)}, bf16[256,768]{1,0:T(8,128)(2,1)}, bf16[256,768]{1,0:T(8,128)(2,1)}, bf16[256,768]{1,0:T(8,128)(2,1)}, bf16[512,576]{1,0:T(8,128)(2,1)}) custom-call(s32[4]{0:T(128)S(1)} %pad_add_fusion.ids, bf16[4,144,768]{2,1,0:T(8,128)(2,1)S(1)} %bitcast.17, bf16[512,192]{1,0:T(8,128)(2,1)S(1)} %get-tuple-element.151.dq, ...), custom_call_target="tpu_custom_call" | custom-call | flops 2000000 | bytes 1024 | tf_op jit(solution)/shard_map/pallas_call | solution.py:48
  110.1 1.5 %collective-permute-start.31 = (bf16[256,768]{1,0:T(8,128)(2,1)}, bf16[256,768]{1,0:T(8,128)(2,1)}, u32[]{:S(2)}, u32[]{:S(2)}) collective-permute-start(bf16[256,768]{1,0:T(8,128)(2,1)} %get-tuple-element.176), channel_id=1, source_target_pairs={{0,24},{4,28},{8,16},{12,20},{16,8},{20,12},{24,0},{28,4},{1,25},{... | collective-permute-start | bytes 1179656 | tf_op jit(solution)/shard_map/ppermute | solution.py:718
  111.7 1.9 %collective-permute-start.35 = (bf16[192,768]{1,0:T(8,128)(2,1)S(1)}, bf16[192,768]{1,0:T(8,128)(2,1)S(1)}, u32[]{:S(2)}, u32[]{:S(2)}) collective-permute-start(bf16[192,768]{1,0:T(8,128)(2,1)S(1)} %get-tuple-element.180), channel_id=1, source_target_pairs={{0,1},{1,0},{2,3},{3,2},{4,5},{5,4},{6,7},{7,6},{8,9},{9,8},{10,11... | collective-permute-start | bytes 884744 | tf_op jit(solution)/shard_map/ppermute | solution.py:721
  113.5 1.7 %collective-permute-done.33.more = bf16[272,576]{1,0:T(8,128)(2,1)S(1)} collective-permute-done((bf16[272,576]{1,0:T(8,128)(2,1)S(1)}, bf16[272,576]{1,0:T(8,128)(2,1)S(1)}, u32[]{:S(2)}, u32[]{:S(2)}) %collective-permute-start.33) | collective-permute-done | bytes 313376 | tf_op jit(solution)/shard_map/ppermute | solution.py:721
  115.5 7.2 %collective-permute-done.35.more = bf16[192,768]{1,0:T(8,128)(2,1)S(1)} collective-permute-done((bf16[192,768]{1,0:T(8,128)(2,1)S(1)}, bf16[192,768]{1,0:T(8,128)(2,1)S(1)}, u32[]{:S(2)}, u32[]{:S(2)}) %collective-permute-start.35) | collective-permute-done | bytes 294944 | tf_op jit(solution)/shard_map/ppermute | solution.py:721
  122.8 2.9 %collective-permute-done.34.more = bf16[144,576]{1,0:T(8,128)(2,1)S(1)} collective-permute-done((bf16[144,576]{1,0:T(8,128)(2,1)S(1)}, bf16[144,576]{1,0:T(8,128)(2,1)S(1)}, u32[]{:S(2)}, u32[]{:S(2)}) %collective-permute-start.34) | collective-permute-done | bytes 165920 | tf_op jit(solution)/shard_map/ppermute | solution.py:721
  125.8 1.4 shard_map.220
  129.2 1.4 %collective-permute-start.38 = (bf16[32,1472]{1,0:T(8,128)(2,1)S(1)}, bf16[32,1472]{1,0:T(8,128)(2,1)S(1)}, u32[]{:S(2)}, u32[]{:S(2)}) collective-permute-start(bf16[32,1472]{1,0:T(8,128)(2,1)S(1)} %get-tuple-element.193), channel_id=1, source_target_pairs={{0,24},{4,28},{8,16},{12,20},{16,8},{20,12},{24,0},{28,4},{1,25},{... | collective-permute-start | bytes 282632 | tf_op jit(solution)/shard_map/ppermute | solution.py:718
  130.6 3.4 %collective-permute-start.39 = (bf16[96,768]{1,0:T(8,128)(2,1)S(1)}, bf16[96,768]{1,0:T(8,128)(2,1)S(1)}, u32[]{:S(2)}, u32[]{:S(2)}) collective-permute-start(bf16[96,768]{1,0:T(8,128)(2,1)S(1)} %get-tuple-element.195), channel_id=1, source_target_pairs={{0,0},{1,9},{2,18},{3,27},{4,4},{5,13},{6,22},{7,31},{8,8},{9,1},{... | collective-permute-start | bytes 442376 | tf_op jit(solution)/shard_map/ppermute | solution.py:1006
  134.1 2.4 %add_bitcast_fusion = (f32[1,128,768]{2,1,0:T(8,128)}, f32[1,128,768]{2,1,0:T(8,128)}) fusion(f32[128,768]{1,0:T(8,128)S(1)} %get-tuple-element.177, bf16[256,768]{1,0:T(8,128)(2,1)} %collective-permute-done.31, bf16[256,768]{1,0:T(8,128)(2,1)} %collective-permute-done.30, bf16[256,768]{1,0:T(8,128)(2,1)} %collective-permute-done.29, ...), kind=kLoop, calls=%fused_computation | loop fusion | flops 1179648 | bytes 2752512 | tf_op jit(solution)/shard_map/broadcast_in_dim | solution.py:1089
  136.5 2.1 %collective-permute-done.39.outer_in = bf16[96,768]{1,0:T(8,128)(2,1)S(1)} collective-permute-done((bf16[96,768]{1,0:T(8,128)(2,1)S(1)}, bf16[96,768]{1,0:T(8,128)(2,1)S(1)}, u32[]{:S(2)}, u32[]{:S(2)}) %collective-permute-start.39) | collective-permute-done | bytes 147488 | tf_op jit(solution)/shard_map/ppermute | solution.py:1006
  138.5 1.8 %shard_map.221 = (f32[24,768]{1,0:T(8,128)}, f32[24,768]{1,0:T(8,128)}, f32[24,768]{1,0:T(8,128)}, f32[24,3072]{1,0:T(8,128)}, f32[1,24]{1,0:T(1,128)}, /*index=...) custom-call(s32[2]{0:T(128)S(1)} %pad_add_fusion.2.where, f32[24,1472]{1,0:T(8,128)S(1)} %get-tuple-element.190.own, ...), custom_call_target="tpu_custom_call" | custom-call | flops 1000000 | bytes 1024 | tf_op jit(solution)/shard_map/pallas_call | solution.py:48
  (90 shorter events, 25.6 us)
Async XLA Ops:
  3.2 16.6 %collective-permute-start.2 = (bf16[112,576]{1,0:T(8,128)(2,1)}, bf16[112,576]{1,0:T(8,128)(2,1)S(1)}, u32[]{:S(2)}, u32[]{:S(2)}) collective-permute-start(bf16[112,576]{1,0:T(8,128)(2,1)} %get-tuple-element.109.w0.refs_0_), channel_id=1, source_target_pairs={{0,3},{1,2},{2,1},{3,0},{4,7},{5,6},{6,5},{7,4},{8,11},{9,10},{10,... | collective-permute-start | bytes 387080 | tf_op jit(solution)/shard_map/ppermute | solution.py:721
  3.3 16.5 %collective-permute-start.1 = (bf16[112,576]{1,0:T(8,128)(2,1)}, bf16[112,576]{1,0:T(8,128)(2,1)S(1)}, u32[]{:S(2)}, u32[]{:S(2)}) collective-permute-start(bf16[112,576]{1,0:T(8,128)(2,1)} %get-tuple-element.109.w0.refs_0_), channel_id=1, source_target_pairs={{0,2},{1,3},{2,0},{3,1},{4,6},{5,7},{6,4},{7,5},{8,10},{9,11},{10,... | collective-permute-start | bytes 387080 | tf_op jit(solution)/shard_map/ppermute | solution.py:721
  5.2 14.6 %collective-permute-start = (bf16[112,576]{1,0:T(8,128)(2,1)}, bf16[112,576]{1,0:T(8,128)(2,1)S(1)}, u32[]{:S(2)}, u32[]{:S(2)}) collective-permute-start(bf16[112,576]{1,0:T(8,128)(2,1)} %get-tuple-element.109.w0.refs_0_), channel_id=1, source_target_pairs={{0,1},{1,0},{2,3},{3,2},{4,5},{5,4},{6,7},{7,6},{8,9},{9,8},{10,11... | collective-permute-start | bytes 387080 | tf_op jit(solution)/shard_map/ppermute | solution.py:721
  19.8 7.5 %collective-permute-start.8 = (bf16[4,144,768]{2,1,0:T(8,128)(2,1)S(1)}, bf16[4,144,768]{2,1,0:T(8,128)(2,1)S(1)}, u32[]{:S(2)}, u32[]{:S(2)}) collective-permute-start(bf16[4,144,768]{2,1,0:T(8,128)(2,1)S(1)} %bitcast.14), channel_id=1, source_target_pairs={{0,4},{4,0},{8,12},{12,8},{16,20},{20,16},{24,28},{28,24},{1,5},{5... | collective-permute-start | bytes 2654216 | tf_op jit(solution)/shard_map/ppermute | solution.py:724
  19.8 4.5 %collective-permute-start.3 = (bf16[576,384]{1,0:T(8,128)(2,1)}, bf16[576,384]{1,0:T(8,128)(2,1)S(1)}, u32[]{:S(2)}, u32[]{:S(2)}) collective-permute-start(bf16[576,384]{1,0:T(8,128)(2,1)} %get-tuple-element.110.refs_7_.refs_4_), channel_id=1, source_target_pairs={{0,4},{4,0},{8,12},{12,8},{16,20},{20,16},{24,28},{28,24},{1,5},{5... | collective-permute-start | bytes 1327112 | tf_op jit(solution)/shard_map/ppermute | solution.py:724
  20.4 22.9 %collective-permute-start.9 = (bf16[576,384]{1,0:T(8,128)(2,1)}, bf16[576,384]{1,0:T(8,128)(2,1)S(1)}, u32[]{:S(2)}, u32[]{:S(2)}) collective-permute-start(bf16[576,384]{1,0:T(8,128)(2,1)} %get-tuple-element.110.refs_7_.refs_4_), channel_id=1, source_target_pairs={{0,2},{1,3},{2,0},{3,1},{4,6},{5,7},{6,4},{7,5},{8,10},{9,11},{10,... | collective-permute-start | bytes 1327112 | tf_op jit(solution)/shard_map/ppermute | solution.py:721
  20.7 6.2 %collective-permute-start.7 = (bf16[112,576]{1,0:T(8,128)(2,1)S(1)}, bf16[112,576]{1,0:T(8,128)(2,1)}, u32[]{:S(2)}, u32[]{:S(2)}) collective-permute-start(bf16[112,576]{1,0:T(8,128)(2,1)S(1)} %collective-permute-done.2.w3.refs_3_), channel_id=1, source_target_pairs={{0,4},{4,0},{8,12},{12,8},{16,20},{20,16},{24,28},{28,24},{1,5},{5... | collective-permute-start | bytes 387080 | tf_op jit(solution)/shard_map/ppermute | solution.py:724
  26.9 29.6 %collective-permute-start.13 = (bf16[576,384]{1,0:T(8,128)(2,1)S(1)}, bf16[576,384]{1,0:T(8,128)(2,1)S(1)}, u32[]{:S(2)}, u32[]{:S(2)}) collective-permute-start(bf16[576,384]{1,0:T(8,128)(2,1)S(1)} %copy-done.2), channel_id=1, source_target_pairs={{0,1},{1,0},{2,3},{3,2},{4,5},{5,4},{6,7},{7,6},{8,9},{9,8},{10,11... | collective-permute-start | bytes 1327112 | tf_op jit(solution)/shard_map/ppermute | solution.py:721
  30.0 13.3 %collective-permute-start.12 = (bf16[128,768]{1,0:T(8,128)(2,1)S(1)}, bf16[128,768]{1,0:T(8,128)(2,1)S(1)}, u32[]{:S(2)}, u32[]{:S(2)}) collective-permute-start(bf16[128,768]{1,0:T(8,128)(2,1)S(1)} %bitcast.20), channel_id=1, source_target_pairs={{0,24},{4,28},{8,16},{12,20},{16,8},{20,12},{24,0},{28,4},{1,25},{... | collective-permute-start | bytes 589832 | tf_op jit(solution)/shard_map/ppermute | solution.py:718
  31.5 11.8 %collective-permute-start.11 = (bf16[128,768]{1,0:T(8,128)(2,1)S(1)}, bf16[128,768]{1,0:T(8,128)(2,1)S(1)}, u32[]{:S(2)}, u32[]{:S(2)}) collective-permute-start(bf16[128,768]{1,0:T(8,128)(2,1)S(1)} %bitcast.21), channel_id=1, source_target_pairs={{0,16},{4,20},{8,24},{12,28},{16,0},{20,4},{24,8},{28,12},{1,17},{... | collective-permute-start | bytes 589832 | tf_op jit(solution)/shard_map/ppermute | solution.py:718
  32.4 11.0 %collective-permute-start.10 = (bf16[128,768]{1,0:T(8,128)(2,1)S(1)}, bf16[128,768]{1,0:T(8,128)(2,1)S(1)}, u32[]{:S(2)}, u32[]{:S(2)}) collective-permute-start(bf16[128,768]{1,0:T(8,128)(2,1)S(1)} %bitcast.22), channel_id=1, source_target_pairs={{0,8},{4,12},{8,0},{12,4},{16,24},{20,28},{24,16},{28,20},{1,9},{5... | collective-permute-start | bytes 589832 | tf_op jit(solution)/shard_map/ppermute | solution.py:718
  43.4 14.7 %collective-permute-start.14 = (bf16[576,384]{1,0:T(8,128)(2,1)S(1)}, bf16[576,384]{1,0:T(8,128)(2,1)S(1)}, u32[]{:S(2)}, u32[]{:S(2)}) collective-permute-start(bf16[576,384]{1,0:T(8,128)(2,1)S(1)} %collective-permute-done.9.refs_9_.refs_6_), channel_id=1, source_target_pairs={{0,1},{1,0},{2,3},{3,2},{4,5},{5,4},{6,7},{7,6},{8,9},{9,8},{10,11... | collective-permute-start | bytes 1327112 | tf_op jit(solution)/shard_map/ppermute | solution.py:721
  71.9 5.2 %collective-permute-start.21 = (bf16[3,4,96,768]{3,2,1,0:T(8,128)(2,1)S(1)}, bf16[3,4,96,768]{3,2,1,0:T(8,128)(2,1)S(1)}, u32[]{:S(2)}, u32[]{:S(2)}) collective-permute-start(bf16[3,4,96,768]{3,2,1,0:T(8,128)(2,1)S(1)} %get-tuple-element.143), channel_id=1, source_target_pairs={{0,4},{4,0},{8,12},{12,8},{16,20},{20,16},{24,28},{28,24},{1,5},{5... | collective-permute-start | bytes 5308424 | tf_op jit(solution)/shard_map/ppermute | solution.py:724
  72.1 9.1 %collective-permute-start.18 = (bf16[512,192]{1,0:T(8,128)(2,1)S(1)}, bf16[512,192]{1,0:T(8,128)(2,1)S(1)}, u32[]{:S(2)}, u32[]{:S(2)}) collective-permute-start(bf16[512,192]{1,0:T(8,128)(2,1)S(1)} %get-tuple-element.134), channel_id=1, source_target_pairs={{0,8},{4,12},{8,0},{12,4},{16,24},{20,28},{24,16},{28,20},{1,9},{5... | collective-permute-start | bytes 589832 | tf_op jit(solution)/shard_map/ppermute | solution.py:718
  73.1 13.6 %collective-permute-start.19 = (bf16[512,192]{1,0:T(8,128)(2,1)S(1)}, bf16[512,192]{1,0:T(8,128)(2,1)S(1)}, u32[]{:S(2)}, u32[]{:S(2)}) collective-permute-start(bf16[512,192]{1,0:T(8,128)(2,1)S(1)} %get-tuple-element.135), channel_id=1, source_target_pairs={{0,16},{4,20},{8,24},{12,28},{16,0},{20,4},{24,8},{28,12},{1,17},{... | collective-permute-start | bytes 589832 | tf_op jit(solution)/shard_map/ppermute | solution.py:718
  74.1 13.2 %collective-permute-start.20 = (bf16[512,192]{1,0:T(8,128)(2,1)S(1)}, bf16[512,192]{1,0:T(8,128)(2,1)S(1)}, u32[]{:S(2)}, u32[]{:S(2)}) collective-permute-start(bf16[512,192]{1,0:T(8,128)(2,1)S(1)} %get-tuple-element.136), channel_id=1, source_target_pairs={{0,24},{4,28},{8,16},{12,20},{16,8},{20,12},{24,0},{28,4},{1,25},{... | collective-permute-start | bytes 589832 | tf_op jit(solution)/shard_map/ppermute | solution.py:718
  78.1 19.6 %collective-permute-start.22 = (bf16[96,768]{1,0:T(8,128)(2,1)S(1)}, bf16[96,768]{1,0:T(8,128)(2,1)S(1)}, u32[]{:S(2)}, u32[]{:S(2)}) collective-permute-start(bf16[96,768]{1,0:T(8,128)(2,1)S(1)} %get-tuple-element.145), channel_id=1, source_target_pairs={{0,8},{4,12},{8,0},{12,4},{16,24},{20,28},{24,16},{28,20},{1,9},{5... | collective-permute-start | bytes 442376 | tf_op jit(solution)/shard_map/ppermute | solution.py:718
  79.2 32.4 %collective-permute-start.32 = (bf16[384,768]{1,0:T(8,128)(2,1)S(1)}, bf16[384,768]{1,0:T(8,128)(2,1)S(1)}, u32[]{:S(2)}, u32[]{:S(2)}) collective-permute-start(bf16[384,768]{1,0:T(8,128)(2,1)S(1)} %get-tuple-element.144), channel_id=1, source_target_pairs={{0,2},{1,3},{2,0},{3,1},{4,6},{5,7},{6,4},{7,5},{8,10},{9,11},{10,... | collective-permute-start | bytes 1769480 | tf_op jit(solution)/shard_map/ppermute | solution.py:721
  87.3 10.3 %collective-permute-start.23 = (bf16[96,768]{1,0:T(8,128)(2,1)S(1)}, bf16[96,768]{1,0:T(8,128)(2,1)S(1)}, u32[]{:S(2)}, u32[]{:S(2)}) collective-permute-start(bf16[96,768]{1,0:T(8,128)(2,1)S(1)} %get-tuple-element.154), channel_id=1, source_target_pairs={{0,16},{4,20},{8,24},{12,28},{16,0},{20,4},{24,8},{28,12},{1,17},{... | collective-permute-start | bytes 442376 | tf_op jit(solution)/shard_map/ppermute | solution.py:718
  88.3 9.3 %collective-permute-start.24 = (bf16[96,768]{1,0:T(8,128)(2,1)S(1)}, bf16[96,768]{1,0:T(8,128)(2,1)S(1)}, u32[]{:S(2)}, u32[]{:S(2)}) collective-permute-start(bf16[96,768]{1,0:T(8,128)(2,1)S(1)} %get-tuple-element.155), channel_id=1, source_target_pairs={{0,24},{4,28},{8,16},{12,20},{16,8},{20,12},{24,0},{28,4},{1,25},{... | collective-permute-start | bytes 442376 | tf_op jit(solution)/shard_map/ppermute | solution.py:718
  97.7 6.8 %collective-permute-start.25 = (bf16[3,512,128]{2,1,0:T(8,128)(2,1)S(1)}, bf16[3,512,128]{2,1,0:T(8,128)(2,1)S(1)}, u32[]{:S(2)}, u32[]{:S(2)}) collective-permute-start(bf16[3,512,128]{2,1,0:T(8,128)(2,1)S(1)} %get-tuple-element.156.doth), channel_id=1, source_target_pairs={{0,4},{4,0},{8,12},{12,8},{16,20},{20,16},{24,28},{28,24},{1,5},{5... | collective-permute-start | bytes 1179656 | tf_op jit(solution)/shard_map/ppermute | solution.py:724
  99.7 3.7 %collective-permute-start.26 = (bf16[2,96,576]{2,1,0:T(8,128)(2,1)S(1)}, bf16[2,96,576]{2,1,0:T(8,128)(2,1)S(1)}, u32[]{:S(2)}, u32[]{:S(2)}) collective-permute-start(bf16[2,96,576]{2,1,0:T(8,128)(2,1)S(1)} %get-tuple-element.159), channel_id=1, source_target_pairs={{0,4},{4,0},{8,12},{12,8},{16,20},{20,16},{24,28},{28,24},{1,5},{5... | collective-permute-start | bytes 663560 | tf_op jit(solution)/shard_map/ppermute | solution.py:724
  104.2 11.0 %collective-permute-start.33 = (bf16[272,576]{1,0:T(8,128)(2,1)S(1)}, bf16[272,576]{1,0:T(8,128)(2,1)S(1)}, u32[]{:S(2)}, u32[]{:S(2)}) collective-permute-start(bf16[272,576]{1,0:T(8,128)(2,1)S(1)} %get-tuple-element.165), channel_id=1, source_target_pairs={{0,1},{1,0},{2,3},{3,2},{4,5},{5,4},{6,7},{7,6},{8,9},{9,8},{10,11... | collective-permute-start | bytes 940040 | tf_op jit(solution)/shard_map/ppermute | solution.py:721
  108.1 21.1 %collective-permute-start.29 = (bf16[256,768]{1,0:T(8,128)(2,1)}, bf16[256,768]{1,0:T(8,128)(2,1)}, u32[]{:S(2)}, u32[]{:S(2)}) collective-permute-start(bf16[256,768]{1,0:T(8,128)(2,1)} %get-tuple-element.174), channel_id=1, source_target_pairs={{0,8},{4,12},{8,0},{12,4},{16,24},{20,28},{24,16},{28,20},{1,9},{5... | collective-permute-start | bytes 1179656 | tf_op jit(solution)/shard_map/ppermute | solution.py:718
  109.3 21.4 %collective-permute-start.30 = (bf16[256,768]{1,0:T(8,128)(2,1)}, bf16[256,768]{1,0:T(8,128)(2,1)}, u32[]{:S(2)}, u32[]{:S(2)}) collective-permute-start(bf16[256,768]{1,0:T(8,128)(2,1)} %get-tuple-element.175), channel_id=1, source_target_pairs={{0,16},{4,20},{8,24},{12,28},{16,0},{20,4},{24,8},{28,12},{1,17},{... | collective-permute-start | bytes 1179656 | tf_op jit(solution)/shard_map/ppermute | solution.py:718
  110.1 24.0 %collective-permute-start.31 = (bf16[256,768]{1,0:T(8,128)(2,1)}, bf16[256,768]{1,0:T(8,128)(2,1)}, u32[]{:S(2)}, u32[]{:S(2)}) collective-permute-start(bf16[256,768]{1,0:T(8,128)(2,1)} %get-tuple-element.176), channel_id=1, source_target_pairs={{0,24},{4,28},{8,16},{12,20},{16,8},{20,12},{24,0},{28,4},{1,25},{... | collective-permute-start | bytes 1179656 | tf_op jit(solution)/shard_map/ppermute | solution.py:718
  111.7 11.0 %collective-permute-start.35 = (bf16[192,768]{1,0:T(8,128)(2,1)S(1)}, bf16[192,768]{1,0:T(8,128)(2,1)S(1)}, u32[]{:S(2)}, u32[]{:S(2)}) collective-permute-start(bf16[192,768]{1,0:T(8,128)(2,1)S(1)} %get-tuple-element.180), channel_id=1, source_target_pairs={{0,1},{1,0},{2,3},{3,2},{4,5},{5,4},{6,7},{7,6},{8,9},{9,8},{10,11... | collective-permute-start | bytes 884744 | tf_op jit(solution)/shard_map/ppermute | solution.py:721
  115.3 10.5 %collective-permute-start.34 = (bf16[144,576]{1,0:T(8,128)(2,1)S(1)}, bf16[144,576]{1,0:T(8,128)(2,1)S(1)}, u32[]{:S(2)}, u32[]{:S(2)}) collective-permute-start(bf16[144,576]{1,0:T(8,128)(2,1)S(1)} %get-tuple-element.184), channel_id=1, source_target_pairs={{0,2},{1,3},{2,0},{3,1},{4,6},{5,7},{6,4},{7,5},{8,10},{9,11},{10,... | collective-permute-start | bytes 497672 | tf_op jit(solution)/shard_map/ppermute | solution.py:721
  127.1 9.3 %collective-permute-start.36 = (bf16[32,1472]{1,0:T(8,128)(2,1)S(1)}, bf16[32,1472]{1,0:T(8,128)(2,1)S(1)}, u32[]{:S(2)}, u32[]{:S(2)}) collective-permute-start(bf16[32,1472]{1,0:T(8,128)(2,1)S(1)} %get-tuple-element.191), channel_id=1, source_target_pairs={{0,8},{4,12},{8,0},{12,4},{16,24},{20,28},{24,16},{28,20},{1,9},{5... | collective-permute-start | bytes 282632 | tf_op jit(solution)/shard_map/ppermute | solution.py:718
  128.2 8.2 %collective-permute-start.37 = (bf16[32,1472]{1,0:T(8,128)(2,1)S(1)}, bf16[32,1472]{1,0:T(8,128)(2,1)S(1)}, u32[]{:S(2)}, u32[]{:S(2)}) collective-permute-start(bf16[32,1472]{1,0:T(8,128)(2,1)S(1)} %get-tuple-element.192), channel_id=1, source_target_pairs={{0,16},{4,20},{8,24},{12,28},{16,0},{20,4},{24,8},{28,12},{1,17},{... | collective-permute-start | bytes 282632 | tf_op jit(solution)/shard_map/ppermute | solution.py:718
  129.2 7.3 %collective-permute-start.38 = (bf16[32,1472]{1,0:T(8,128)(2,1)S(1)}, bf16[32,1472]{1,0:T(8,128)(2,1)S(1)}, u32[]{:S(2)}, u32[]{:S(2)}) collective-permute-start(bf16[32,1472]{1,0:T(8,128)(2,1)S(1)} %get-tuple-element.193), channel_id=1, source_target_pairs={{0,24},{4,28},{8,16},{12,20},{16,8},{20,12},{24,0},{28,4},{1,25},{... | collective-permute-start | bytes 282632 | tf_op jit(solution)/shard_map/ppermute | solution.py:718
  130.6 7.9 %collective-permute-start.39 = (bf16[96,768]{1,0:T(8,128)(2,1)S(1)}, bf16[96,768]{1,0:T(8,128)(2,1)S(1)}, u32[]{:S(2)}, u32[]{:S(2)}) collective-permute-start(bf16[96,768]{1,0:T(8,128)(2,1)S(1)} %get-tuple-element.195), channel_id=1, source_target_pairs={{0,0},{1,9},{2,18},{3,27},{4,4},{5,13},{6,22},{7,31},{8,8},{9,1},{... | collective-permute-start | bytes 442376 | tf_op jit(solution)/shard_map/ppermute | solution.py:1006
  (16 other events, 72.1 us)
